TPU v7x, 128 devices: a whole 4x4x4 slice. The times are simulated.
128 devices in a mesh: ctx: 64 (over y, z_hi, x, core), tp: 2 (over z_lo).
Axes of the slice: x: 4, y: 4, z: 4 (z_hi: 2, z_lo: 2; z = z_hi * 2 + z_lo), core: 2. Of those that a mesh axis runs over, the one named last changes fastest.
Arguments:
- residual: bfloat16 [16384, 5120], P('ctx', 'tp'), may hold values from -6 to 6
- shared_out: bfloat16 [16384, 5120], P('ctx', 'tp'), may hold values from -4 to 4
- expert_out: bfloat16 [128, 64, 4, 5120], P('ctx', None, None, 'tp'), may hold values from -6 to 6
- routing: int32 [16384, 1], P('ctx'), may hold values from 0 to 127; in each aligned block of 256 rows (0 to 255, 256 to 511, ...) at most 4 rows name the same one
- gate_score: float32 [16384, 1], P('ctx'), may hold values from 0.1 to 1
- norm_gain: bfloat16 [5120], replicated, may hold values from 0.25 to 1.75
- w_query: bfloat16 [5120, 2560], P(None, 'tp'), may hold values from -2 to 2
- w_key: bfloat16 [5120, 512], P(None, 'tp'), may hold values from -1 to 1
- w_value: bfloat16 [5120, 512], P(None, 'tp'), may hold values from -0.078125 to 0.078125
Outputs:
- hidden_state: bfloat16 [16384, 5120], P('ctx', 'tp')
- attended: bfloat16 [16384, 2560], P('ctx', 'tp')
Inputs may be any that keep to these rules, and one draw needn't show every extreme that they name: `routing`: in each device's aligned block of 256 rows no expert is named by more than 4 rows, a bound that some block reaches.
All inputs are finite; a program needn't handle non-finite values.
Results may differ from a plain program's by a relative error of at most 0.014.
Values may be sent and summed in bfloat16 or wider, within the bound.
No kernel may reach another device: no remote copies, remote signals or barrier semaphores. Data moves between devices by JAX's collectives and lax.ppermute only.
A program may use at most 128 MiB of HBM per device.

v0:
```python
import math

import jax
import jax.numpy as jnp
from jax import lax
from jax.sharding import PartitionSpec as P

HD = 128


ROPE_BASE = 500000.0
NORM_EPS = 1e-05
NEG_FILL = -1e30


def token_positions(storage, ctx_count, tok_rows):
    half_block = tok_rows // 2
    device = storage // tok_rows
    within = storage % tok_rows
    early_pos = device * half_block + within
    late_pos = (2 * ctx_count - 1 - device) * half_block + (within - half_block)
    return jnp.where(within < half_block, early_pos, late_pos)


def rotate(projected, positions):
    row_count = projected.shape[0]
    head_count = projected.shape[1] // HD
    half_dim = HD // 2
    frequency = ROPE_BASE ** (-(jnp.arange(half_dim, dtype=jnp.float32) * 2.0 / HD))
    angles = positions.astype(jnp.float32)[:, None] * frequency[None, :]
    cos_part = jnp.cos(angles)[:, None, :]
    sin_part = jnp.sin(angles)[:, None, :]
    paired = projected.reshape(row_count, head_count, 2, half_dim)
    first_half = paired[:, :, 0, :]
    second_half = paired[:, :, 1, :]
    out_first = first_half * cos_part - second_half * sin_part
    out_second = second_half * cos_part + first_half * sin_part
    return jnp.stack([out_first, out_second], axis=2).reshape(row_count, head_count * HD)


def slot_numbers(expert_ids, expert_count):
    row_count = expert_ids.shape[0]
    onehot = (expert_ids[:, None] == jnp.arange(expert_count, dtype=jnp.int32)[None, :]).astype(
        jnp.float32
    )
    earlier = (jnp.arange(row_count)[:, None] > jnp.arange(row_count)[None, :]).astype(jnp.float32)
    counts = jnp.dot(earlier, onehot, preferred_element_type=jnp.float32)
    return jnp.sum(counts * onehot, axis=1).astype(jnp.int32)


def position_order(rows, tok_rows):
    shard_count = rows.shape[0] // tok_rows
    split = rows.reshape((shard_count, 2, tok_rows // 2) + rows.shape[1:])
    early_rows = split[:, 0].reshape((shard_count * (tok_rows // 2),) + rows.shape[1:])
    late_rows = split[::-1, 1].reshape((shard_count * (tok_rows // 2),) + rows.shape[1:])
    return jnp.concatenate([early_rows, late_rows], axis=0)


def attend_piece(carry_state, query_heads, query_pos, key_piece, value_piece, key_pos):
    kv_local = query_heads.shape[1]
    key_heads = key_piece.reshape(key_piece.shape[0], kv_local, HD)
    value_heads = value_piece.reshape(value_piece.shape[0], kv_local, HD)
    scale = 1.0 / HD**0.5

    def compute(state_in):
        running_max, denominator, weighted = state_in
        scores = (
            jnp.einsum("qhgd,khd->hgqk", query_heads, key_heads, preferred_element_type=jnp.float32)
            * scale
        )
        visible = key_pos[None, :] <= query_pos[:, None]
        scores = jnp.where(visible, scores, NEG_FILL)
        new_max = jnp.maximum(running_max, jnp.max(scores, axis=-1))
        weights_exp = jnp.where(visible, jnp.exp(scores - new_max[..., None]), 0.0)
        rescale = jnp.exp(running_max - new_max)
        denominator = denominator * rescale + jnp.sum(weights_exp, axis=-1)
        rounded = weights_exp.astype(jnp.bfloat16)
        weighted = weighted * rescale[..., None] + jnp.einsum(
            "hgqk,khd->hgqd", rounded, value_heads, preferred_element_type=jnp.float32
        )
        return (new_max, denominator, weighted)

    masked_out = jnp.min(key_pos) > jnp.max(query_pos)
    return lax.cond(masked_out, lambda state_in: state_in, compute, carry_state)


def shards(
    residual, shared_out, expert_out, routing, gate_score, norm_gain, w_query, w_key, w_value
):
    tok_rows = residual.shape[0]
    half_width = residual.shape[1]
    half_rows = tok_rows // 2
    ctx_count = lax.axis_size("ctx")
    ctx_index = lax.axis_index("ctx")
    tp_index = lax.axis_index("tp")
    returned = lax.all_to_all(expert_out, "ctx", split_axis=1, concat_axis=0, tiled=True)
    expert_count = returned.shape[0]
    slot_cap = returned.shape[2]
    expert_ids = routing[:, 0]
    slot_index = slot_numbers(expert_ids, expert_count)
    picked = jnp.take(
        returned.reshape(expert_count * slot_cap, half_width),
        expert_ids * slot_cap + slot_index,
        axis=0,
    )
    hidden_state = (
        residual.astype(jnp.float32)
        + shared_out.astype(jnp.float32)
        + gate_score * picked.astype(jnp.float32)
    ).astype(jnp.bfloat16)
    norm_scale = norm_gain.astype(jnp.float32)
    local_rows = hidden_state.astype(jnp.float32)
    square_sums = lax.psum(jnp.sum(local_rows * local_rows, axis=1, keepdims=True), "tp")
    full_width = half_width * lax.axis_size("tp")
    local_gain = lax.dynamic_slice_in_dim(norm_scale, tp_index * half_width, half_width)
    normed_part = (local_rows * lax.rsqrt(square_sums / full_width + NORM_EPS) * local_gain).astype(
        jnp.bfloat16
    )
    normed = lax.all_gather(normed_part, "tp", axis=1, tiled=True)
    query_pos = token_positions(
        ctx_index * tok_rows + jnp.arange(tok_rows, dtype=jnp.int32), ctx_count, tok_rows
    )
    queries = rotate(
        jnp.dot(normed, w_query, preferred_element_type=jnp.float32), query_pos
    ).astype(jnp.bfloat16)
    keys_rot = rotate(jnp.dot(normed, w_key, preferred_element_type=jnp.float32), query_pos).astype(
        jnp.bfloat16
    )
    values = jnp.dot(normed, w_value, preferred_element_type=jnp.float32).astype(jnp.bfloat16)
    kv_local = w_key.shape[1] // HD
    group = w_query.shape[1] // w_key.shape[1]
    query_heads = queries.reshape(tok_rows, kv_local, group, HD)
    early_heads = query_heads[:half_rows]
    late_heads = query_heads[half_rows:]
    early_pos = query_pos[:half_rows]
    late_pos = query_pos[half_rows:]
    start_state = (
        jnp.full((kv_local, group, tok_rows), NEG_FILL, jnp.float32),
        jnp.zeros((kv_local, group, tok_rows), jnp.float32),
        jnp.zeros((kv_local, group, tok_rows, HD), jnp.float32),
    )
    gathered = (
        lax.all_gather(keys_rot, "ctx", axis=0, tiled=True),
        lax.all_gather(values, "ctx", axis=0, tiled=True),
    )
    key_rows = gathered[0]
    row_count = key_rows.shape[0]
    ordered_keys = position_order(key_rows, tok_rows)
    ordered_values = position_order(gathered[1], tok_rows)
    storage_rows = position_order(jnp.arange(row_count, dtype=jnp.int32), tok_rows)
    key_block = math.gcd(row_count // 2, 2048)

    def advance(block_index, state_in):
        offset = block_index * key_block
        key_piece = lax.dynamic_slice_in_dim(ordered_keys, offset, key_block, 0)
        value_piece = lax.dynamic_slice_in_dim(ordered_values, offset, key_block, 0)
        storage = lax.dynamic_slice_in_dim(storage_rows, offset, key_block, 0)
        key_pos = token_positions(storage, ctx_count, tok_rows)
        early_state = tuple((lax.slice_in_dim(part, 0, half_rows, axis=2) for part in state_in))
        late_state = tuple(
            (lax.slice_in_dim(part, half_rows, tok_rows, axis=2) for part in state_in)
        )
        early_state = attend_piece(
            early_state, early_heads, early_pos, key_piece, value_piece, key_pos
        )
        late_state = attend_piece(late_state, late_heads, late_pos, key_piece, value_piece, key_pos)
        return tuple(
            (
                jnp.concatenate([first, second], axis=2)
                for first, second in zip(early_state, late_state)
            )
        )

    final_state = lax.fori_loop(0, row_count // key_block, advance, start_state)
    running_max, denominator, weighted = final_state
    result = weighted / denominator[..., None]
    attended = (
        jnp.transpose(result, (2, 0, 1, 3))
        .reshape(tok_rows, kv_local * group * HD)
        .astype(jnp.bfloat16)
    )
    return (hidden_state, attended)


def solution(mesh):
    return jax.shard_map(
        shards,
        mesh=mesh,
        in_specs=(
            P("ctx", "tp"),
            P("ctx", "tp"),
            P("ctx", None, None, "tp"),
            P("ctx", None),
            P("ctx", None),
            P(),
            P(None, "tp"),
            P(None, "tp"),
            P(None, "tp"),
        ),
        out_specs=(P("ctx", "tp"), P("ctx", "tp")),
        check_vma=False,
    )
```

profile of v0, /device:TPU:1, one launch (start us, length us, event | category | flops | bytes accessed | tf_op | source)
XLA Modules:
  0.0 537.4 jit_solution(12672792048630428138)
XLA Ops:
  7.2 4.3 copy.59
  11.5 12.5 %all-to-all-start = ((bf16[2,64,4,2560]{3,2,0,1:T(4,128)(2,1)}), bf16[2,64,4,2560]{3,2,0,1:T(4,128)(2,1)}, u32[]{:S(2)}, u32[]{:S(2)}) async-start(bf16[2,64,4,2560]{3,2,0,1:T(4,128)(2,1)} %copy.59), calls=%async_computation | async-start | bytes 5242880 | tf_op jit(solution)/shard_map/all_to_all | solution.py:96
  24.4 36.0 %all-to-all-done = bf16[2,64,4,2560]{3,2,0,1:T(4,128)(2,1)} async-done(((bf16[2,64,4,2560]{3,2,0,1:T(4,128)(2,1)}), bf16[2,64,4,2560]{3,2,0,1:T(4,128)(2,1)}, u32[]{:S(2)}, u32[]{:S(2)}) %all-to-all-start) | async-done | bytes 2621472 | tf_op jit(solution)/shard_map/all_to_all | solution.py:96
  60.4 5.3 reshape.191
  65.7 5.9 %gather_fusion = bf16[256,2560]{1,0:T(8,128)(2,1)} fusion(bf16[512,2560]{1,0:T(8,128)(2,1)} %reshape.191, s32[1024]{0:T(1024)S(1)} %pad_clamp_fusion), kind=kCustom, calls=%fused_computation | custom fusion | bytes 2622464 | tf_op jit(solution)/shard_map/jit(_take)/gather | solution.py:101
  71.6 4.0 fusion.32
  75.6 3.8 psum.7
  82.2 38.8 %all-gather.4.cloned.1.call-done = bf16[256,5120]{1,0:T(8,128)(2,1)} async-done(((bf16[256,2560]{1,0:T(8,128)(2,1)}), bf16[256,5120]{1,0:T(8,128)(2,1)}) %all-gather.4.cloned.1.call-update) | async-done | bytes 2621456 | tf_op jit(solution)/shard_map/all_gather | solution.py:119
  121.0 3.2 convolution_convert_fusion
  124.8 3.8 fusion.46
  130.2 8.2 %fusion.47 = f32[256,1280]{0,1:T(8,128)S(1)} fusion(bf16[256,5120]{1,0:T(8,128)(2,1)S(1)} %copy-done.2, bf16[5120,1280]{1,0:T(8,128)(2,1)} %param.21), kind=kOutput, calls=%fused_computation.100 | convolution fusion | flops 3355443200 | bytes 17039360 | tf_op jit(solution)/shard_map/dot_general | solution.py:124
  139.3 70.2 %all-gather.8.cloned.1.call-done = bf16[16384,256]{1,0:T(8,128)(2,1)} async-done(((bf16[256,256]{1,0:T(8,128)(2,1)}), bf16[16384,256]{1,0:T(8,128)(2,1)}) %all-gather.8.cloned.1.call-update) | async-done | bytes 8388624 | tf_op jit(solution)/shard_map/all_gather | solution.py:144
  209.4 6.0 %fusion.43 = (bf16[64,1,128,256]{3,2,1,0:T(8,128)(2,1)}, bf16[64,1,128,256]{3,2,1,0:T(8,128)(2,1)}) fusion(bf16[64,2,128,256]{3,2,1,0:T(8,128)(2,1)} %bitcast.98), kind=kLoop, calls=%fused_computation.96 | loop fusion | bytes 16777216 | tf_op jit(solution)/shard_map/slice | solution.py:54
  215.5 6.4 %copy.85 = bf16[8192,256]{0,1:T(8,128)(2,1)} copy(bf16[8192,256]{1,0:T(8,128)(2,1)} %bitcast.96) | data formatting | bytes 8388608 | tf_op jit(solution)/shard_map/reshape;squeeze | solution.py:54
  221.9 84.2 %all-gather.6.cloned.1.call-done = bf16[16384,256]{0,1:T(8,128)(2,1)} async-done(((bf16[256,256]{0,1:T(8,128)(2,1)}), bf16[16384,256]{0,1:T(8,128)(2,1)}) %all-gather.6.cloned.1.call-update) | async-done | bytes 8388624 | tf_op jit(solution)/shard_map/all_gather | solution.py:143
  306.0 11.9 %copy.60 = bf16[16384,256]{1,0:T(8,128)(2,1)} copy(bf16[16384,256]{0,1:T(8,128)(2,1)} %all-gather.6.cloned.1.call-done) | data formatting | bytes 16777216 | tf_op jit(solution)/shard_map/all_gather | solution.py:143
  317.9 6.0 %fusion.44 = (bf16[64,1,128,256]{3,2,1,0:T(8,128)(2,1)}, bf16[64,1,128,256]{3,2,1,0:T(8,128)(2,1)}) fusion(bf16[64,2,128,256]{3,2,1,0:T(8,128)(2,1)} %bitcast.93), kind=kLoop, calls=%fused_computation.97 | loop fusion | bytes 16777216 | tf_op jit(solution)/shard_map/slice | solution.py:54
  323.9 6.4 %copy.61 = bf16[8192,256]{0,1:T(8,128)(2,1)} copy(bf16[8192,256]{1,0:T(8,128)(2,1)} %bitcast.97) | data formatting | bytes 8388608 | tf_op jit(solution)/shard_map/reshape;squeeze | solution.py:54
  330.3 4.7 rev.10
  335.0 6.4 %copy.62 = bf16[8192,256]{0,1:T(8,128)(2,1)} copy(bf16[8192,256]{1,0:T(8,128)(2,1)} %bitcast.94) | data formatting | bytes 8388608 | tf_op jit(solution)/shard_map/reshape;squeeze | solution.py:55
  341.4 4.6 rev.11
  346.0 6.4 %copy.86 = bf16[8192,256]{0,1:T(8,128)(2,1)} copy(bf16[8192,256]{1,0:T(8,128)(2,1)} %bitcast.95) | data formatting | bytes 8388608 | tf_op jit(solution)/shard_map/reshape;squeeze | solution.py:55
  352.4 7.6 %pad_maximum_fusion.3 = bf16[16384,256]{0,1:T(8,128)(2,1)} fusion(bf16[8192,256]{0,1:T(8,128)(2,1)} %copy.62, bf16[8192,256]{0,1:T(8,128)(2,1)} %copy.61), kind=kLoop, calls=%fused_computation.49 | loop fusion | flops 16777216 | bytes 16777216 | tf_op jit(solution)/shard_map/concatenate | solution.py:56
  360.0 7.6 %pad_maximum_fusion.4 = bf16[16384,256]{0,1:T(8,128)(2,1)} fusion(bf16[8192,256]{0,1:T(8,128)(2,1)} %copy.86, bf16[8192,256]{0,1:T(8,128)(2,1)} %copy.85), kind=kLoop, calls=%fused_computation.50 | loop fusion | flops 16777216 | bytes 16777216 | tf_op jit(solution)/shard_map/concatenate | solution.py:56
  368.8 156.6 %while.19 = (s32[]{:T(128)}, f32[2,5,256]{2,1,0:T(8,128)S(1)}, f32[2,5,256]{2,1,0:T(8,128)S(1)}, f32[2,5,256,128]{3,2,1,0:T(8,128)}, s32[16384]{0:T(1024)S(1)}, ...) while((s32[]{:T(128)}, f32[2,5,256]{2,1,0:T(8,128)S(1)}, ...), condition=%wide.region_15.16_spmd, body=%wide.region_5.15_spmd.sunk | while | flops 2754086912 | bytes 82179536 | solution.py:174
  373.4 2.8 constant_dynamic-slice_fusion.3
  376.2 9.7 %conditional.5 = (f32[2,5,128]{2,1,0:T(8,128)S(1)}, f32[2,5,128]{2,1,0:T(8,128)S(1)}, f32[2,5,128,128]{3,2,1,0:T(8,128)S(1)}) conditional(s32[]{:T(128)} %convert_element_type.136, (s32[2048]{0:T(1024)S(1)}, s32[128]{0:T(128)S(1)}, bf16[2048,2,128]{0,2,1:T(8,128)(2,1)S(1)}, bf16[128,2,5,128]{3,0,2,1:T(8,128)(2,1)S(1)}, f32[2,5,128]{2,1,0:T(8,128)S(1)}, ...), branch_computations={%region_7.9_spmd, %region_10.10_spmd} | conditional | flops 1376848384 | bytes 36321816 | solution.py:84
  381.2 4.7 fusion.6
  385.9 9.7 %conditional.4 = (f32[2,5,128]{2,1,0:T(8,128)S(1)}, f32[2,5,128]{2,1,0:T(8,128)S(1)}, f32[2,5,128,128]{3,2,1,0:T(8,128)S(1)}) conditional(s32[]{:T(128)} %convert_element_type.135, (s32[2048]{0:T(1024)S(1)}, s32[128]{0:T(128)S(1)}, bf16[2048,2,128]{0,2,1:T(8,128)(2,1)S(1)}, bf16[128,2,5,128]{3,0,2,1:T(8,128)(2,1)S(1)}, ...), branch_computations={%region_11.13_spmd, %region_14.14_spmd} | conditional | flops 1376848384 | bytes 36321816 | solution.py:84
  390.9 4.7 fusion.21
  401.5 2.8 constant_dynamic-slice_fusion.3
  404.3 9.7 %conditional.4 = (f32[2,5,128]{2,1,0:T(8,128)S(1)}, f32[2,5,128]{2,1,0:T(8,128)S(1)}, f32[2,5,128,128]{3,2,1,0:T(8,128)S(1)}) conditional(s32[]{:T(128)} %convert_element_type.135, (s32[2048]{0:T(1024)S(1)}, s32[128]{0:T(128)S(1)}, bf16[2048,2,128]{0,2,1:T(8,128)(2,1)S(1)}, bf16[128,2,5,128]{3,0,2,1:T(8,128)(2,1)S(1)}, ...), branch_computations={%region_11.13_spmd, %region_14.14_spmd} | conditional | flops 1376848384 | bytes 36321816 | solution.py:84
  409.3 4.7 fusion.21
  419.9 2.8 constant_dynamic-slice_fusion.3
  422.7 9.7 %conditional.4 = (f32[2,5,128]{2,1,0:T(8,128)S(1)}, f32[2,5,128]{2,1,0:T(8,128)S(1)}, f32[2,5,128,128]{3,2,1,0:T(8,128)S(1)}) conditional(s32[]{:T(128)} %convert_element_type.135, (s32[2048]{0:T(1024)S(1)}, s32[128]{0:T(128)S(1)}, bf16[2048,2,128]{0,2,1:T(8,128)(2,1)S(1)}, bf16[128,2,5,128]{3,0,2,1:T(8,128)(2,1)S(1)}, ...), branch_computations={%region_11.13_spmd, %region_14.14_spmd} | conditional | flops 1376848384 | bytes 36321816 | solution.py:84
  427.6 4.7 fusion.21
  438.2 2.8 constant_dynamic-slice_fusion.3
  441.0 9.7 %conditional.4 = (f32[2,5,128]{2,1,0:T(8,128)S(1)}, f32[2,5,128]{2,1,0:T(8,128)S(1)}, f32[2,5,128,128]{3,2,1,0:T(8,128)S(1)}) conditional(s32[]{:T(128)} %convert_element_type.135, (s32[2048]{0:T(1024)S(1)}, s32[128]{0:T(128)S(1)}, bf16[2048,2,128]{0,2,1:T(8,128)(2,1)S(1)}, bf16[128,2,5,128]{3,0,2,1:T(8,128)(2,1)S(1)}, ...), branch_computations={%region_11.13_spmd, %region_14.14_spmd} | conditional | flops 1376848384 | bytes 36321816 | solution.py:84
  446.0 4.7 fusion.21
  459.4 9.7 %conditional.4 = (f32[2,5,128]{2,1,0:T(8,128)S(1)}, f32[2,5,128]{2,1,0:T(8,128)S(1)}, f32[2,5,128,128]{3,2,1,0:T(8,128)S(1)}) conditional(s32[]{:T(128)} %convert_element_type.135, (s32[2048]{0:T(1024)S(1)}, s32[128]{0:T(128)S(1)}, bf16[2048,2,128]{0,2,1:T(8,128)(2,1)S(1)}, bf16[128,2,5,128]{3,0,2,1:T(8,128)(2,1)S(1)}, ...), branch_computations={%region_11.13_spmd, %region_14.14_spmd} | conditional | flops 1376848384 | bytes 36321816 | solution.py:84
  464.4 4.7 fusion.21
  477.7 9.7 %conditional.4 = (f32[2,5,128]{2,1,0:T(8,128)S(1)}, f32[2,5,128]{2,1,0:T(8,128)S(1)}, f32[2,5,128,128]{3,2,1,0:T(8,128)S(1)}) conditional(s32[]{:T(128)} %convert_element_type.135, (s32[2048]{0:T(1024)S(1)}, s32[128]{0:T(128)S(1)}, bf16[2048,2,128]{0,2,1:T(8,128)(2,1)S(1)}, bf16[128,2,5,128]{3,0,2,1:T(8,128)(2,1)S(1)}, ...), branch_computations={%region_11.13_spmd, %region_14.14_spmd} | conditional | flops 1376848384 | bytes 36321816 | solution.py:84
  482.7 4.7 fusion.21
  496.1 9.7 %conditional.4 = (f32[2,5,128]{2,1,0:T(8,128)S(1)}, f32[2,5,128]{2,1,0:T(8,128)S(1)}, f32[2,5,128,128]{3,2,1,0:T(8,128)S(1)}) conditional(s32[]{:T(128)} %convert_element_type.135, (s32[2048]{0:T(1024)S(1)}, s32[128]{0:T(128)S(1)}, bf16[2048,2,128]{0,2,1:T(8,128)(2,1)S(1)}, bf16[128,2,5,128]{3,0,2,1:T(8,128)(2,1)S(1)}, ...), branch_computations={%region_11.13_spmd, %region_14.14_spmd} | conditional | flops 1376848384 | bytes 36321816 | solution.py:84
  501.1 4.7 fusion.21
  514.5 9.7 %conditional.4 = (f32[2,5,128]{2,1,0:T(8,128)S(1)}, f32[2,5,128]{2,1,0:T(8,128)S(1)}, f32[2,5,128,128]{3,2,1,0:T(8,128)S(1)}) conditional(s32[]{:T(128)} %convert_element_type.135, (s32[2048]{0:T(1024)S(1)}, s32[128]{0:T(128)S(1)}, bf16[2048,2,128]{0,2,1:T(8,128)(2,1)S(1)}, bf16[128,2,5,128]{3,0,2,1:T(8,128)(2,1)S(1)}, ...), branch_computations={%region_11.13_spmd, %region_14.14_spmd} | conditional | flops 1376848384 | bytes 36321816 | solution.py:84
  519.4 4.7 fusion.21
  525.4 3.0 copy.68
  (155 shorter events, 91.5 us)
Async XLA Ops:
  7.2 113.8 %copy-start = (bf16[5120,256]{1,0:T(8,128)(2,1)S(1)}, bf16[5120,256]{1,0:T(8,128)(2,1)}, u32[]{:S(2)}) copy-start(bf16[5120,256]{1,0:T(8,128)(2,1)} %param.23) | copy-start | bytes 7864324
  7.2 16.9 %copy-start.5 = (s32[256,1]{0,1:T(1,128)S(1)}, s32[256,1]{0,1:T(1,128)}, u32[]{:S(2)}) copy-start(s32[256,1]{0,1:T(1,128)} %param.18) | copy-start | bytes 3076
  7.2 17.1 %copy-start.3 = (bf16[5120]{0:T(1024)(128)(2,1)S(1)}, bf16[5120]{0:T(1024)(128)(2,1)}, u32[]{:S(2)}) copy-start(bf16[5120]{0:T(1024)(128)(2,1)} %param.20) | copy-start | bytes 30724
  11.5 48.9 %all-to-all-start = ((bf16[2,64,4,2560]{3,2,0,1:T(4,128)(2,1)}), bf16[2,64,4,2560]{3,2,0,1:T(4,128)(2,1)}, u32[]{:S(2)}, u32[]{:S(2)}) async-start(bf16[2,64,4,2560]{3,2,0,1:T(4,128)(2,1)} %copy.59), calls=%async_computation | async-start | bytes 5242880 | tf_op jit(solution)/shard_map/all_to_all | solution.py:96
  24.0 97.0 %all-gather.4.cloned.1.call-start = ((), (), s32[]{:S(2)}) async-start(), calls=%async_computation.1 | async-start | bytes 3932160 | tf_op jit(solution)/shard_map/all_gather | solution.py:119
  65.7 5.9 %copy-start.4 = (f32[256,1]{0,1:T(1,128)S(1)}, f32[256,1]{0,1:T(1,128)}, u32[]{:S(2)}) copy-start(f32[256,1]{0,1:T(1,128)} %param.19) | copy-start | bytes 3076
  82.2 127.3 %all-gather.8.cloned.1.call-start = ((), (), s32[]{:S(2)}) async-start(), calls=%async_computation.3 | async-start | bytes 8519680 | tf_op jit(solution)/shard_map/all_gather | solution.py:144
  124.2 6.0 %copy-start.2 = (bf16[256,5120]{1,0:T(8,128)(2,1)S(1)}, bf16[256,5120]{1,0:T(8,128)(2,1)}, u32[]{:S(2)}) copy-start(bf16[256,5120]{1,0:T(8,128)(2,1)} %all-gather.4.cloned.1.call-done) | copy-start | bytes 7864324
  124.2 181.8 %all-gather.6.cloned.1.call-start = ((), (), s32[]{:S(2)}) async-start(), calls=%async_computation.2 | async-start | bytes 8519680 | tf_op jit(solution)/shard_map/all_gather | solution.py:143
  525.4 5.5 %copy-start.1 = (bf16[5120,256]{1,0:T(8,128)(2,1)S(1)}, bf16[5120,256]{1,0:T(8,128)(2,1)}, u32[]{:S(2)}) copy-start(bf16[5120,256]{1,0:T(8,128)(2,1)} %param.23) | copy-start | bytes 7864324
Sparse Core Ops, SparseCore 0:
  82.3 38.6 all-gather.3
  124.4 85.0 all-gather.7
  213.0 93.0 all-gather.5
where the time goes:
time: 540 us; the launch traced here: 537 us
  waiting for transfers between devices  229 us (42%)
  local copies, waits for them, and re-layouts  114 us (21%)
  matrix products  76.9 us (14%)
  other arithmetic  66 us (12%)
  loops' own time  21.2 us (4%)
  between operations  13.9 us (3%)
  starting transfers between devices  12.8 us (2%)
    all_gather x1, waiting for transfers between devices, shards(): lax.all_gather(keys_rot, 'ctx', axis=0, tiled=True)  84.2 us
    all_gather x1, waiting for transfers between devices, shards(): lax.all_gather(values, 'ctx', axis=0, tiled=True)  70.2 us
    dot_general x9, matrix products, compute(): jnp.einsum('hgqk,khd->hgqd', rounded, value_heads, preferred_element_type...  42.6 us
    all_gather x1, waiting for transfers between devices, shards(): normed = lax.all_gather(normed_part, 'tp', axis=1, tiled=True)  38.8 us
    all_to_all x1, waiting for transfers between devices, shards(): lax.all_to_all(expert_out, 'ctx', split_axis=1, concat_axis=0, tiled=True)  36 us
    reduce_sum x9, other arithmetic, compute(): denominator = denominator * rescale + jnp.sum(weights_exp, axis=-1)  22.5 us
    dynamic_slice x8, local copies, waits for them, and re-layouts, advance(): value_piece = lax.dynamic_slice_in_dim(ordered_values, offset, key_block, 0)  22.3 us
    another operation x1, loops' own time, shards(): final_state = lax.fori_loop(0, row_count // key_block, advance, start_state)  20.9 us
  transfers between devices with their start and end apart: 4, of which 4 were waited for; matrix products, arithmetic and copies ran while one was open for 5% of the time, Pallas kernels for 0%

commit v1 on v0

v1 whole, which is shorter than its diff:
```python
import functools
import math

import jax
import jax.numpy as jnp
from jax import lax
from jax.experimental import pallas as pl
from jax.experimental.pallas import tpu as pltpu
from jax.sharding import PartitionSpec as P

HD = 128
ROPE_BASE = 500000.0
NORM_EPS = 1e-05
NEG_FILL = -1e30
NY, NZ, NX, NK = 4, 2, 4, 2
GROUP = 5
HALF = 128
VMEM_LIMIT = 56 * 1024 * 1024


def split_index(c):
    return c // (NZ * NX * NK), (c // (NX * NK)) % NZ, (c // NK) % NX, c % NK


def join_index(y, z, x, k):
    return (((y % NY) * NZ + z % NZ) * NX + x % NX) * NK + k % NK


def permute(value, move):
    pairs = [(c, join_index(*move(*split_index(c)))) for c in range(NY * NZ * NX * NK)]
    return lax.ppermute(value, "ctx", pairs)


def core_swap(value):
    return permute(value, lambda y, z, x, k: (y, z, x, 1 - k))


def z_swap(value):
    return permute(value, lambda y, z, x, k: (y, 1 - z, x, k))


def first_axis(value, step):
    return permute(
        value, lambda y, z, x, k: (y, z, x - step, k) if k == 0 else (y - step, z, x, k)
    )


def second_axis(value, step):
    return permute(
        value, lambda y, z, x, k: (y - step, z, x, k) if k == 0 else (y, z, x - step, k)
    )


def params():
    return pltpu.CompilerParams(vmem_limit_bytes=VMEM_LIMIT)


def vmem():
    return pl.BlockSpec(memory_space=pltpu.VMEM)


def smem():
    return pl.BlockSpec(memory_space=pltpu.SMEM)


def pick_kernel(ids_col, ids_row, gate, returned, residual, shared, out, hot):
    @pl.when(pl.program_id(0) == 0)
    def _():
        rows = ids_col.shape[0]
        same = ids_col[...] == ids_row[...]
        row = lax.broadcasted_iota(jnp.int32, (rows, rows), 0)
        col = lax.broadcasted_iota(jnp.int32, (rows, rows), 1)
        slot = jnp.sum(jnp.where(same & (col < row), 1.0, 0.0), axis=1, keepdims=True)
        place = ids_col[...] * 4 + slot.astype(jnp.int32)
        lanes = lax.broadcasted_iota(jnp.int32, hot.shape, 1)
        hot[...] = jnp.where(lanes == place, 1.0, 0.0).astype(jnp.bfloat16)

    picked = jnp.dot(hot[...], returned[...], preferred_element_type=jnp.float32)
    total = residual[...].astype(jnp.float32) + shared[...].astype(jnp.float32)
    out[...] = (total + gate[...] * picked).astype(jnp.bfloat16)


def pick(ids, gate, returned, residual, shared):
    rows, width = residual.shape
    slots = returned.shape[0]
    block = 640
    wide = pl.BlockSpec((rows, block), lambda i: (0, i))
    return pl.pallas_call(
        pick_kernel,
        grid=(width // block,),
        in_specs=[
            pl.BlockSpec((rows, 1), lambda i: (0, 0)),
            pl.BlockSpec((1, rows), lambda i: (0, 0)),
            pl.BlockSpec((rows, 1), lambda i: (0, 0)),
            pl.BlockSpec((slots, block), lambda i: (0, i)),
            wide,
            wide,
        ],
        out_specs=wide,
        out_shape=jax.ShapeDtypeStruct((rows, width), jnp.bfloat16),
        scratch_shapes=[pltpu.VMEM((rows, slots), jnp.bfloat16)],
        compiler_params=params(),
        name="pick",
    )(ids, ids.reshape(1, rows), gate, returned, residual, shared)


def turn(x, cos, sin):
    return x * cos + pltpu.roll(x, HD // 2, 1) * sin


def key_value_kernel(h0, h1, gain, wk, wv, cos, sin, kv, normed):
    half = h0.shape[1]
    lo = h0[...].astype(jnp.float32)
    hi = h1[...].astype(jnp.float32)
    squares = jnp.sum(lo * lo, axis=1, keepdims=True) + jnp.sum(hi * hi, axis=1, keepdims=True)
    scale = lax.rsqrt(squares / (2 * half) + NORM_EPS)
    normed[:, :half] = (lo * scale * gain[:, :half].astype(jnp.float32)).astype(jnp.bfloat16)
    normed[:, half:] = (hi * scale * gain[:, half:].astype(jnp.float32)).astype(jnp.bfloat16)
    keys = jnp.dot(normed[...], wk[...], preferred_element_type=jnp.float32)
    values = jnp.dot(normed[...], wv[...], preferred_element_type=jnp.float32)
    for head in range(2):
        cols = slice(head * HD, (head + 1) * HD)
        kv[head, :, :HD] = turn(keys[:, cols], cos[...], sin[...]).astype(jnp.bfloat16)
        kv[head, :, HD:] = values[:, cols].astype(jnp.bfloat16)


def key_value(h0, h1, gain, wk, wv, cos, sin):
    rows, half = h0.shape
    return pl.pallas_call(
        key_value_kernel,
        in_specs=[vmem()] * 7,
        out_specs=[vmem()] * 2,
        out_shape=[
            jax.ShapeDtypeStruct((2, rows, 2 * HD), jnp.bfloat16),
            jax.ShapeDtypeStruct((rows, 2 * half), jnp.bfloat16),
        ],
        compiler_params=params(),
        cost_estimate=pl.CostEstimate(
            flops=2 * rows * 2 * half * 512, bytes_accessed=9_000_000, transcendentals=rows
        ),
        name="key_value",
    )(h0, h1, gain, wk, wv, cos, sin)


def query_kernel(factor, normed, wq, cos, sin, out):
    prod = jnp.dot(normed[...], wq[...], preferred_element_type=jnp.float32)
    for head in range(out.shape[0]):
        turned = turn(prod[:, head * HD : (head + 1) * HD], cos[...], sin[...])
        out[head] = (turned * factor).astype(jnp.bfloat16)


def query(normed, wq, cos, sin):
    rows, width = normed.shape
    heads = wq.shape[1] // HD
    per = 2
    factor = 1.0 / HD**0.5 * math.log2(math.e)
    return pl.pallas_call(
        functools.partial(query_kernel, factor),
        grid=(heads // per,),
        in_specs=[
            pl.BlockSpec((rows, width), lambda i: (0, 0)),
            pl.BlockSpec((width, per * HD), lambda i: (0, i)),
            pl.BlockSpec((rows, HD), lambda i: (0, 0)),
            pl.BlockSpec((rows, HD), lambda i: (0, 0)),
        ],
        out_specs=pl.BlockSpec((per, rows, HD), lambda i: (i, 0, 0)),
        out_shape=jax.ShapeDtypeStruct((heads, rows, HD), jnp.bfloat16),
        compiler_params=params(),
        cost_estimate=pl.CostEstimate(
            flops=2 * rows * width * heads * HD, bytes_accessed=17_000_000, transcendentals=0
        ),
        name="query",
    )(normed, wq, cos, sin)


def attend_kernel(counts, diag, resume, finish, *refs):
    flags, q, refs = refs[0], refs[1], refs[2:]
    kvs, refs = refs[: len(counts)], refs[len(counts) :]
    if resume:
        olds, refs = refs[:3], refs[3:]
    if finish:
        outs, (acc, den, top) = refs[:2], refs[2:]
    else:
        outs, (acc, den, top) = None, refs[:3]
    ones = jnp.ones((2 * HALF, HD), jnp.bfloat16)

    if resume:
        acc[...] = olds[0][...]
        den[...] = olds[1][...]
        top[...] = olds[2][...]
    else:
        acc[...] = jnp.zeros_like(acc)
        den[...] = jnp.zeros_like(den)
        top[...] = jnp.full_like(top, NEG_FILL)

    def rows_of(ref, lead, early, cols):
        at = pl.ds(early * HALF, HALF)
        if isinstance(lead, tuple):
            return jnp.concatenate([ref[0, lead[0], at, cols], ref[1, lead[0], at, cols]], axis=0)
        return jnp.concatenate([ref[lead, 0, at, cols], ref[lead, 1, at, cols]], axis=0)

    def update(side, head, keys, values, mask):
        query_rows = rows_of(q, (head,), side, slice(None))
        scores = lax.dot_general(
            query_rows, keys, (((1,), (1,)), ((), ())), preferred_element_type=jnp.float32
        )
        if mask is not None:
            scores = jnp.where(mask, scores, NEG_FILL)
        old = top[side, head]
        new = jnp.maximum(old, jnp.max(scores, axis=1, keepdims=True))
        weights = jnp.exp2(scores - new[:, :1]).astype(jnp.bfloat16)
        wide = jnp.concatenate([values, jnp.concatenate([ones] * (keys.shape[0] // ones.shape[0]))], axis=1)
        prod = jnp.dot(weights, wide, preferred_element_type=jnp.float32)
        keep = jnp.exp2(old - new)
        acc[side, head] = acc[side, head] * keep + prod[:, :HD]
        den[side, head] = den[side, head] * keep + prod[:, HD:]
        top[side, head] = new

    def per_head(head, carry):
        if diag:
            core = flags[0]
            row = lax.broadcasted_iota(jnp.int32, (2 * HALF, 2 * HALF), 0)
            col = lax.broadcasted_iota(jnp.int32, (2 * HALF, 2 * HALF), 1)
            for side in (0, 1):
                first = core if side == 0 else 1 - core
                row_pos = jnp.where(row < HALF, row + first * HALF, row - first * HALF)
                col_pos = jnp.where(col < HALF, col + first * HALF, col - first * HALF)
                update(
                    side,
                    head,
                    rows_of(kvs[0], 0, side, slice(0, HD)),
                    rows_of(kvs[0], 0, side, slice(HD, 2 * HD)),
                    col_pos <= row_pos,
                )
        start = 0
        for index, count in enumerate(counts):
            for base in range(0, count, 4):
                picks = range(base, min(base + 4, count))
                update(
                    1,
                    head,
                    jnp.concatenate([rows_of(kvs[index], b, 0, slice(0, HD)) for b in picks]),
                    jnp.concatenate([rows_of(kvs[index], b, 0, slice(HD, 2 * HD)) for b in picks]),
                    None,
                )
            for b in range(count):
                if diag and index == 0 and b == 0:
                    continue
                side = 1 - flags[start + b]
                update(
                    side,
                    head,
                    rows_of(kvs[index], b, side, slice(0, HD)),
                    rows_of(kvs[index], b, side, slice(HD, 2 * HD)),
                    None,
                )
            start += count
        return carry

    lax.fori_loop(0, GROUP, per_head, 0)

    if finish:
        part, logs = outs
        total = den[...]
        some = total > 0.0
        part[...] = jnp.where(some, acc[...] / jnp.where(some, total, 1.0), 0.0).astype(jnp.bfloat16)
        level = jnp.where(some, top[...] + jnp.log2(jnp.where(some, total, 1.0)), NEG_FILL)
        tiles = level.reshape(2 * GROUP * 2, HD, HD)
        row = lax.broadcasted_iota(jnp.int32, tiles.shape, 1)
        col = lax.broadcasted_iota(jnp.int32, tiles.shape, 2)
        logs[...] = jnp.sum(jnp.where(row == col, tiles, 0.0), axis=1)


STATE = (2, GROUP, 2 * HALF, HD)


def attend(flags, q, kvs, state, diag=False, finish=False):
    counts = tuple(kv.shape[0] for kv in kvs)
    state_shapes = [jax.ShapeDtypeStruct(STATE, jnp.float32)] * 3
    olds = [] if state is None else list(state)
    if finish:
        shapes = [
            jax.ShapeDtypeStruct(STATE, jnp.bfloat16),
            jax.ShapeDtypeStruct((4 * GROUP, HD), jnp.float32),
        ]
        scratch = [pltpu.VMEM(STATE, jnp.float32)] * 3
    else:
        shapes, scratch = state_shapes, []
    n = sum(counts)
    return pl.pallas_call(
        functools.partial(attend_kernel, counts, diag, state is not None, finish),
        in_specs=[smem()] + [vmem()] * (1 + len(kvs) + len(olds)),
        out_specs=[vmem()] * len(shapes),
        out_shape=shapes,
        scratch_shapes=scratch,
        compiler_params=params(),
        cost_estimate=pl.CostEstimate(
            flops=n * 2 * 1280 * 256 * 128 * 8,
            bytes_accessed=n * 262144 + 4_000_000,
            transcendentals=n * 2 * 1280 * 256,
        ),
        name="attend",
    )(flags, q, *kvs, *olds)


def merge_kernel(acc, den, top, part, logs, out):
    row = lax.broadcasted_iota(jnp.int32, (HD, HD), 0)
    col = lax.broadcasted_iota(jnp.int32, (HD, HD), 1)
    for side in range(2):
        for head in range(GROUP):
            for core in range(2):
                rows = slice(core * HALF, (core + 1) * HALF)
                total = den[side, head, rows]
                line = logs[pl.ds((side * GROUP + head) * 2 + core, 1), :]
                other = jnp.sum(jnp.where(row == col, line, 0.0), axis=1, keepdims=True)
                mine = top[side, head, rows] + jnp.log2(total)
                high = jnp.maximum(mine, other)
                first = jnp.exp2(mine - high)
                second = jnp.exp2(other - high)
                value = acc[side, head, rows] / total * first
                value = value + part[side, head, rows].astype(jnp.float32) * second
                out[core, side, :, head * HD : (head + 1) * HD] = (value / (first + second)).astype(
                    jnp.bfloat16
                )


def merge(state, part, logs):
    return pl.pallas_call(
        merge_kernel,
        in_specs=[vmem()] * 5,
        out_specs=vmem(),
        out_shape=jax.ShapeDtypeStruct((2, 2, HALF, GROUP * HD), jnp.bfloat16),
        compiler_params=params(),
        name="merge",
    )(*state, part, logs)


def rotations(ctx_index, rows):
    row = jnp.arange(rows, dtype=jnp.int32)
    half = rows // 2
    count = NY * NZ * NX * NK
    pos = jnp.where(row < half, ctx_index * half + row, (2 * count - 1 - ctx_index) * half + row - half)
    frequency = ROPE_BASE ** (-(jnp.arange(HD // 2, dtype=jnp.float32) * 2.0 / HD))
    angles = pos.astype(jnp.float32)[:, None] * frequency[None, :]
    cos, sin = jnp.cos(angles), jnp.sin(angles)
    return jnp.concatenate([cos, cos], axis=1), jnp.concatenate([-sin, sin], axis=1)


def chip_order(y, z, x):
    return (y * NZ + z) * NX + x


def shards(residual, shared_out, expert_out, routing, gate_score, norm_gain, w_query, w_key, w_value):
    rows, half_width = residual.shape
    ctx_index = lax.axis_index("ctx")
    tp_index = lax.axis_index("tp")
    y, z, x, k = split_index(ctx_index)
    cos, sin = rotations(ctx_index, rows)

    own_experts, sources, slots, _ = expert_out.shape
    outgoing = jnp.transpose(expert_out, (1, 0, 2, 3)).reshape(sources, own_experts * slots, half_width)
    returned = lax.all_to_all(outgoing, "ctx", split_axis=0, concat_axis=0, tiled=True)
    returned = returned.reshape(sources * own_experts * slots, half_width)
    hidden = pick(routing, gate_score, returned, residual, shared_out)

    other = lax.ppermute(hidden, "tp", [(0, 1), (1, 0)])
    h0 = jnp.where(tp_index == 0, hidden, other)
    h1 = jnp.where(tp_index == 0, other, hidden)
    kv, normed = key_value(h0, h1, norm_gain.reshape(1, -1), w_key, w_value, cos, sin)
    kv_mine = lax.dynamic_index_in_dim(kv, k, 0, keepdims=False)
    kv_other = lax.dynamic_index_in_dim(kv, 1 - k, 0, keepdims=False)
    block = jnp.stack([kv_mine, core_swap(kv_other)])[None]

    near = [first_axis(block, step) for step in (1, -1, 2)]

    queries = query(normed, w_query, cos, sin).reshape(2, GROUP, rows, HD)
    q_mine = lax.dynamic_index_in_dim(queries, k, 0, keepdims=False)
    q_other = lax.dynamic_index_in_dim(queries, 1 - k, 0, keepdims=False)
    q_own = jnp.stack([q_mine, core_swap(q_other)])
    q_pair = z_swap(q_own)

    line = jnp.concatenate([block] + near)
    far = [second_axis(line, step) for step in (1, -1, 2)]

    steps = jnp.array([0, 1, -1, 2], jnp.int32)

    def before(first, second, chip):
        by = jnp.where(k == 0, second, first)
        bx = jnp.where(k == 0, first, second)
        return (chip_order((y + by) % NY, z, (x + bx) % NX) < chip).astype(jnp.int32)

    own_chip = chip_order(y, z, x)
    pair_chip = chip_order(y, 1 - z, x)
    zero = jnp.zeros((4,), jnp.int32)
    own_near = before(steps, zero, own_chip).at[0].set(k)
    pair_near = before(steps, zero, pair_chip)
    own_far = jnp.concatenate([before(steps, zero + s, own_chip) for s in (1, -1, 2)])
    pair_far = jnp.concatenate([before(steps, zero + s, pair_chip) for s in (1, -1, 2)])

    own_state = attend(own_near, q_own, [line], None, diag=True)
    pair_state = attend(pair_near, q_pair, [line], None)
    pair_state = attend(pair_far[:8], q_pair, far[:2], pair_state)
    part, logs = attend(pair_far[8:], q_pair, far[2:], pair_state, finish=True)
    part = z_swap(part)
    logs = z_swap(logs)
    own_state = attend(own_far, q_own, far, own_state)
    out = merge(own_state, part, logs)
    keep = lax.dynamic_index_in_dim(out, 0, 0, keepdims=False).reshape(rows, GROUP * HD)
    sent = core_swap(out[1].reshape(rows, GROUP * HD))
    attended = jnp.where(
        k == 0,
        jnp.concatenate([keep, sent], axis=1),
        jnp.concatenate([sent, keep], axis=1),
    )
    return hidden, attended


def solution(mesh):
    return jax.shard_map(
        shards,
        mesh=mesh,
        in_specs=(
            P("ctx", "tp"),
            P("ctx", "tp"),
            P("ctx", None, None, "tp"),
            P("ctx", None),
            P("ctx", None),
            P(),
            P(None, "tp"),
            P(None, "tp"),
            P(None, "tp"),
        ),
        out_specs=(P("ctx", "tp"), P("ctx", "tp")),
        check_vma=False,
    )
```

time: 540 us -> 228 us (0.42)
  waiting for transfers between devices: 229 us -> 70.7 us
  Pallas kernels: 0 us -> 108 us
  local copies, waits for them, and re-layouts: 114 us -> 16.7 us
  matrix products: 76.9 us -> 0 us
  other arithmetic: 66 us -> 7.48 us
  loops' own time: 21.2 us -> 0 us
  between operations: 13.9 us -> 0.81 us
  starting transfers between devices: 12.8 us -> 24.4 us
    all_gather x3 -> x0, waiting for transfers between devices: 193 us -> none  [the longest x1 84.2 us: shards(): lax.all_gather(keys_rot, 'ctx', axis=0, tiled=True)]
    pallas_call x0 -> x9, Pallas kernels: none -> 108 us  [the longest x5 81.9 us: attend(): pl.pallas_call(functools.partial(attend_kernel, counts, diag, state is no...]
    dot_general x22 -> x0, matrix products: 76.9 us -> none  [the longest x9 42.6 us: compute(): jnp.einsum('hgqk,khd->hgqd', rounded, value_heads, preferred_element_type...]
    ppermute x0 -> x13, waiting for transfers between devices: none -> 35.8 us  [the longest x1 27.4 us: shards(): other = lax.ppermute(hidden, 'tp', [(0, 1), (1, 0)])]
    reduce_sum x10 -> x0, other arithmetic: 26.5 us -> none  [the longest x9 22.5 us: compute(): denominator = denominator * rescale + jnp.sum(weights_exp, axis=-1)]
    another operation x4 -> x0, local copies, waits for them, and re-layouts: 25.6 us -> none  [the longest x2 12.8 us: position_order(): split[:, 0].reshape((shard_count * (tok_rows // 2),) + rows.shape[1:])]
    slice x19 -> x0, local copies, waits for them, and re-layouts: 23.4 us -> none  [the longest x3 12.1 us: position_order(): split[:, 0].reshape((shard_count * (tok_rows // 2),) + rows.shape[1:])]
    concatenate x27 -> x4, other arithmetic: 24.7 us -> 2.31 us  [the longest x1 0.86 us: rotations(): jnp.concatenate([cos, cos], axis=1)]
  transfers between devices with their start and end apart: 4 -> 14, of which waited for: 4 -> 6; matrix products, arithmetic and copies ran while one was open for 5% -> 3% of each run, Pallas kernels for 0% -> 35%
where the time goes in v1:
time: 228 us
  Pallas kernels  108 us (47%)
  waiting for transfers between devices  70.7 us (31%)
  starting transfers between devices  24.4 us (11%)
  local copies, waits for them, and re-layouts  16.7 us (7%)
  other arithmetic  7.48 us (3%)
    pallas_call x5, Pallas kernels, attend(): pl.pallas_call(functools.partial(attend_kernel, counts, diag, state is no...  81.9 us
    all_to_all x1, waiting for transfers between devices, shards(): lax.all_to_all(outgoing, 'ctx', split_axis=0, concat_axis=0, tiled=True)  34.9 us
    ppermute x1, waiting for transfers between devices, shards(): other = lax.ppermute(hidden, 'tp', [(0, 1), (1, 0)])  27.4 us
    all_to_all x1, starting transfers between devices, shards(): lax.all_to_all(outgoing, 'ctx', split_axis=0, concat_axis=0, tiled=True)  12.4 us
    ppermute x12, starting transfers between devices, permute(): return lax.ppermute(value, 'ctx', pairs)  11.2 us
    unnamed x31, local copies, waits for them, and re-layouts  9.91 us
    pallas_call x1, Pallas kernels, query(): pl.pallas_call(functools.partial(query_kernel, factor), grid=(heads // pe...  9.62 us
    ppermute x12, waiting for transfers between devices, permute(): return lax.ppermute(value, 'ctx', pairs)  8.4 us
  transfers between devices with their start and end apart: 14, of which 6 were waited for; matrix products, arithmetic and copies ran while one was open for 3% of the time, Pallas kernels for 35%

profile of v1, /device:TPU:1, one launch (start us, length us, event | category | flops | bytes accessed | tf_op | source)
XLA Modules:
  0.0 227.7 jit_solution(10438768376828751857)
XLA Ops:
  0.6 2.2 copy.18
  2.8 2.9 %copy.19 = bf16[64,8,2560]{2,1,0:T(8,128)(2,1)} copy(bf16[64,8,2560]{2,0,1:T(8,128)(2,1)S(1)} %bitcast.18) | data formatting | bytes 5242880 | tf_op jit(solution)/shard_map/reshape | solution.py:361
  5.7 12.4 %all-to-all-start = ((bf16[64,8,2560]{2,1,0:T(8,128)(2,1)}), bf16[64,8,2560]{2,1,0:T(8,128)(2,1)S(1)}, u32[]{:S(2)}, u32[]{:S(2)}) async-start(bf16[64,8,2560]{2,1,0:T(8,128)(2,1)} %copy.19), calls=%async_computation | async-start | bytes 5242880 | tf_op jit(solution)/shard_map/all_to_all | solution.py:362
  18.2 0.8 copy.20.ids_col
  19.0 0.8 copy.21.gate
  19.8 34.9 %all-to-all-done = bf16[64,8,2560]{2,1,0:T(8,128)(2,1)S(1)} async-done(((bf16[64,8,2560]{2,1,0:T(8,128)(2,1)}), bf16[64,8,2560]{2,1,0:T(8,128)(2,1)S(1)}, u32[]{:S(2)}, u32[]{:S(2)}) %all-to-all-start) | async-done | bytes 2621472 | tf_op jit(solution)/shard_map/all_to_all | solution.py:362
  54.7 1.5 copy-done
  56.1 5.3 %pick.1 = bf16[256,2560]{1,0:T(8,128)(2,1)} custom-call(s32[256,1]{1,0:T(8,128)} %copy.20.ids_col, s32[1,256]{1,0:T(1,128)} %bitcast.24, f32[256,1]{1,0:T(8,128)} %copy.21.gate, bf16[512,2560]{1,0:T(8,128)(2,1)} %bitcast.17, bf16[256,2560]{1,0:T(8,128)(2,1)} %residual.1, bf16[256,2560]{1,0:T(8,128)(2,1)} %shared.1), custom_call_target="tpu_custom_call" | custom-call | tf_op jit(solution)/shard_map/pick/pallas_call | solution.py:88
  61.5 0.7 collective-permute-start
  62.2 0.6 reshape.68.gain
  62.8 0.5 fusion
  63.4 0.9 pad_maximum_fusion.2
  64.3 0.5 compare_convert_fusion
  64.8 27.4 %collective-permute-done = bf16[256,2560]{1,0:T(8,128)(2,1)S(1)} collective-permute-done((bf16[256,2560]{1,0:T(8,128)(2,1)}, bf16[256,2560]{1,0:T(8,128)(2,1)S(1)}, u32[]{:S(2)}, u32[]{:S(2)}) %collective-permute-start) | collective-permute-done | bytes 1310752 | tf_op jit(solution)/shard_map/ppermute | solution.py:366
  92.2 3.0 %broadcast_select_fusion = (bf16[256,2560]{1,0:T(8,128)(2,1)}, bf16[256,2560]{1,0:T(8,128)(2,1)}) fusion(bf16[256,2560]{1,0:T(8,128)(2,1)S(1)} %collective-permute-done, bf16[256,2560]{1,0:T(8,128)(2,1)} %pick.1, pred[]{:T(512)S(6)} %eq.45), kind=kLoop, calls=%fused_computation | loop fusion | flops 1310720 | bytes 5242881 | tf_op jit(solution)/shard_map/jit(_where)/select_n | solution.py:368
  95.2 6.7 %key_value.1 = (bf16[2,256,256]{2,1,0:T(8,128)(2,1)}, bf16[256,5120]{1,0:T(8,128)(2,1)}) custom-call(bf16[256,2560]{1,0:T(8,128)(2,1)} %get-tuple-element.55.h0, bf16[256,2560]{1,0:T(8,128)(2,1)} %get-tuple-element.54.h1, bf16[1,5120]{1,0:T(2,128)(2,1)} %reshape.68.gain, bf16[5120,256]{1,0:T(8,128)(2,1)} %wk.1, bf16[5120,256]{1,0:T(8,128)(2,1)} %wv.1, ...), custom_call_target="tpu_custom_call" | custom-call | flops 1342177280 | bytes 9000000 | tf_op jit(solution)/shard_map/key_value/pallas_call | solution.py:129
  101.9 1.0 constant_dynamic-slice_fusion
  102.9 0.8 collective-permute-start.2
  103.6 9.6 %query.1 = bf16[10,256,128]{2,1,0:T(8,128)(2,1)} custom-call(bf16[256,5120]{1,0:T(8,128)(2,1)} %get-tuple-element.30.normed, bf16[5120,1280]{1,0:T(8,128)(2,1)} %wq.1, f32[256,128]{1,0:T(8,128)} %get-tuple-element.73.cos, f32[256,128]{1,0:T(8,128)} %get-tuple-element.74.sin), custom_call_target="tpu_custom_call" | custom-call | flops 3355443200 | bytes 17000000 | tf_op jit(solution)/shard_map/query/pallas_call | solution.py:157
  113.3 0.9 collective-permute-start.3
  114.1 0.7 collective-permute-start.4
  114.8 0.7 collective-permute-start.5
  115.5 1.1 constant_dynamic-slice_fusion.1
  116.8 2.1 collective-permute-done.3
  118.9 4.6 %collective-permute-done.4 = bf16[1,2,256,256]{3,2,1,0:T(8,128)(2,1)S(1)} collective-permute-done((bf16[1,2,256,256]{3,2,1,0:T(8,128)(2,1)S(1)}, bf16[1,2,256,256]{3,2,1,0:T(8,128)(2,1)S(1)}, u32[]{:S(2)}, u32[]{:S(2)}) %collective-permute-start.4) | collective-permute-done | bytes 262176 | tf_op jit(solution)/shard_map/ppermute | solution.py:31
  123.7 1.5 collective-permute-start.7
  125.3 0.7 add_convert_fusion.1.refs_0_
  126.0 0.6 collective-permute-start.8
  126.7 0.6 add_convert_fusion.refs_0_
  127.3 0.5 copy-done.13
  127.8 13.8 %attend.5 = (f32[2,5,256,128]{3,2,1,0:T(8,128)}, f32[2,5,256,128]{3,2,1,0:T(8,128)}, f32[2,5,256,128]{3,2,1,0:T(8,128)}) custom-call(s32[4]{0:T(128)} %copy-done.13, bf16[2,5,256,128]{3,2,1,0:T(8,128)(2,1)} %copy-done.3, bf16[4,2,256,256]{3,2,1,0:T(8,128)(2,1)} %copy-done.1), custom_call_target="tpu_custom_call" | custom-call | flops 2684354560 | bytes 5048576 | tf_op jit(solution)/shard_map/attend/pallas_call | solution.py:290
  141.7 0.4 collective-permute-done.9.refs_1_
  142.1 0.9 copy-done.12
  143.0 11.1 %attend.7 = (f32[2,5,256,128]{3,2,1,0:T(8,128)}, f32[2,5,256,128]{3,2,1,0:T(8,128)}, f32[2,5,256,128]{3,2,1,0:T(8,128)}) custom-call(s32[4]{0:T(128)} %get-tuple-element.46.refs_0_, bf16[2,5,256,128]{3,2,1,0:T(8,128)(2,1)} %copy-done.12, bf16[4,2,256,256]{3,2,1,0:T(8,128)(2,1)} %copy-done.1), custom_call_target="tpu_custom_call" | custom-call | flops 2684354560 | bytes 5048576 | tf_op jit(solution)/shard_map/attend/pallas_call | solution.py:290
  154.1 1.0 copy-done.9
  155.1 0.3 copy-done.10
  155.4 19.2 %attend.8 = (f32[2,5,256,128]{3,2,1,0:T(8,128)}, f32[2,5,256,128]{3,2,1,0:T(8,128)}, f32[2,5,256,128]{3,2,1,0:T(8,128)}) custom-call(s32[8]{0:T(128)} %add_convert_fusion.1.refs_0_, bf16[2,5,256,128]{3,2,1,0:T(8,128)(2,1)} %copy-done.12, bf16[4,2,256,256]{3,2,1,0:T(8,128)(2,1)} %copy-done.9, bf16[4,2,256,256]{3,2,1,0:T(8,128)(2,1)} %copy-done.10, ...), custom_call_target="tpu_custom_call" | custom-call | flops 5368709120 | bytes 6097152 | tf_op jit(solution)/shard_map/attend/pallas_call | solution.py:290
  174.6 1.1 copy-done.11
  175.7 11.7 %attend.9 = (bf16[2,5,256,128]{3,2,1,0:T(8,128)(2,1)}, f32[20,128]{1,0:T(8,128)}) custom-call(s32[4]{0:T(128)} %get-tuple-element.69.refs_0_, bf16[2,5,256,128]{3,2,1,0:T(8,128)(2,1)} %copy-done.12, bf16[4,2,256,256]{3,2,1,0:T(8,128)(2,1)} %copy-done.11, f32[2,5,256,128]{3,2,1,0:T(8,128)} %get-tuple-element.41.refs_3_, ...), custom_call_target="tpu_custom_call" | custom-call | flops 2684354560 | bytes 5048576 | tf_op jit(solution)/shard_map/attend/pallas_call | solution.py:290
  187.4 1.9 collective-permute-start.10
  189.3 1.1 collective-permute-start.11
  190.4 26.1 %attend.6 = (f32[2,5,256,128]{3,2,1,0:T(8,128)}, f32[2,5,256,128]{3,2,1,0:T(8,128)}, f32[2,5,256,128]{3,2,1,0:T(8,128)}) custom-call(s32[12]{0:T(128)} %add_convert_fusion.refs_0_, bf16[2,5,256,128]{3,2,1,0:T(8,128)(2,1)} %copy-done.3, bf16[4,2,256,256]{3,2,1,0:T(8,128)(2,1)} %copy-done.9, bf16[4,2,256,256]{3,2,1,0:T(8,128)(2,1)} %copy-done.10, ...), custom_call_target="tpu_custom_call" | custom-call | flops 8053063680 | bytes 7145728 | tf_op jit(solution)/shard_map/attend/pallas_call | solution.py:290
  216.5 0.6 copy-done.4
  217.3 4.1 %merge.1 = bf16[2,2,128,640]{3,2,1,0:T(8,128)(2,1)} custom-call(f32[2,5,256,128]{3,2,1,0:T(8,128)} %get-tuple-element.35.acc, f32[2,5,256,128]{3,2,1,0:T(8,128)} %get-tuple-element.36.den, f32[2,5,256,128]{3,2,1,0:T(8,128)} %get-tuple-element.37.top, bf16[2,5,256,128]{3,2,1,0:T(8,128)(2,1)} %copy-done.2, f32[20,128]{1,0:T(8,128)} %copy-done.4), custom_call_target="tpu_custom_call" | custom-call | tf_op jit(solution)/shard_map/merge/pallas_call | solution.py:328
  221.4 1.1 fusion.38
  222.6 2.9 %collective-permute-start.12 = (bf16[256,640]{1,0:T(8,128)(2,1)S(1)}, bf16[256,640]{1,0:T(8,128)(2,1)S(1)}, u32[]{:S(2)}, u32[]{:S(2)}) collective-permute-start(bf16[256,640]{1,0:T(8,128)(2,1)S(1)} %bitcast.22), channel_id=1, source_target_pairs={{0,2},{2,0},{4,6},{6,4},{8,10},{10,8},{12,14},{14,12},{16,18},{18,... | collective-permute-start | bytes 983048 | tf_op jit(solution)/shard_map/ppermute | solution.py:31
  225.5 1.3 collective-permute-done.12
  226.7 1.0 maximum_select_fusion
  (41 shorter events, 0.8 us)
Async XLA Ops:
  5.7 12.4 %copy-start.6 = (s32[256,1]{0,1:T(1,128)S(1)}, s32[256,1]{0,1:T(1,128)}, u32[]{:S(2)}) copy-start(s32[256,1]{0,1:T(1,128)} %param.15) | copy-start | bytes 3076
  5.7 13.3 %copy-start.7 = (f32[256,1]{0,1:T(1,128)S(1)}, f32[256,1]{0,1:T(1,128)}, u32[]{:S(2)}) copy-start(f32[256,1]{0,1:T(1,128)} %param.16) | copy-start | bytes 3076
  5.7 48.9 %all-to-all-start = ((bf16[64,8,2560]{2,1,0:T(8,128)(2,1)}), bf16[64,8,2560]{2,1,0:T(8,128)(2,1)S(1)}, u32[]{:S(2)}, u32[]{:S(2)}) async-start(bf16[64,8,2560]{2,1,0:T(8,128)(2,1)} %copy.19), calls=%async_computation | async-start | bytes 5242880 | tf_op jit(solution)/shard_map/all_to_all | solution.py:362
  54.7 1.5 copy-start
  56.1 6.1 %copy-start.5 = (bf16[5120]{0:T(1024)(128)(2,1)S(1)}, bf16[5120]{0:T(1024)(128)(2,1)}, u32[]{:S(2)}) copy-start(bf16[5120]{0:T(1024)(128)(2,1)} %param.17) | copy-start | bytes 30724
  56.1 8.1 %copy-start.8 = (s32[4]{0:T(128)S(1)}, s32[4]{0:T(128)}, u32[]{:S(2)}) copy-start(s32[4]{0:T(128)} %constant.196.clone) | copy-start | bytes 52
  61.5 30.7 %collective-permute-start = (bf16[256,2560]{1,0:T(8,128)(2,1)}, bf16[256,2560]{1,0:T(8,128)(2,1)S(1)}, u32[]{:S(2)}, u32[]{:S(2)}) collective-permute-start(bf16[256,2560]{1,0:T(8,128)(2,1)} %pick.1), channel_id=1, source_target_pairs={{0,1},{1,0},{2,3},{3,2},{4,5},{5,4},{6,7},{7,6},{8,9},{9,8},{10,11... | collective-permute-start | bytes 3932168 | tf_op jit(solution)/shard_map/ppermute | solution.py:366
  102.9 10.4 %collective-permute-start.2 = (bf16[256,256]{1,0:T(8,128)(2,1)S(1)}, bf16[256,256]{1,0:T(8,128)(2,1)S(1)}, u32[]{:S(2)}, u32[]{:S(2)}) collective-permute-start(bf16[256,256]{1,0:T(8,128)(2,1)S(1)} %get-tuple-element.61), channel_id=1, source_target_pairs={{0,2},{2,0},{4,6},{6,4},{8,10},{10,8},{12,14},{14,12},{16,18},{18,... | collective-permute-start | bytes 393224 | tf_op jit(solution)/shard_map/ppermute | solution.py:31
  113.3 5.6 %collective-permute-start.3 = (bf16[1,2,256,256]{3,2,1,0:T(8,128)(2,1)S(1)}, bf16[1,2,256,256]{3,2,1,0:T(8,128)(2,1)S(1)}, u32[]{:S(2)}, u32[]{:S(2)}) collective-permute-start(bf16[1,2,256,256]{3,2,1,0:T(8,128)(2,1)S(1)} %maximum_bitcast_fusion), channel_id=1, source_target_pairs={{0,12},{2,98},{4,0},{6,102},{8,4},{10,106},{12,8},{14,110},{16,28}... | collective-permute-start | bytes 786440 | tf_op jit(solution)/shard_map/ppermute | solution.py:31
  114.1 9.3 %collective-permute-start.4 = (bf16[1,2,256,256]{3,2,1,0:T(8,128)(2,1)S(1)}, bf16[1,2,256,256]{3,2,1,0:T(8,128)(2,1)S(1)}, u32[]{:S(2)}, u32[]{:S(2)}) collective-permute-start(bf16[1,2,256,256]{3,2,1,0:T(8,128)(2,1)S(1)} %maximum_bitcast_fusion), channel_id=1, source_target_pairs={{0,4},{2,34},{4,8},{6,38},{8,12},{10,42},{12,0},{14,46},{16,20},{1... | collective-permute-start | bytes 786440 | tf_op jit(solution)/shard_map/ppermute | solution.py:31
  114.8 8.7 %collective-permute-start.5 = (bf16[1,2,256,256]{3,2,1,0:T(8,128)(2,1)S(1)}, bf16[1,2,256,256]{3,2,1,0:T(8,128)(2,1)S(1)}, u32[]{:S(2)}, u32[]{:S(2)}) collective-permute-start(bf16[1,2,256,256]{3,2,1,0:T(8,128)(2,1)S(1)} %maximum_bitcast_fusion), channel_id=1, source_target_pairs={{0,8},{2,66},{4,12},{6,70},{8,0},{10,74},{12,4},{14,78},{16,24},{1... | collective-permute-start | bytes 786440 | tf_op jit(solution)/shard_map/ppermute | solution.py:31
  116.7 8.5 %collective-permute-start.1 = (bf16[5,256,128]{2,1,0:T(8,128)(2,1)S(1)}, bf16[5,256,128]{2,1,0:T(8,128)(2,1)S(1)}, u32[]{:S(2)}, u32[]{:S(2)}) collective-permute-start(bf16[5,256,128]{2,1,0:T(8,128)(2,1)S(1)} %get-tuple-element.59), channel_id=1, source_target_pairs={{0,2},{2,0},{4,6},{6,4},{8,10},{10,8},{12,14},{14,12},{16,18},{18,... | collective-permute-start | bytes 983048 | tf_op jit(solution)/shard_map/ppermute | solution.py:31
  123.6 3.7 %copy-start.1 = (bf16[4,2,256,256]{3,2,1,0:T(8,128)(2,1)}, bf16[4,2,256,256]{3,2,1,0:T(8,128)(2,1)S(1)}, u32[]{:S(2)}) copy-start(bf16[4,2,256,256]{3,2,1,0:T(8,128)(2,1)S(1)} %pad_maximum_fusion.refs_2_) | copy-start | bytes 3145732
  123.6 30.4 %collective-permute-start.6 = (bf16[4,2,256,256]{3,2,1,0:T(8,128)(2,1)S(1)}, bf16[4,2,256,256]{3,2,1,0:T(8,128)(2,1)S(1)}, u32[]{:S(2)}, u32[]{:S(2)}) collective-permute-start(bf16[4,2,256,256]{3,2,1,0:T(8,128)(2,1)S(1)} %pad_maximum_fusion.refs_2_), channel_id=1, source_target_pairs={{0,96},{2,14},{4,100},{6,2},{8,104},{10,6},{12,108},{14,10},{16,11... | collective-permute-start | bytes 3145736 | tf_op jit(solution)/shard_map/ppermute | solution.py:31
  123.7 30.3 %collective-permute-start.7 = (bf16[4,2,256,256]{3,2,1,0:T(8,128)(2,1)S(1)}, bf16[4,2,256,256]{3,2,1,0:T(8,128)(2,1)S(1)}, u32[]{:S(2)}, u32[]{:S(2)}) collective-permute-start(bf16[4,2,256,256]{3,2,1,0:T(8,128)(2,1)S(1)} %pad_maximum_fusion.refs_2_), channel_id=1, source_target_pairs={{0,32},{2,6},{4,36},{6,10},{8,40},{10,14},{12,44},{14,2},{16,48},{... | collective-permute-start | bytes 3145736 | tf_op jit(solution)/shard_map/ppermute | solution.py:31
  125.2 2.1 copy-start.3
  125.2 16.9 %collective-permute-start.9 = (bf16[2,5,256,128]{3,2,1,0:T(8,128)(2,1)S(1)}, bf16[2,5,256,128]{3,2,1,0:T(8,128)(2,1)S(1)}, u32[]{:S(2)}, u32[]{:S(2)}) collective-permute-start(bf16[2,5,256,128]{3,2,1,0:T(8,128)(2,1)S(1)} %pad_maximum_fusion.1.refs_1_), channel_id=1, source_target_pairs={{0,16},{2,18},{4,20},{6,22},{8,24},{10,26},{12,28},{14,30},{16,0},... | collective-permute-start | bytes 1966088 | tf_op jit(solution)/shard_map/ppermute | solution.py:31
  126.0 48.6 %collective-permute-start.8 = (bf16[4,2,256,256]{3,2,1,0:T(8,128)(2,1)S(1)}, bf16[4,2,256,256]{3,2,1,0:T(8,128)(2,1)S(1)}, u32[]{:S(2)}, u32[]{:S(2)}) collective-permute-start(bf16[4,2,256,256]{3,2,1,0:T(8,128)(2,1)S(1)} %pad_maximum_fusion.refs_2_), channel_id=1, source_target_pairs={{0,64},{2,10},{4,68},{6,14},{8,72},{10,2},{12,76},{14,6},{16,80},{... | collective-permute-start | bytes 3145736 | tf_op jit(solution)/shard_map/ppermute | solution.py:31
  127.3 0.5 copy-start.13
  142.1 0.9 copy-start.12
  154.0 1.0 copy-start.9
  154.1 1.4 copy-start.10
  174.6 1.1 copy-start.11
  187.4 29.1 %collective-permute-start.10 = (bf16[2,5,256,128]{3,2,1,0:T(8,128)(2,1)}, bf16[2,5,256,128]{3,2,1,0:T(8,128)(2,1)S(1)}, u32[]{:S(2)}, u32[]{:S(2)}) collective-permute-start(bf16[2,5,256,128]{3,2,1,0:T(8,128)(2,1)} %get-tuple-element.44), channel_id=1, source_target_pairs={{0,16},{2,18},{4,20},{6,22},{8,24},{10,26},{12,28},{14,30},{16,0},... | collective-permute-start | bytes 1966088 | tf_op jit(solution)/shard_map/ppermute | solution.py:31
  189.3 27.2 %collective-permute-start.11 = (f32[20,128]{1,0:T(8,128)}, f32[20,128]{1,0:T(8,128)S(1)}, u32[]{:S(2)}, u32[]{:S(2)}) collective-permute-start(f32[20,128]{1,0:T(8,128)} %get-tuple-element.45), channel_id=1, source_target_pairs={{0,16},{2,18},{4,20},{6,22},{8,24},{10,26},{12,28},{14,30},{16,0},... | collective-permute-start | bytes 30728 | tf_op jit(solution)/shard_map/ppermute | solution.py:31
  216.5 0.6 copy-start.4
  216.5 0.8 copy-start.2
  222.6 4.1 %collective-permute-start.12 = (bf16[256,640]{1,0:T(8,128)(2,1)S(1)}, bf16[256,640]{1,0:T(8,128)(2,1)S(1)}, u32[]{:S(2)}, u32[]{:S(2)}) collective-permute-start(bf16[256,640]{1,0:T(8,128)(2,1)S(1)} %bitcast.22), channel_id=1, source_target_pairs={{0,2},{2,0},{4,6},{6,4},{8,10},{10,8},{12,14},{14,12},{16,18},{18,... | collective-permute-start | bytes 983048 | tf_op jit(solution)/shard_map/ppermute | solution.py:31

commit v2 on v1

v2 whole, which is shorter than its diff:
```python
import functools
import math

import jax
import jax.numpy as jnp
from jax import lax
from jax.experimental import pallas as pl
from jax.experimental.pallas import tpu as pltpu
from jax.sharding import PartitionSpec as P

HD = 128
ROPE_BASE = 500000.0
NORM_EPS = 1e-05
NEG_FILL = -1e30
NY, NZ, NX, NK = 4, 2, 4, 2
GROUP = 5
HALF = 128
def split_index(c):
    return c // (NZ * NX * NK), (c // (NX * NK)) % NZ, (c // NK) % NX, c % NK


def join_index(y, z, x, k):
    return (((y % NY) * NZ + z % NZ) * NX + x % NX) * NK + k % NK


def permute(value, move):
    pairs = [(c, join_index(*move(*split_index(c)))) for c in range(NY * NZ * NX * NK)]
    return lax.ppermute(value, "ctx", pairs)


def core_swap(value):
    return permute(value, lambda y, z, x, k: (y, z, x, 1 - k))


def z_swap(value):
    return permute(value, lambda y, z, x, k: (y, 1 - z, x, k))


def first_axis(value, step):
    return permute(
        value, lambda y, z, x, k: (y, z, x - step, k) if k == 0 else (y - step, z, x, k)
    )


def second_axis(value, step):
    return permute(
        value, lambda y, z, x, k: (y - step, z, x, k) if k == 0 else (y, z, x - step, k)
    )


def params(mib=24):
    return pltpu.CompilerParams(vmem_limit_bytes=mib * 1024 * 1024)


def vmem():
    return pl.BlockSpec(memory_space=pltpu.VMEM)


def smem():
    return pl.BlockSpec(memory_space=pltpu.SMEM)


def choose_kernel(ids_col, ids_row, hot):
    rows = ids_col.shape[0]
    same = ids_col[...] == ids_row[...]
    row = lax.broadcasted_iota(jnp.int32, (rows, rows), 0)
    col = lax.broadcasted_iota(jnp.int32, (rows, rows), 1)
    slot = jnp.sum(jnp.where(same & (col < row), 1.0, 0.0), axis=1, keepdims=True)
    place = ids_col[...] * 4 + slot.astype(jnp.int32)
    lanes = lax.broadcasted_iota(jnp.int32, hot.shape, 1)
    hot[...] = jnp.where(lanes == place, 1.0, 0.0).astype(jnp.bfloat16)


def choose(ids, slots):
    rows = ids.shape[0]
    return pl.pallas_call(
        choose_kernel,
        in_specs=[vmem()] * 2,
        out_specs=vmem(),
        out_shape=jax.ShapeDtypeStruct((rows, slots), jnp.bfloat16),
        compiler_params=params(),
        cost_estimate=pl.CostEstimate(flops=2_000_000, bytes_accessed=600_000, transcendentals=0),
        name="choose",
    )(ids, ids.reshape(1, rows))


def pick_kernel(hot, gate, returned, residual, shared, out):
    picked = jnp.dot(hot[...], returned[...], preferred_element_type=jnp.float32)
    total = residual[...].astype(jnp.float32) + shared[...].astype(jnp.float32)
    out[...] = (total + gate[...] * picked).astype(jnp.bfloat16)


def pick(hot, gate, returned, residual, shared):
    rows, width = residual.shape
    slots = returned.shape[0]
    block = 640
    wide = pl.BlockSpec((rows, block), lambda i: (0, i))
    return pl.pallas_call(
        pick_kernel,
        grid=(width // block,),
        in_specs=[
            pl.BlockSpec((rows, slots), lambda i: (0, 0)),
            pl.BlockSpec((rows, 1), lambda i: (0, 0)),
            pl.BlockSpec((slots, block), lambda i: (0, i)),
            wide,
            wide,
        ],
        out_specs=wide,
        out_shape=jax.ShapeDtypeStruct((rows, width), jnp.bfloat16),
        compiler_params=params(),
        name="pick",
    )(hot, gate, returned, residual, shared)


def turn(x, cos, sin):
    return x * cos + pltpu.roll(x, HD // 2, 1) * sin


def gained(h, gain):
    return (h.astype(jnp.float32) * gain[0].astype(jnp.float32)).astype(jnp.bfloat16)


def key_value_first_kernel(tp, h, gain, wk, wv, part, squares):
    wide = h[...].astype(jnp.float32)
    squares[...] = jnp.sum(wide * wide, axis=1, keepdims=True)
    x = gained(h[...], gain[...])
    part[:, : 2 * HD] = jnp.dot(x, wk[...], preferred_element_type=jnp.float32)
    part[:, 2 * HD :] = jnp.dot(x, wv[...], preferred_element_type=jnp.float32)


def half_specs(rows, half, other, blocks):
    def of(tp):
        return 1 - tp[0] if other else tp[0]

    return [
        pl.BlockSpec((rows, half), lambda i, tp: (0, 0)),
        pl.BlockSpec((1, 1, half), lambda i, tp: (of(tp), 0, 0)),
    ] + [pl.BlockSpec((half, cols), lambda i, tp: (of(tp), i)) for cols in blocks]


def whole(*shape):
    return pl.BlockSpec(shape, lambda i, tp: (0,) * len(shape))


def projection_cost(rows, half, cols):
    return pl.CostEstimate(
        flops=2 * rows * half * cols,
        bytes_accessed=2 * half * cols + 2 * rows * half + 4 * rows * cols,
        transcendentals=0,
    )


def key_value_first(tp, h, gain, wk, wv):
    rows, half = h.shape
    cols = wk.shape[1]
    return pl.pallas_call(
        key_value_first_kernel,
        grid_spec=pltpu.PrefetchScalarGridSpec(
            num_scalar_prefetch=1,
            grid=(1,),
            in_specs=half_specs(rows, half, False, (cols, cols)),
            out_specs=[whole(rows, 2 * cols), whole(rows, 1)],
        ),
        out_shape=[
            jax.ShapeDtypeStruct((rows, 2 * cols), jnp.float32),
            jax.ShapeDtypeStruct((rows, 1), jnp.float32),
        ],
        compiler_params=params(),
        cost_estimate=projection_cost(rows, half, 2 * cols),
        name="key_value_first",
    )(tp, h, gain, wk, wv)


def key_value_kernel(tp, h, gain, wk, wv, part, squares, cos, sin, kv, scale):
    half = h.shape[1]
    wide = h[...].astype(jnp.float32)
    total = squares[...] + jnp.sum(wide * wide, axis=1, keepdims=True)
    factor = lax.rsqrt(total / (2 * half) + NORM_EPS)
    scale[...] = factor
    x = gained(h[...], gain[...])
    keys = part[:, : 2 * HD] + jnp.dot(x, wk[...], preferred_element_type=jnp.float32)
    values = part[:, 2 * HD :] + jnp.dot(x, wv[...], preferred_element_type=jnp.float32)
    for head in range(2):
        cols = slice(head * HD, (head + 1) * HD)
        turned = turn(keys[:, cols] * factor, cos[...], sin[...]).astype(jnp.bfloat16)
        value = (values[:, cols] * factor).T.astype(jnp.bfloat16)
        for side in range(2):
            rows = slice(side * HALF, (side + 1) * HALF)
            kv[head, side, 0] = turned[rows]
            kv[head, side, 1] = value[:, rows]


def key_value(tp, h, gain, wk, wv, part, squares, cos, sin):
    rows, half = h.shape
    cols = wk.shape[1]
    return pl.pallas_call(
        key_value_kernel,
        grid_spec=pltpu.PrefetchScalarGridSpec(
            num_scalar_prefetch=1,
            grid=(1,),
            in_specs=half_specs(rows, half, True, (cols, cols))
            + [whole(rows, 2 * cols), whole(rows, 1), whole(rows, HD), whole(rows, HD)],
            out_specs=[whole(2, 2, 2, HALF, HD), whole(rows, 1)],
        ),
        out_shape=[
            jax.ShapeDtypeStruct((2, 2, 2, HALF, HD), jnp.bfloat16),
            jax.ShapeDtypeStruct((rows, 1), jnp.float32),
        ],
        compiler_params=params(),
        cost_estimate=projection_cost(rows, half, 2 * cols),
        name="key_value",
    )(tp, h, gain, wk, wv, part, squares, cos, sin)


def query_first_kernel(tp, h, gain, wq, part, x):
    @pl.when(pl.program_id(0) == 0)
    def _():
        x[...] = gained(h[...], gain[...])

    part[...] = jnp.dot(x[...], wq[...], preferred_element_type=jnp.float32)


def query_first(tp, h, gain, wq):
    rows, half = h.shape
    cols, block = wq.shape[1], 2 * HD
    return pl.pallas_call(
        query_first_kernel,
        grid_spec=pltpu.PrefetchScalarGridSpec(
            num_scalar_prefetch=1,
            grid=(cols // block,),
            in_specs=half_specs(rows, half, False, (block,)),
            out_specs=pl.BlockSpec((rows, block), lambda i, tp: (0, i)),
            scratch_shapes=[pltpu.VMEM((rows, half), jnp.bfloat16)],
        ),
        out_shape=jax.ShapeDtypeStruct((rows, cols), jnp.float32),
        compiler_params=params(),
        cost_estimate=projection_cost(rows, half, cols),
        name="query_first",
    )(tp, h, gain, wq)


def query_kernel(tp, h, gain, wq, part, scale, cos, sin, out, x):
    @pl.when(pl.program_id(0) == 0)
    def _():
        x[...] = gained(h[...], gain[...])

    prod = part[...] + jnp.dot(x[...], wq[...], preferred_element_type=jnp.float32)
    prod = prod * (scale[...] * (1.0 / HD**0.5 * math.log2(math.e)))
    for head in range(2):
        turned = turn(prod[:, head * HD : (head + 1) * HD], cos[...], sin[...]).T.astype(jnp.bfloat16)
        for side in range(2):
            out[head, side] = turned[:, side * HALF : (side + 1) * HALF]


def query(tp, h, gain, wq, part, scale, cos, sin):
    rows, half = h.shape
    cols, block = wq.shape[1], 2 * HD
    return pl.pallas_call(
        query_kernel,
        grid_spec=pltpu.PrefetchScalarGridSpec(
            num_scalar_prefetch=1,
            grid=(cols // block,),
            in_specs=half_specs(rows, half, True, (block,))
            + [
                pl.BlockSpec((rows, block), lambda i, tp: (0, i)),
                whole(rows, 1),
                whole(rows, HD),
                whole(rows, HD),
            ],
            out_specs=pl.BlockSpec((2, 2, HD, HALF), lambda i, tp: (i, 0, 0, 0)),
            scratch_shapes=[pltpu.VMEM((rows, half), jnp.bfloat16)],
        ),
        out_shape=jax.ShapeDtypeStruct((cols // HD, 2, HD, HALF), jnp.bfloat16),
        compiler_params=params(),
        cost_estimate=projection_cost(rows, half, cols),
        name="query",
    )(tp, h, gain, wq, part, scale, cos, sin)


ONES = 16


def attend_kernel(counts, diag, resume, finish, *refs):
    flags, q, refs = refs[0], refs[1], refs[2:]
    kvs, refs = refs[: len(counts)], refs[len(counts) :]
    olds = refs[:3] if resume else ()
    refs = refs[len(olds) :]
    part = logs = None
    if finish:
        part, logs, refs = refs[0], refs[1], refs[2:]
    acc, den, top, klist, vlist = refs
    total = klist.shape[0]

    if resume:
        acc[...] = olds[0][...]
        den[...] = olds[1][...]
        top[...] = olds[2][...]
    else:
        acc[...] = jnp.zeros_like(acc)
        den[...] = jnp.zeros_like(den)
        top[...] = jnp.full_like(top, NEG_FILL)

    vlist[:, HD:, :] = jnp.ones((total, ONES, 2 * HALF), jnp.bfloat16)

    def put(place, kv, block, side):
        for core in range(2):
            span = slice(core * HALF, (core + 1) * HALF)
            klist[place, span, :] = kv[block, core, side, 0]
            vlist[place, :HD, span] = kv[block, core, side, 1]

    last = total - 2 if diag else total - 1
    front, back = jnp.int32(0), jnp.int32(last)
    start = 0
    for kv, count in zip(kvs, counts):
        for block in range(count):
            put(front, kv, block, 0)
            front = front + 1
            if diag and start + block == 0:
                continue
            early = flags[start + block]
            put(jnp.where(early == 1, back, front), kv, block, 1 - early)
            front = front + 1 - early
            back = back - early
        start += count
    n_late = front
    n_early = last - back

    def update(side, places, mask):
        keys = jnp.concatenate([klist[p] for p in places], axis=0)
        scores = []
        for head in range(GROUP):
            columns = jnp.concatenate([q[0, head, side], q[1, head, side]], axis=1)
            scores.append(jnp.dot(keys, columns, preferred_element_type=jnp.float32))
        values = jnp.concatenate([vlist[p] for p in places], axis=1)
        for head in range(GROUP):
            s = scores[head]
            if mask is not None:
                s = jnp.where(mask, s, NEG_FILL)
            old = top[side, head]
            new = jnp.maximum(old, jnp.max(s, axis=0, keepdims=True))
            weights = jnp.exp2(s - new[:1]).astype(jnp.bfloat16)
            prod = jnp.dot(values, weights, preferred_element_type=jnp.float32)
            keep = jnp.exp2(old - new)
            acc[side, head] = acc[side, head] * keep[:1] + prod[:HD]
            den[side, head] = den[side, head] * keep + prod[HD : HD + 8]
            top[side, head] = new

    if diag:
        core = flags[0]
        row = lax.broadcasted_iota(jnp.int32, (2 * HALF, 2 * HALF), 0)
        col = lax.broadcasted_iota(jnp.int32, (2 * HALF, 2 * HALF), 1)

        def own(side, carry):
            first = jnp.where(side == 0, core, 1 - core)
            key_pos = jnp.where(row < HALF, row + first * HALF, row - first * HALF)
            query_pos = jnp.where(col < HALF, col + first * HALF, col - first * HALF)
            put(total - 1, kvs[0], 0, side)
            update(side, (total - 1,), key_pos <= query_pos)
            return carry

        lax.fori_loop(0, 2, own, 0)

    pairs = n_late // 2
    early_pairs = n_early // 2
    def two(i, carry):
        late = i < pairs
        j = i - pairs
        one = jnp.where(late, 2 * i, last - 2 * j)
        other = jnp.where(late, 2 * i + 1, last - 2 * j - 1)
        update(jnp.where(late, 1, 0), (one, other), None)
        return carry

    lax.fori_loop(0, pairs + early_pairs, two, 0)
    odd_late = n_late - 2 * pairs
    odd_early = n_early - 2 * early_pairs

    def one(i, carry):
        late = i < odd_late
        update(jnp.where(late, 1, 0), (jnp.where(late, n_late - 1, last - n_early + 1),), None)
        return carry

    lax.fori_loop(0, odd_late + odd_early, one, 0)

    if finish:
        for side in range(2):
            for head in range(GROUP):
                denominator = den[side, head]
                some = denominator > 0.0
                safe = jnp.where(some, denominator, 1.0)
                inverse = jnp.where(some, 1.0 / safe, 0.0)
                part[side, head] = (acc[side, head] * inverse[:1]).astype(jnp.bfloat16)
                level = jnp.where(some, top[side, head] + jnp.log2(safe), NEG_FILL)
                place = side * GROUP + head
                logs[place : place + 1, :] = level[:1]


ACC = (2, GROUP, HD, 2 * HALF)
ROWS = (2, GROUP, 8, 2 * HALF)


def attend(flags, q, kvs, state, diag=False, finish=False):
    counts = tuple(kv.shape[0] for kv in kvs)
    n = sum(counts)
    total = 2 * n
    olds = [] if state is None else list(state)
    states = (ACC, ROWS, ROWS)
    scratch = [
        pltpu.VMEM((total, 2 * HALF, HD), jnp.bfloat16),
        pltpu.VMEM((total, HD + ONES, 2 * HALF), jnp.bfloat16),
    ]
    if finish:
        shapes = [
            jax.ShapeDtypeStruct(ACC, jnp.bfloat16),
            jax.ShapeDtypeStruct((2 * GROUP, 2 * HALF), jnp.float32),
        ]
        scratch = [pltpu.VMEM(shape, jnp.float32) for shape in states] + scratch
    else:
        shapes = [jax.ShapeDtypeStruct(shape, jnp.float32) for shape in states]
    return pl.pallas_call(
        functools.partial(attend_kernel, counts, diag, state is not None, finish),
        in_specs=[smem()] + [vmem()] * (1 + len(kvs) + len(olds)),
        out_specs=[vmem()] * len(shapes),
        out_shape=shapes,
        scratch_shapes=scratch,
        compiler_params=params(),
        cost_estimate=pl.CostEstimate(
            flops=n * 2 * 1280 * 256 * 128 * 8,
            bytes_accessed=n * 262144 + 4_000_000,
            transcendentals=n * 2 * 1280 * 256,
        ),
        name="attend",
    )(flags, q, *kvs, *olds)


def merge_kernel(acc, den, top, part, logs, out):
    for side in range(2):
        for head in range(GROUP):
            place = side * GROUP + head
            total = den[side, head][:1]
            other = logs[place : place + 1, :]
            mine = top[side, head][:1] + jnp.log2(total)
            high = jnp.maximum(mine, other)
            first = jnp.exp2(mine - high)
            second = jnp.exp2(other - high)
            weight = 1.0 / (first + second)
            value = acc[side, head] * (first * weight / total)
            value = value + part[side, head].astype(jnp.float32) * (second * weight)
            rows = value.T.astype(jnp.bfloat16)
            for core in range(2):
                out[core, side, :, head * HD : (head + 1) * HD] = rows[core * HALF : (core + 1) * HALF]


def merge(state, part, logs):
    return pl.pallas_call(
        merge_kernel,
        in_specs=[vmem()] * 5,
        out_specs=vmem(),
        out_shape=jax.ShapeDtypeStruct((2, 2, HALF, GROUP * HD), jnp.bfloat16),
        compiler_params=params(),
        name="merge",
    )(*state, part, logs)


def rotations(ctx_index, rows):
    row = jnp.arange(rows, dtype=jnp.int32)
    half = rows // 2
    count = NY * NZ * NX * NK
    pos = jnp.where(row < half, ctx_index * half + row, (2 * count - 1 - ctx_index) * half + row - half)
    frequency = ROPE_BASE ** (-(jnp.arange(HD // 2, dtype=jnp.float32) * 2.0 / HD))
    angles = pos.astype(jnp.float32)[:, None] * frequency[None, :]
    cos, sin = jnp.cos(angles), jnp.sin(angles)
    return jnp.concatenate([cos, cos], axis=1), jnp.concatenate([-sin, sin], axis=1)


def chip_order(y, z, x):
    return (y * NZ + z) * NX + x


def shards(residual, shared_out, expert_out, routing, gate_score, norm_gain, w_query, w_key, w_value):
    rows, half_width = residual.shape
    ctx_index = lax.axis_index("ctx")
    tp_index = lax.axis_index("tp")
    y, z, x, k = split_index(ctx_index)
    cos, sin = rotations(ctx_index, rows)

    own_experts, sources, slots, _ = expert_out.shape
    outgoing = jnp.transpose(expert_out, (1, 0, 2, 3)).reshape(sources, own_experts * slots, half_width)
    returned = lax.all_to_all(outgoing, "ctx", split_axis=0, concat_axis=0, tiled=True)
    returned = returned.reshape(sources * own_experts * slots, half_width)
    hidden = pick(choose(routing, returned.shape[0]), gate_score, returned, residual, shared_out)

    other = lax.ppermute(hidden, "tp", [(0, 1), (1, 0)])
    tp = tp_index.reshape(1)
    gain = norm_gain.reshape(2, 1, half_width)
    kv_part, squares = key_value_first(tp, hidden, gain, w_key, w_value)
    query_part = query_first(tp, hidden, gain, w_query)
    kv, scale = key_value(tp, other, gain, w_key, w_value, kv_part, squares, cos, sin)
    kv_mine = lax.dynamic_index_in_dim(kv, k, 0, keepdims=False)
    kv_other = lax.dynamic_index_in_dim(kv, 1 - k, 0, keepdims=False)
    block = jnp.stack([kv_mine, core_swap(kv_other)])[None]

    near = [first_axis(block, step) for step in (1, -1, 2)]

    queries = query(tp, other, gain, w_query, query_part, scale, cos, sin)
    queries = queries.reshape(2, GROUP, 2, HD, HALF)
    q_mine = lax.dynamic_index_in_dim(queries, k, 0, keepdims=False)
    q_other = lax.dynamic_index_in_dim(queries, 1 - k, 0, keepdims=False)
    q_own = jnp.stack([q_mine, core_swap(q_other)])
    q_pair = z_swap(q_own)

    line = jnp.concatenate([block] + near)
    far = [second_axis(line, step) for step in (1, -1, 2)]

    steps = jnp.array([0, 1, -1, 2], jnp.int32)

    def before(first, second, chip):
        by = jnp.where(k == 0, second, first)
        bx = jnp.where(k == 0, first, second)
        return (chip_order((y + by) % NY, z, (x + bx) % NX) < chip).astype(jnp.int32)

    own_chip = chip_order(y, z, x)
    pair_chip = chip_order(y, 1 - z, x)
    zero = jnp.zeros((4,), jnp.int32)
    own_near = before(steps, zero, own_chip).at[0].set(k)
    pair_near = before(steps, zero, pair_chip)
    own_far = jnp.concatenate([before(steps, zero + s, own_chip) for s in (1, -1, 2)])
    pair_far = jnp.concatenate([before(steps, zero + s, pair_chip) for s in (1, -1, 2)])

    own_state = attend(own_near, q_own, [line], None, diag=True)
    pair_state = attend(pair_near, q_pair, [line], None)
    pair_state = attend(pair_far[:8], q_pair, far[:2], pair_state)
    part, logs = attend(pair_far[8:], q_pair, far[2:], pair_state, finish=True)
    part = z_swap(part)
    logs = z_swap(logs)
    own_state = attend(own_far, q_own, far, own_state)
    out = merge(own_state, part, logs)
    keep = lax.dynamic_index_in_dim(out, 0, 0, keepdims=False).reshape(rows, GROUP * HD)
    sent = core_swap(out[1].reshape(rows, GROUP * HD))
    attended = jnp.where(
        k == 0,
        jnp.concatenate([keep, sent], axis=1),
        jnp.concatenate([sent, keep], axis=1),
    )
    return hidden, attended


def solution(mesh):
    return jax.shard_map(
        shards,
        mesh=mesh,
        in_specs=(
            P("ctx", "tp"),
            P("ctx", "tp"),
            P("ctx", None, None, "tp"),
            P("ctx", None),
            P("ctx", None),
            P(),
            P(None, "tp"),
            P(None, "tp"),
            P(None, "tp"),
        ),
        out_specs=(P("ctx", "tp"), P("ctx", "tp")),
        check_vma=False,
    )
```

time: 228 us -> 177 us (0.78)
  Pallas kernels: 108 us -> 53.1 us
  other arithmetic: 7.48 us -> 2.1 us
  waiting for transfers between devices: 70.7 us -> 75.7 us
  local copies, waits for them, and re-layouts: 16.7 us -> 19.5 us
    pallas_call x5, Pallas kernels: 81.9 us -> 36.5 us  [attend(): pl.pallas_call(functools.partial(attend_kernel, counts, diag, state is no...]
    ppermute x12, waiting for transfers between devices: 8.4 us -> 23 us  [permute(): return lax.ppermute(value, 'ctx', pairs)]
    ppermute x1, waiting for transfers between devices: 27.4 us -> 16.7 us  [shards(): other = lax.ppermute(hidden, 'tp', [(0, 1), (1, 0)])]
    unnamed x31 -> x39, local copies, waits for them, and re-layouts: 9.91 us -> 16.4 us
    pallas_call x1, Pallas kernels: 4.09 us -> 0.42 us  [merge(): pl.pallas_call(merge_kernel, in_specs=[vmem()] * 5, out_specs=vmem(), out...]
    pallas_call x2 -> x5, Pallas kernels: 16.3 us -> 13.2 us  [the longest x1 6 us: query(): pl.pallas_call(query_kernel, grid_spec=pltpu.PrefetchScalarGridSpec(num_s...]
    select_n x1 -> x0, other arithmetic: 3.01 us -> none  [shards(): h1 = jnp.where(tp_index == 0, other, hidden)]
    pallas_call x1, Pallas kernels: 5.33 us -> 3 us  [pick(): pl.pallas_call(pick_kernel, grid=(width // block,), in_specs=[pl.BlockSpe...]
  transfers between devices with their start and end apart: 14 -> 14, of which waited for: 6 -> 8; matrix products, arithmetic and copies ran while one was open for 3% -> 1% of each run, Pallas kernels for 35% -> 24%
where the time goes in v2:
time: 177 us; the launch traced here: 176 us
  waiting for transfers between devices  75.7 us (43%)
  Pallas kernels  53.1 us (30%)
  starting transfers between devices  24.8 us (14%)
  local copies, waits for them, and re-layouts  19.5 us (11%)
  other arithmetic  2.1 us (1%)
    pallas_call x5, Pallas kernels, attend(): pl.pallas_call(functools.partial(attend_kernel, counts, diag, state is no...  36.5 us
    all_to_all x1, waiting for transfers between devices, shards(): lax.all_to_all(outgoing, 'ctx', split_axis=0, concat_axis=0, tiled=True)  35.9 us
    ppermute x12, waiting for transfers between devices, permute(): return lax.ppermute(value, 'ctx', pairs)  23 us
    ppermute x1, waiting for transfers between devices, shards(): other = lax.ppermute(hidden, 'tp', [(0, 1), (1, 0)])  16.7 us
    unnamed x39, local copies, waits for them, and re-layouts  16.4 us
    all_to_all x1, starting transfers between devices, shards(): lax.all_to_all(outgoing, 'ctx', split_axis=0, concat_axis=0, tiled=True)  12.4 us
    ppermute x12, starting transfers between devices, permute(): return lax.ppermute(value, 'ctx', pairs)  11.6 us
    pallas_call x1, Pallas kernels, query(): pl.pallas_call(query_kernel, grid_spec=pltpu.PrefetchScalarGridSpec(num_s...  6 us
  transfers between devices with their start and end apart: 14, of which 8 were waited for; matrix products, arithmetic and copies ran while one was open for 1% of the time, Pallas kernels for 24%

profile of v2, /device:TPU:1, one launch (start us, length us, event | category | flops | bytes accessed | tf_op | source)
XLA Modules:
  0.0 176.2 jit_solution(844569192997701419)
XLA Ops:
  0.6 2.2 %copy.23 = bf16[2,64,4,2560]{3,1,2,0:T(8,128)(2,1)S(1)} copy(bf16[2,64,4,2560]{3,2,1,0:T(4,128)(2,1)} %param.14) | data formatting | bytes 5242880 | tf_op args[2]
  2.8 2.9 %copy.24 = bf16[64,8,2560]{2,1,0:T(8,128)(2,1)} copy(bf16[64,8,2560]{2,0,1:T(8,128)(2,1)S(1)} %bitcast.23) | data formatting | bytes 5242880 | tf_op jit(solution)/shard_map/reshape | solution.py:487
  5.8 12.4 %all-to-all-start = ((bf16[64,8,2560]{2,1,0:T(8,128)(2,1)}), bf16[64,8,2560]{2,1,0:T(8,128)(2,1)S(1)}, u32[]{:S(2)}, u32[]{:S(2)}) async-start(bf16[64,8,2560]{2,1,0:T(8,128)(2,1)} %copy.24), calls=%async_computation | async-start | bytes 5242880 | tf_op jit(solution)/shard_map/all_to_all | solution.py:488
  18.2 0.1 copy.22.ids_col
  18.4 0.1 copy.25.gate
  18.5 0.3 choose.1.hot
  18.8 35.9 %all-to-all-done = bf16[64,8,2560]{2,1,0:T(8,128)(2,1)S(1)} async-done(((bf16[64,8,2560]{2,1,0:T(8,128)(2,1)}), bf16[64,8,2560]{2,1,0:T(8,128)(2,1)S(1)}, u32[]{:S(2)}, u32[]{:S(2)}) %all-to-all-start) | async-done | bytes 2621472 | tf_op jit(solution)/shard_map/all_to_all | solution.py:488
  54.7 1.5 copy-done.6
  56.2 1.7 copy-done.7
  57.9 1.3 copy-done.8
  59.2 1.3 copy-done.9
  60.6 3.0 %pick.1.h = bf16[256,2560]{1,0:T(8,128)(2,1)} custom-call(bf16[256,512]{1,0:T(8,128)(2,1)S(1)} %choose.1.hot, f32[256,1]{1,0:T(8,128)S(1)} %copy.25.gate, bf16[512,2560]{1,0:T(8,128)(2,1)S(1)} %bitcast.20, bf16[256,2560]{1,0:T(8,128)(2,1)S(1)} %copy-done.8, bf16[256,2560]{1,0:T(8,128)(2,1)S(1)} %copy-done.9), custom_call_target="tpu_custom_call" | custom-call | tf_op jit(solution)/shard_map/pick/pallas_call | solution.py:98
  63.6 0.7 collective-permute-start
  64.4 0.5 fusion
  64.9 0.1 pad_maximum_fusion.2
  65.2 1.3 copy-done.1
  66.5 1.7 copy-done.4
  68.2 1.0 key_value_first.1
  69.2 0.3 copy-done.2
  69.5 4.7 %copy-done = bf16[5120,1280]{1,0:T(8,128)(2,1)S(1)} copy-done((bf16[5120,1280]{1,0:T(8,128)(2,1)S(1)}, bf16[5120,1280]{1,0:T(8,128)(2,1)}, u32[]{:S(2)}) %copy-start) | copy-done | bytes 13107224
  74.3 3.3 %query_first.1.part = f32[256,1280]{1,0:T(8,128)S(1)} custom-call(s32[1]{0:T(128)} %bitcast.4.tp, bf16[256,2560]{1,0:T(8,128)(2,1)S(1)} %copy-done.2, bf16[2,1,2560]{2,1,0:T(2,128)(2,1)S(1)} %reshape.76.gain, bf16[5120,1280]{1,0:T(8,128)(2,1)S(1)} %copy-done), custom_call_target="tpu_custom_call" | custom-call | flops 1677721600 | bytes 9175040 | tf_op jit(solution)/shard_map/query_first/pallas_call | solution.py:226
  77.6 16.7 %collective-permute-done.h = bf16[256,2560]{1,0:T(8,128)(2,1)} collective-permute-done((bf16[256,2560]{1,0:T(8,128)(2,1)}, bf16[256,2560]{1,0:T(8,128)(2,1)}, u32[]{:S(2)}, u32[]{:S(2)}) %collective-permute-start) | collective-permute-done | bytes 1310752 | tf_op jit(solution)/shard_map/ppermute | solution.py:492
  94.4 2.6 %key_value.1 = (bf16[2,2,2,128,128]{4,3,2,1,0:T(8,128)(2,1)S(1)}, f32[256,1]{1,0:T(8,128)S(1)}) custom-call(s32[1]{0:T(128)} %bitcast.4.tp, bf16[256,2560]{1,0:T(8,128)(2,1)} %collective-permute-done.h, bf16[2,1,2560]{2,1,0:T(2,128)(2,1)S(1)} %reshape.76.gain, bf16[5120,256]{1,0:T(8,128)(2,1)S(1)} %copy-done.3, bf16[5120,256]{1,0:T(8,128)(2,1)S(1)} %copy-done.5, ...), custom_call_target="tpu_custom_call" | custom-call | flops 671088640 | bytes 4456448 | tf_op jit(solution)/shard_map/key_value/pallas_call | solution.py:196
  97.0 0.8 collective-permute-start.2
  97.8 6.0 %query.1 = bf16[10,2,128,128]{3,2,1,0:T(8,128)(2,1)S(1)} custom-call(s32[1]{0:T(128)} %bitcast.4.tp, bf16[256,2560]{1,0:T(8,128)(2,1)} %collective-permute-done.h, bf16[2,1,2560]{2,1,0:T(2,128)(2,1)S(1)} %reshape.76.gain, bf16[5120,1280]{1,0:T(8,128)(2,1)S(1)} %bitcast.19, f32[256,1280]{1,0:T(8,128)S(1)} %query_first.1.part, ...), custom_call_target="tpu_custom_call" | custom-call | flops 1677721600 | bytes 9175040 | tf_op jit(solution)/shard_map/query/pallas_call | solution.py:258
  103.8 0.9 collective-permute-start.3
  104.7 0.7 collective-permute-start.4
  105.4 0.7 collective-permute-start.5
  106.3 3.2 %collective-permute-done.3 = bf16[1,2,2,2,128,128]{5,4,3,2,1,0:T(8,128)(2,1)S(1)} collective-permute-done((bf16[1,2,2,2,128,128]{5,4,3,2,1,0:T(8,128)(2,1)S(1)}, bf16[1,2,2,2,128,128]{5,4,3,2,1,0:T(8,128)(2,1)S(1)}, u32[]{:S(2)}, u32[]{:S(2)}) %collective-permute-start.3) | collective-permute-done | bytes 262176 | tf_op jit(solution)/shard_map/ppermute | solution.py:28
  109.4 4.6 %collective-permute-done.4 = bf16[1,2,2,2,128,128]{5,4,3,2,1,0:T(8,128)(2,1)S(1)} collective-permute-done((bf16[1,2,2,2,128,128]{5,4,3,2,1,0:T(8,128)(2,1)S(1)}, bf16[1,2,2,2,128,128]{5,4,3,2,1,0:T(8,128)(2,1)S(1)}, u32[]{:S(2)}, u32[]{:S(2)}) %collective-permute-start.4) | collective-permute-done | bytes 262176 | tf_op jit(solution)/shard_map/ppermute | solution.py:28
  114.0 0.1 pad_maximum_fusion.refs_2_
  114.2 1.5 collective-permute-start.7
  115.8 0.1 collective-permute-start.9
  115.9 0.9 collective-permute-start.8
  116.9 5.6 %attend.5 = (f32[2,5,128,256]{3,2,1,0:T(8,128)S(1)}, f32[2,5,8,256]{3,2,1,0:T(8,128)S(1)}, f32[2,5,8,256]{3,2,1,0:T(8,128)S(1)}) custom-call(s32[4]{0:T(128)S(1)} %constant_dynamic-update-slice_fusion.refs_0_, bf16[2,5,2,128,128]{4,3,2,1,0:T(8,128)(2,1)S(1)} %pad_maximum_fusion.1.refs_1_, bf16[4,2,2,2,128,128]{5,4,3,2,1,0:T(8,128)(2,1)S(1)} %pad_maximum_fusion.refs_2_), custom_call_target="tpu_custom_call" | custom-call | flops 2684354560 | bytes 5048576 | tf_op jit(solution)/shard_map/attend/pallas_call | solution.py:419
  122.5 10.1 %collective-permute-done.9.refs_1_ = bf16[2,5,2,128,128]{4,3,2,1,0:T(8,128)(2,1)S(1)} collective-permute-done((bf16[2,5,2,128,128]{4,3,2,1,0:T(8,128)(2,1)S(1)}, bf16[2,5,2,128,128]{4,3,2,1,0:T(8,128)(2,1)S(1)}, u32[]{:S(2)}, u32[]{:S(2)}) %collective-permute-start.9) | collective-permute-done | bytes 655392 | tf_op jit(solution)/shard_map/ppermute | solution.py:28
  132.6 4.9 %attend.7 = (f32[2,5,128,256]{3,2,1,0:T(8,128)S(1)}, f32[2,5,8,256]{3,2,1,0:T(8,128)S(1)}, f32[2,5,8,256]{3,2,1,0:T(8,128)S(1)}) custom-call(s32[4]{0:T(128)S(1)} %get-tuple-element.50.refs_0_, bf16[2,5,2,128,128]{4,3,2,1,0:T(8,128)(2,1)S(1)} %collective-permute-done.9.refs_1_, bf16[4,2,2,2,128,128]{5,4,3,2,1,0:T(8,128)(2,1)S(1)} %pad_maximum_fusion.refs_2_), custom_call_target="tpu_custom_call" | custom-call | flops 2684354560 | bytes 5048576 | tf_op jit(solution)/shard_map/attend/pallas_call | solution.py:419
  137.5 3.2 %collective-permute-done.7.refs_3_ = bf16[4,2,2,2,128,128]{5,4,3,2,1,0:T(8,128)(2,1)S(1)} collective-permute-done((bf16[4,2,2,2,128,128]{5,4,3,2,1,0:T(8,128)(2,1)S(1)}, bf16[4,2,2,2,128,128]{5,4,3,2,1,0:T(8,128)(2,1)S(1)}, u32[]{:S(2)}, u32[]{:S(2)}) %collective-permute-start.7) | collective-permute-done | bytes 1048608 | tf_op jit(solution)/shard_map/ppermute | solution.py:28
  140.7 8.6 %attend.8 = (f32[2,5,128,256]{3,2,1,0:T(8,128)S(1)}, f32[2,5,8,256]{3,2,1,0:T(8,128)S(1)}, f32[2,5,8,256]{3,2,1,0:T(8,128)S(1)}) custom-call(s32[8]{0:T(128)S(1)} %add_convert_fusion.1.refs_0_, bf16[2,5,2,128,128]{4,3,2,1,0:T(8,128)(2,1)S(1)} %collective-permute-done.9.refs_1_, bf16[4,2,2,2,128,128]{5,4,3,2,1,0:T(8,128)(2,1)S(1)} %collective-permute-done.6.refs_2_, ...), custom_call_target="tpu_custom_call" | custom-call | flops 5368709120 | bytes 6097152 | tf_op jit(solution)/shard_map/attend/pallas_call | solution.py:419
  149.4 5.0 %attend.9 = (bf16[2,5,128,256]{3,2,1,0:T(8,128)(2,1)S(1)}, f32[10,256]{1,0:T(8,128)S(1)}) custom-call(s32[4]{0:T(128)S(1)} %get-tuple-element.71.refs_0_, bf16[2,5,2,128,128]{4,3,2,1,0:T(8,128)(2,1)S(1)} %collective-permute-done.9.refs_1_, bf16[4,2,2,2,128,128]{5,4,3,2,1,0:T(8,128)(2,1)S(1)} %collective-permute-done.8.refs_4_.refs_2_, ...), custom_call_target="tpu_custom_call" | custom-call | flops 2684354560 | bytes 5048576 | tf_op jit(solution)/shard_map/attend/pallas_call | solution.py:419
  154.3 0.6 collective-permute-start.10
  154.9 2.5 %collective-permute-start.11 = (f32[10,256]{1,0:T(8,128)S(1)}, f32[10,256]{1,0:T(8,128)S(1)}, u32[]{:S(2)}, u32[]{:S(2)}) collective-permute-start(f32[10,256]{1,0:T(8,128)S(1)} %get-tuple-element.49), channel_id=1, source_target_pairs={{0,16},{2,18},{4,20},{6,22},{8,24},{10,26},{12,28},{14,30},{16,0},... | collective-permute-start | bytes 30728 | tf_op jit(solution)/shard_map/ppermute | solution.py:28
  157.4 12.5 %attend.6 = (f32[2,5,128,256]{3,2,1,0:T(8,128)S(1)}, f32[2,5,8,256]{3,2,1,0:T(8,128)S(1)}, f32[2,5,8,256]{3,2,1,0:T(8,128)S(1)}) custom-call(s32[12]{0:T(128)S(1)} %add_convert_fusion.refs_0_, bf16[2,5,2,128,128]{4,3,2,1,0:T(8,128)(2,1)S(1)} %pad_maximum_fusion.1.refs_1_, bf16[4,2,2,2,128,128]{5,4,3,2,1,0:T(8,128)(2,1)S(1)} %collective-permute-done.6.refs_2_, ...), custom_call_target="tpu_custom_call" | custom-call | flops 8053063680 | bytes 7145728 | tf_op jit(solution)/shard_map/attend/pallas_call | solution.py:419
  169.8 0.7 collective-permute-done.11.logs
  170.5 0.4 merge.1
  171.0 3.0 %collective-permute-start.12 = (bf16[256,640]{1,0:T(8,128)(2,1)S(1)}, bf16[256,640]{1,0:T(8,128)(2,1)S(1)}, u32[]{:S(2)}, u32[]{:S(2)}) collective-permute-start(bf16[256,640]{1,0:T(8,128)(2,1)S(1)} %bitcast.26), channel_id=1, source_target_pairs={{0,2},{2,0},{4,6},{6,4},{8,10},{10,8},{12,14},{14,12},{16,18},{18,... | collective-permute-start | bytes 983048 | tf_op jit(solution)/shard_map/ppermute | solution.py:28
  174.0 1.3 collective-permute-done.12
  175.2 1.0 maximum_select_fusion
  (52 shorter events, 0.7 us)
Async XLA Ops:
  5.8 12.4 %copy-start.10 = (s32[256,1]{0,1:T(1,128)S(1)}, s32[256,1]{0,1:T(1,128)}, u32[]{:S(2)}) copy-start(s32[256,1]{0,1:T(1,128)} %param.15) | copy-start | bytes 3076
  5.8 12.6 %copy-start.12 = (f32[256,1]{0,1:T(1,128)S(1)}, f32[256,1]{0,1:T(1,128)}, u32[]{:S(2)}) copy-start(f32[256,1]{0,1:T(1,128)} %param.16) | copy-start | bytes 3076
  5.8 48.9 %all-to-all-start = ((bf16[64,8,2560]{2,1,0:T(8,128)(2,1)}), bf16[64,8,2560]{2,1,0:T(8,128)(2,1)S(1)}, u32[]{:S(2)}, u32[]{:S(2)}) async-start(bf16[64,8,2560]{2,1,0:T(8,128)(2,1)} %copy.24), calls=%async_computation | async-start | bytes 5242880 | tf_op jit(solution)/shard_map/all_to_all | solution.py:488
  54.7 1.5 copy-start.6
  56.2 1.7 copy-start.7
  57.9 1.3 copy-start.8
  59.2 1.3 copy-start.9
  60.5 3.8 %copy-start.11 = (bf16[5120]{0:T(1024)(128)(2,1)S(1)}, bf16[5120]{0:T(1024)(128)(2,1)}, u32[]{:S(2)}) copy-start(bf16[5120]{0:T(1024)(128)(2,1)} %param.17) | copy-start | bytes 30724
  60.5 4.5 %copy-start.13 = (s32[4]{0:T(128)S(1)}, s32[4]{0:T(128)}, u32[]{:S(2)}) copy-start(s32[4]{0:T(128)} %constant.196.clone) | copy-start | bytes 52
  60.5 4.6 %copy-start.3 = (bf16[5120,256]{1,0:T(8,128)(2,1)S(1)}, bf16[5120,256]{1,0:T(8,128)(2,1)}, u32[]{:S(2)}) copy-start(bf16[5120,256]{1,0:T(8,128)(2,1)} %wk.3) | copy-start | bytes 7864324
  63.6 30.8 %collective-permute-start = (bf16[256,2560]{1,0:T(8,128)(2,1)}, bf16[256,2560]{1,0:T(8,128)(2,1)}, u32[]{:S(2)}, u32[]{:S(2)}) collective-permute-start(bf16[256,2560]{1,0:T(8,128)(2,1)} %pick.1.h), channel_id=1, source_target_pairs={{0,1},{1,0},{2,3},{3,2},{4,5},{5,4},{6,7},{7,6},{8,9},{9,8},{10,11... | collective-permute-start | bytes 3932168 | tf_op jit(solution)/shard_map/ppermute | solution.py:492
  65.1 1.3 copy-start.1
  66.5 1.7 copy-start.4
  68.2 1.3 copy-start.2
  69.5 4.7 %copy-start = (bf16[5120,1280]{1,0:T(8,128)(2,1)S(1)}, bf16[5120,1280]{1,0:T(8,128)(2,1)}, u32[]{:S(2)}) copy-start(bf16[5120,1280]{1,0:T(8,128)(2,1)} %wq.3) | copy-start | bytes 39321604
  74.2 20.1 %copy-start.5 = (bf16[5120,256]{1,0:T(8,128)(2,1)S(1)}, bf16[5120,256]{1,0:T(8,128)(2,1)}, u32[]{:S(2)}) copy-start(bf16[5120,256]{1,0:T(8,128)(2,1)} %wv.3) | copy-start | bytes 7864324
  74.2 23.5 %slice-start = ((s8[13107200]{0:T(1024)(128)(4,1)}), s8[4194304]{0:T(1024)(128)(4,1)S(1)}, s32[]{:S(2)}) async-start(s8[13107200]{0:T(1024)(128)(4,1)} %bitcast.18), calls=%async_computation.1 | async-start | bytes 8388608
  74.2 23.5 %slice-start.1 = ((s8[13107200]{0:T(1024)(128)(4,1)}), s8[4194304]{0:T(1024)(128)(4,1)S(1)}, s32[]{:S(2)}) async-start(s8[13107200]{0:T(1024)(128)(4,1)} %bitcast.18), calls=%async_computation.2 | async-start | bytes 8388608
  74.3 23.5 %slice-start.2 = ((s8[13107200]{0:T(1024)(128)(4,1)}), s8[4194304]{0:T(1024)(128)(4,1)S(1)}, s32[]{:S(2)}) async-start(s8[13107200]{0:T(1024)(128)(4,1)} %bitcast.18), calls=%async_computation.3 | async-start | bytes 8388608
  94.4 3.4 %slice-start.3 = ((s8[13107200]{0:T(1024)(128)(4,1)}), s8[524288]{0:T(1024)(128)(4,1)S(1)}, s32[]{:S(2)}) async-start(s8[13107200]{0:T(1024)(128)(4,1)} %bitcast.18), calls=%async_computation.4 | async-start | bytes 1048576
  97.0 6.8 %collective-permute-start.2 = (bf16[2,2,128,128]{3,2,1,0:T(8,128)(2,1)S(1)}, bf16[2,2,128,128]{3,2,1,0:T(8,128)(2,1)S(1)}, u32[]{:S(2)}, u32[]{:S(2)}) collective-permute-start(bf16[2,2,128,128]{3,2,1,0:T(8,128)(2,1)S(1)} %get-tuple-element.63), channel_id=1, source_target_pairs={{0,2},{2,0},{4,6},{6,4},{8,10},{10,8},{12,14},{14,12},{16,18},{18,... | collective-permute-start | bytes 393224 | tf_op jit(solution)/shard_map/ppermute | solution.py:28
  103.8 5.6 %collective-permute-start.3 = (bf16[1,2,2,2,128,128]{5,4,3,2,1,0:T(8,128)(2,1)S(1)}, bf16[1,2,2,2,128,128]{5,4,3,2,1,0:T(8,128)(2,1)S(1)}, u32[]{:S(2)}, u32[]{:S(2)}) collective-permute-start(bf16[1,2,2,2,128,128]{5,4,3,2,1,0:T(8,128)(2,1)S(1)} %maximum_bitcast_fusion), channel_id=1, source_target_pairs={{0,12},{2,98},{4,0},{6,102},{8,4},{10,106},{12,8},{14,110},{16,28}... | collective-permute-start | bytes 786440 | tf_op jit(solution)/shard_map/ppermute | solution.py:28
  104.7 9.3 %collective-permute-start.4 = (bf16[1,2,2,2,128,128]{5,4,3,2,1,0:T(8,128)(2,1)S(1)}, bf16[1,2,2,2,128,128]{5,4,3,2,1,0:T(8,128)(2,1)S(1)}, u32[]{:S(2)}, u32[]{:S(2)}) collective-permute-start(bf16[1,2,2,2,128,128]{5,4,3,2,1,0:T(8,128)(2,1)S(1)} %maximum_bitcast_fusion), channel_id=1, source_target_pairs={{0,4},{2,34},{4,8},{6,38},{8,12},{10,42},{12,0},{14,46},{16,20},{1... | collective-permute-start | bytes 786440 | tf_op jit(solution)/shard_map/ppermute | solution.py:28
  105.4 8.7 %collective-permute-start.5 = (bf16[1,2,2,2,128,128]{5,4,3,2,1,0:T(8,128)(2,1)S(1)}, bf16[1,2,2,2,128,128]{5,4,3,2,1,0:T(8,128)(2,1)S(1)}, u32[]{:S(2)}, u32[]{:S(2)}) collective-permute-start(bf16[1,2,2,2,128,128]{5,4,3,2,1,0:T(8,128)(2,1)S(1)} %maximum_bitcast_fusion), channel_id=1, source_target_pairs={{0,8},{2,66},{4,12},{6,70},{8,0},{10,74},{12,4},{14,78},{16,24},{1... | collective-permute-start | bytes 786440 | tf_op jit(solution)/shard_map/ppermute | solution.py:28
  106.2 9.5 %collective-permute-start.1 = (bf16[5,2,128,128]{3,2,1,0:T(8,128)(2,1)S(1)}, bf16[5,2,128,128]{3,2,1,0:T(8,128)(2,1)S(1)}, u32[]{:S(2)}, u32[]{:S(2)}) collective-permute-start(bf16[5,2,128,128]{3,2,1,0:T(8,128)(2,1)S(1)} %get-tuple-element.61), channel_id=1, source_target_pairs={{0,2},{2,0},{4,6},{6,4},{8,10},{10,8},{12,14},{14,12},{16,18},{18,... | collective-permute-start | bytes 983048 | tf_op jit(solution)/shard_map/ppermute | solution.py:28
  114.2 23.4 %collective-permute-start.6 = (bf16[4,2,2,2,128,128]{5,4,3,2,1,0:T(8,128)(2,1)S(1)}, bf16[4,2,2,2,128,128]{5,4,3,2,1,0:T(8,128)(2,1)S(1)}, u32[]{:S(2)}, u32[]{:S(2)}) collective-permute-start(bf16[4,2,2,2,128,128]{5,4,3,2,1,0:T(8,128)(2,1)S(1)} %pad_maximum_fusion.refs_2_), channel_id=1, source_target_pairs={{0,96},{2,14},{4,100},{6,2},{8,104},{10,6},{12,108},{14,10},{16,11... | collective-permute-start | bytes 3145736 | tf_op jit(solution)/shard_map/ppermute | solution.py:28
  114.2 26.5 %collective-permute-start.7 = (bf16[4,2,2,2,128,128]{5,4,3,2,1,0:T(8,128)(2,1)S(1)}, bf16[4,2,2,2,128,128]{5,4,3,2,1,0:T(8,128)(2,1)S(1)}, u32[]{:S(2)}, u32[]{:S(2)}) collective-permute-start(bf16[4,2,2,2,128,128]{5,4,3,2,1,0:T(8,128)(2,1)S(1)} %pad_maximum_fusion.refs_2_), channel_id=1, source_target_pairs={{0,32},{2,6},{4,36},{6,10},{8,40},{10,14},{12,44},{14,2},{16,48},{... | collective-permute-start | bytes 3145736 | tf_op jit(solution)/shard_map/ppermute | solution.py:28
  115.8 16.9 %collective-permute-start.9 = (bf16[2,5,2,128,128]{4,3,2,1,0:T(8,128)(2,1)S(1)}, bf16[2,5,2,128,128]{4,3,2,1,0:T(8,128)(2,1)S(1)}, u32[]{:S(2)}, u32[]{:S(2)}) collective-permute-start(bf16[2,5,2,128,128]{4,3,2,1,0:T(8,128)(2,1)S(1)} %pad_maximum_fusion.1.refs_1_), channel_id=1, source_target_pairs={{0,16},{2,18},{4,20},{6,22},{8,24},{10,26},{12,28},{14,30},{16,0},... | collective-permute-start | bytes 1966088 | tf_op jit(solution)/shard_map/ppermute | solution.py:28
  115.9 33.4 %collective-permute-start.8 = (bf16[4,2,2,2,128,128]{5,4,3,2,1,0:T(8,128)(2,1)S(1)}, bf16[4,2,2,2,128,128]{5,4,3,2,1,0:T(8,128)(2,1)S(1)}, u32[]{:S(2)}, u32[]{:S(2)}) collective-permute-start(bf16[4,2,2,2,128,128]{5,4,3,2,1,0:T(8,128)(2,1)S(1)} %pad_maximum_fusion.refs_2_), channel_id=1, source_target_pairs={{0,64},{2,10},{4,68},{6,14},{8,72},{10,2},{12,76},{14,6},{16,80},{... | collective-permute-start | bytes 3145736 | tf_op jit(solution)/shard_map/ppermute | solution.py:28
  154.3 16.2 %collective-permute-start.10 = (bf16[2,5,128,256]{3,2,1,0:T(8,128)(2,1)S(1)}, bf16[2,5,128,256]{3,2,1,0:T(8,128)(2,1)S(1)}, u32[]{:S(2)}, u32[]{:S(2)}) collective-permute-start(bf16[2,5,128,256]{3,2,1,0:T(8,128)(2,1)S(1)} %get-tuple-element.48), channel_id=1, source_target_pairs={{0,16},{2,18},{4,20},{6,22},{8,24},{10,26},{12,28},{14,30},{16,0},... | collective-permute-start | bytes 1966088 | tf_op jit(solution)/shard_map/ppermute | solution.py:28
  154.9 15.6 %collective-permute-start.11 = (f32[10,256]{1,0:T(8,128)S(1)}, f32[10,256]{1,0:T(8,128)S(1)}, u32[]{:S(2)}, u32[]{:S(2)}) collective-permute-start(f32[10,256]{1,0:T(8,128)S(1)} %get-tuple-element.49), channel_id=1, source_target_pairs={{0,16},{2,18},{4,20},{6,22},{8,24},{10,26},{12,28},{14,30},{16,0},... | collective-permute-start | bytes 30728 | tf_op jit(solution)/shard_map/ppermute | solution.py:28
  171.0 4.2 %collective-permute-start.12 = (bf16[256,640]{1,0:T(8,128)(2,1)S(1)}, bf16[256,640]{1,0:T(8,128)(2,1)S(1)}, u32[]{:S(2)}, u32[]{:S(2)}) collective-permute-start(bf16[256,640]{1,0:T(8,128)(2,1)S(1)} %bitcast.26), channel_id=1, source_target_pairs={{0,2},{2,0},{4,6},{6,4},{8,10},{10,8},{12,14},{14,12},{16,18},{18,... | collective-permute-start | bytes 983048 | tf_op jit(solution)/shard_map/ppermute | solution.py:28

commit v3 on v2

v3 whole, which is shorter than its diff:
```python
import functools
import math

import jax
import jax.numpy as jnp
from jax import lax
from jax.experimental import pallas as pl
from jax.experimental.pallas import tpu as pltpu
from jax.sharding import PartitionSpec as P

HD = 128
ROPE_BASE = 500000.0
NORM_EPS = 1e-05
NEG_FILL = -1e30
NY, NZ, NX, NK = 4, 2, 4, 2
GROUP = 5
HALF = 128
ALONE = 60
def split_index(c):
    return c // (NZ * NX * NK), (c // (NX * NK)) % NZ, (c // NK) % NX, c % NK


def join_index(y, z, x, k):
    return (((y % NY) * NZ + z % NZ) * NX + x % NX) * NK + k % NK


def permute(value, move):
    pairs = [(c, join_index(*move(*split_index(c)))) for c in range(NY * NZ * NX * NK)]
    return lax.ppermute(value, "ctx", pairs)


def core_swap(value):
    return permute(value, lambda y, z, x, k: (y, z, x, 1 - k))


def to_pair(value):
    return permute(value, lambda y, z, x, k: (y, 1 - z, x, k))


def to_pair_other(value):
    return permute(value, lambda y, z, x, k: (y, 1 - z, x, 1 - k))


def first_axis(value, step):
    return permute(
        value, lambda y, z, x, k: (y, z, x - step, k) if k == 0 else (y - step, z, x, k)
    )


def second_axis(value, step):
    return permute(
        value, lambda y, z, x, k: (y - step, z, x, k) if k == 0 else (y, z, x - step, k)
    )


def params(mib=24):
    return pltpu.CompilerParams(vmem_limit_bytes=mib * 1024 * 1024)


def takes(microseconds):
    return pl.CostEstimate(flops=int(microseconds * 1.15e9), bytes_accessed=0, transcendentals=0)


def vmem():
    return pl.BlockSpec(memory_space=pltpu.VMEM)


def anywhere():
    return pl.BlockSpec(memory_space=pl.ANY)


def hbm():
    return pl.BlockSpec(memory_space=pltpu.HBM)


def smem():
    return pl.BlockSpec(memory_space=pltpu.SMEM)


def choose_kernel(ids_col, ids_row, hot):
    rows = ids_col.shape[0]
    same = ids_col[...] == ids_row[...]
    row = lax.broadcasted_iota(jnp.int32, (rows, rows), 0)
    col = lax.broadcasted_iota(jnp.int32, (rows, rows), 1)
    slot = jnp.sum(jnp.where(same & (col < row), 1.0, 0.0), axis=1, keepdims=True)
    place = ids_col[...] * 4 + slot.astype(jnp.int32)
    lanes = lax.broadcasted_iota(jnp.int32, hot.shape, 1)
    hot[...] = jnp.where(lanes == place, 1.0, 0.0).astype(jnp.bfloat16)


def choose(ids, slots):
    rows = ids.shape[0]
    return pl.pallas_call(
        choose_kernel,
        in_specs=[vmem()] * 2,
        out_specs=vmem(),
        out_shape=jax.ShapeDtypeStruct((rows, slots), jnp.bfloat16),
        compiler_params=params(),
        cost_estimate=pl.CostEstimate(flops=2_000_000, bytes_accessed=600_000, transcendentals=0),
        name="choose",
    )(ids, ids.reshape(1, rows))


def relayout_kernel(experts, out, loaded, ready, arrive, leave):
    chunks, slots = loaded.shape[0], experts.shape[2]
    group = loaded.shape[2]

    def load(i):
        return pltpu.make_async_copy(experts.at[:, pl.ds(i * group, group)], loaded.at[i], arrive.at[i])

    def store(i):
        return pltpu.make_async_copy(ready.at[i], out.at[pl.ds(i * group, group)], leave.at[i])

    for i in range(chunks):
        load(i).start()
    for i in range(chunks):
        load(i).wait()
        for expert in range(experts.shape[0]):
            ready[i, :, expert * slots : (expert + 1) * slots, :] = loaded[i, expert]
        store(i).start()
    for i in range(chunks):
        store(i).wait()


def relayout(expert_out):
    experts, sources, slots, width = expert_out.shape
    chunks = 8
    group = sources // chunks
    return pl.pallas_call(
        relayout_kernel,
        in_specs=[anywhere()],
        out_specs=anywhere(),
        out_shape=jax.ShapeDtypeStruct((sources, experts * slots, width), jnp.bfloat16),
        scratch_shapes=[
            pltpu.VMEM((chunks, experts, group, slots, width), jnp.bfloat16),
            pltpu.VMEM((chunks, group, experts * slots, width), jnp.bfloat16),
            pltpu.SemaphoreType.DMA((chunks,)),
            pltpu.SemaphoreType.DMA((chunks,)),
        ],
        compiler_params=params(ALONE),
        name="relayout",
    )(expert_out)


def pick_kernel(first, hot, gate, returned, residual, shared, after, out, base, extra, done, arrive, leave):
    chunks, block, width = base.shape
    cols = slice(first, first + width)

    def loads(i):
        rows = pl.ds(i * block, block)
        return [
            pltpu.make_async_copy(residual.at[rows, cols], base.at[i], arrive.at[0, i]),
            pltpu.make_async_copy(shared.at[rows, cols], extra.at[i], arrive.at[1, i]),
        ]

    def store(i):
        return pltpu.make_async_copy(done.at[i], out.at[pl.ds(i * block, block)], leave.at[i])

    for i in range(chunks):
        for copy in loads(i):
            copy.start()
    for i in range(chunks):
        rows = slice(i * block, (i + 1) * block)
        picked = jnp.dot(hot[rows], returned[:, cols], preferred_element_type=jnp.float32)
        for copy in loads(i):
            copy.wait()
        total = base[i].astype(jnp.float32) + extra[i].astype(jnp.float32)
        done[i] = (total + gate[rows] * picked).astype(jnp.bfloat16)
        store(i).start()
    for i in range(chunks):
        store(i).wait()


def pick(part, hot, gate, returned, residual, shared, after):
    rows, width = residual.shape
    width = width // 2
    chunks = 2
    tile = pltpu.VMEM((chunks, rows // chunks, width), jnp.bfloat16)
    return pl.pallas_call(
        functools.partial(pick_kernel, part * width),
        in_specs=[vmem()] * 3 + [hbm()] * 2 + [anywhere()],
        out_specs=hbm(),
        out_shape=jax.ShapeDtypeStruct((rows, width), jnp.bfloat16),
        scratch_shapes=[
            tile,
            tile,
            tile,
            pltpu.SemaphoreType.DMA((2, chunks)),
            pltpu.SemaphoreType.DMA((chunks,)),
        ],
        compiler_params=params(10),
        cost_estimate=takes(2.5),
        name="pick",
    )(hot, gate, returned, residual, shared, after)


KV_TILES, Q_TILES = 4, 2 * GROUP


def turn(x, cos, sin):
    return x * cos + pltpu.roll(x, HD // 2, 1) * sin


def gained(h, gain):
    return (h.astype(jnp.float32) * gain.astype(jnp.float32)).astype(jnp.bfloat16)


def squared(h):
    wide = h.astype(jnp.float32)
    return jnp.sum(wide * wide, axis=1, keepdims=True)


def product(x, weights, part):
    rows = pl.ds(pl.multiple_of(part * x.shape[1], x.shape[1]), x.shape[1])
    return [jnp.dot(x, w[rows, :], preferred_element_type=jnp.float32) for w in weights]


def own_kernel(where, ha, hb, gain, wk, wv, wq, part, squares):
    squares[...] = squared(ha[...]) + squared(hb[...])
    tp = where[0]
    x = jnp.concatenate([gained(ha[...], gain[2 * tp]), gained(hb[...], gain[2 * tp + 1])], axis=1)
    start = 0
    for values in product(x, (wk, wv, wq), tp):
        part[:, start : start + values.shape[1]] = values
        start += values.shape[1]


def more_kernel(where, h, gain, wk, wv, wq, old, old_squares, part, squares):
    squares[...] = old_squares[...] + squared(h[...])
    start = 0
    part_in = 2 - 2 * where[0]
    for values in product(gained(h[...], gain[part_in]), (wk, wv, wq), part_in):
        cols = slice(start, start + values.shape[1])
        part[:, cols] = old[:, cols] + values
        start += values.shape[1]


def last_kernel(where, h, gain, wk, wv, wq, old, old_squares, cos, sin, kv_mine, q_mine, q_other, other):
    total = old_squares[...] + squared(h[...])
    factor = lax.rsqrt(total / (4 * h.shape[1]) + NORM_EPS)
    part_in = 3 - 2 * where[0]
    keys, values, queries = product(gained(h[...], gain[part_in]), (wk, wv, wq), part_in)
    width = 2 * HD
    keys = (old[:, :width] + keys) * factor
    values = (old[:, width : 2 * width] + values) * factor
    queries = (old[:, 2 * width :] + queries) * (factor * (1.0 / HD**0.5 * math.log2(math.e)))

    def columns(array, head):
        return array[:, head * HD : (head + 1) * HD]

    def sides(array, axis):
        return jnp.split(array.astype(jnp.bfloat16), 2, axis=axis)

    groups = []
    for group in range(2):
        key = sides(turn(columns(keys, group), cos[...], sin[...]), 0)
        value = sides(columns(values, group).T, 1)
        kv = [key[0], value[0], key[1], value[1]]
        q = []
        for head in range(GROUP):
            q += sides(turn(columns(queries, group * GROUP + head), cos[...], sin[...]).T, 1)
        groups.append((kv, q))

    def write(mine, others):
        for i in range(KV_TILES):
            kv_mine[i // 2, i % 2] = mine[0][i]
            other[i] = others[0][i]
        for i in range(Q_TILES):
            q_mine[i // 2, i % 2] = mine[1][i]
            q_other[i // 2, i % 2] = others[1][i]
            other[KV_TILES + i] = others[1][i]

    pl.when(where[1] == 0)(lambda: write(*groups))
    pl.when(where[1] == 1)(lambda: write(*groups[::-1]))


def project(kernel, where, ins, outs, time, name):
    return pl.pallas_call(
        kernel,
        in_specs=[smem()] + [vmem()] * len(ins),
        out_specs=[vmem()] * len(outs),
        out_shape=[jax.ShapeDtypeStruct(shape, dtype) for shape, dtype in outs],
        compiler_params=params(),
        cost_estimate=takes(time),
        name=name,
    )(where, *ins)


def project_own(where, ha, hb, gain, weights):
    rows, cols = ha.shape[0], sum(w.shape[1] for w in weights)
    outs = [((rows, cols), jnp.float32), ((rows, 1), jnp.float32)]
    return project(own_kernel, where, (ha, hb, gain, *weights), outs, 5, "project_own")


def project_more(where, h, gain, weights, partial):
    outs = [(array.shape, array.dtype) for array in partial]
    return project(more_kernel, where, (h, gain, *weights, *partial), outs, 2, "project_more")


def project_last(where, h, gain, weights, partial, cos, sin):
    q = (GROUP, 2, HD, HALF)
    shapes = [(2, 2, HALF, HD), q, q, (KV_TILES + Q_TILES, HALF, HD)]
    outs = [(shape, jnp.bfloat16) for shape in shapes]
    return project(last_kernel, where, (h, gain, *weights, *partial, cos, sin), outs, 2, "project_last")


ONES = 16


def attend_kernel(counts, diag, resume, finish, waits, *refs):
    flags, q, refs = refs[0], refs[1], refs[2:]
    kvs, refs = refs[: len(counts)], refs[len(counts) :]
    olds = refs[:3] if resume else ()
    refs = refs[len(olds) + waits :]
    parts = ()
    if finish:
        parts, refs = refs[:2], refs[2:]
    acc, den, top, klist, vlist = refs
    total = klist.shape[0]

    if resume:
        acc[...] = olds[0][...]
        den[...] = olds[1][...]
        top[...] = olds[2][...]
    else:
        acc[...] = jnp.zeros_like(acc)
        den[...] = jnp.zeros_like(den)
        top[...] = jnp.full_like(top, NEG_FILL)

    vlist[:, HD:, :] = jnp.ones((total, ONES, 2 * HALF), jnp.bfloat16)

    def put(place, kv, block, side):
        for core in range(2):
            span = slice(core * HALF, (core + 1) * HALF)
            klist[place, span, :] = kv[block, core, side, 0]
            vlist[place, :HD, span] = kv[block, core, side, 1]

    last = total - 2 if diag else total - 1
    front, back = jnp.int32(0), jnp.int32(last)
    start = 0
    for kv, count in zip(kvs, counts):
        for block in range(count):
            put(front, kv, block, 0)
            front = front + 1
            if diag and start + block == 0:
                continue
            early = flags[start + block]
            put(jnp.where(early == 1, back, front), kv, block, 1 - early)
            front = front + 1 - early
            back = back - early
        start += count
    n_late = front
    n_early = last - back

    def update(side, places, mask):
        keys = jnp.concatenate([klist[p] for p in places], axis=0)
        scores = []
        for head in range(GROUP):
            columns = jnp.concatenate([q[0, head, side], q[1, head, side]], axis=1)
            scores.append(jnp.dot(keys, columns, preferred_element_type=jnp.float32))
        values = jnp.concatenate([vlist[p] for p in places], axis=1)
        for head in range(GROUP):
            s = scores[head]
            if mask is not None:
                s = jnp.where(mask, s, NEG_FILL)
            old = top[side, head]
            new = jnp.maximum(old, jnp.max(s, axis=0, keepdims=True))
            weights = jnp.exp2(s - new[:1]).astype(jnp.bfloat16)
            prod = jnp.dot(values, weights, preferred_element_type=jnp.float32)
            keep = jnp.exp2(old - new)
            acc[side, head] = acc[side, head] * keep[:1] + prod[:HD]
            den[side, head] = den[side, head] * keep + prod[HD : HD + 8]
            top[side, head] = new

    if diag:
        core = flags[0]
        row = lax.broadcasted_iota(jnp.int32, (2 * HALF, 2 * HALF), 0)
        col = lax.broadcasted_iota(jnp.int32, (2 * HALF, 2 * HALF), 1)

        def own(side, carry):
            first = jnp.where(side == 0, core, 1 - core)
            key_pos = jnp.where(row < HALF, row + first * HALF, row - first * HALF)
            query_pos = jnp.where(col < HALF, col + first * HALF, col - first * HALF)
            put(total - 1, kvs[0], 0, side)
            update(side, (total - 1,), key_pos <= query_pos)
            return carry

        lax.fori_loop(0, 2, own, 0)

    pairs = n_late // 2
    early_pairs = n_early // 2
    def two(i, carry):
        late = i < pairs
        j = i - pairs
        one = jnp.where(late, 2 * i, last - 2 * j)
        other = jnp.where(late, 2 * i + 1, last - 2 * j - 1)
        update(jnp.where(late, 1, 0), (one, other), None)
        return carry

    lax.fori_loop(0, pairs + early_pairs, two, 0)
    odd_late = n_late - 2 * pairs
    odd_early = n_early - 2 * early_pairs

    def one(i, carry):
        late = i < odd_late
        update(jnp.where(late, 1, 0), (jnp.where(late, n_late - 1, last - n_early + 1),), None)
        return carry

    lax.fori_loop(0, odd_late + odd_early, one, 0)

    if finish:
        write_parts(acc, den, top, parts)


def write_parts(acc, den, top, parts):
    for side in range(2):
        for head in range(GROUP):
            denominator = den[side, head]
            some = denominator > 0.0
            safe = jnp.where(some, denominator, 1.0)
            inverse = jnp.where(some, 1.0 / safe, 0.0)
            value = (acc[side, head] * inverse[:1]).astype(jnp.bfloat16)
            level = jnp.where(some, top[side, head] + jnp.log2(safe), NEG_FILL)
            high = level.astype(jnp.bfloat16)
            low = (level - high.astype(jnp.float32)).astype(jnp.bfloat16)
            levels = jnp.concatenate([high, low], axis=0)
            for core in range(2):
                rows = slice(core * HALF, (core + 1) * HALF)
                parts[core][side, head, :HD] = value[:, rows]
                parts[core][side, head, HD:] = levels[:, rows]


ACC = (2, GROUP, HD, 2 * HALF)
ROWS = (2, GROUP, 8, 2 * HALF)
PART = (2, GROUP, HD + 16, HALF)


def attend(flags, q, kvs, state, diag=False, finish=False, after=(), time=None):
    counts = tuple(kv.shape[0] for kv in kvs)
    n = sum(counts)
    total = 2 * n
    olds = [] if state is None else list(state)
    states = (ACC, ROWS, ROWS)
    scratch = [
        pltpu.VMEM((total, 2 * HALF, HD), jnp.bfloat16),
        pltpu.VMEM((total, HD + ONES, 2 * HALF), jnp.bfloat16),
    ]
    if finish:
        shapes = [jax.ShapeDtypeStruct(PART, jnp.bfloat16)] * 2
        scratch = [pltpu.VMEM(shape, jnp.float32) for shape in states] + scratch
    else:
        shapes = [jax.ShapeDtypeStruct(shape, jnp.float32) for shape in states]
    return pl.pallas_call(
        functools.partial(attend_kernel, counts, diag, state is not None, finish, len(after)),
        in_specs=[smem()] + [vmem()] * (1 + len(kvs) + len(olds)) + [anywhere()] * len(after),
        out_specs=[vmem()] * len(shapes),
        out_shape=shapes,
        scratch_shapes=scratch,
        compiler_params=params(),
        cost_estimate=takes(1.15 * n if time is None else time),
        name="attend",
    )(flags, q, *kvs, *olds, *after)


def divide_kernel(waits, *refs):
    acc, den, top = refs[:3]
    write_parts(acc, den, top, refs[3 + waits :])


def divide(state, after):
    return pl.pallas_call(
        functools.partial(divide_kernel, len(after)),
        in_specs=[vmem()] * 3 + [anywhere()] * len(after),
        out_specs=[vmem()] * 2,
        out_shape=[jax.ShapeDtypeStruct(PART, jnp.bfloat16)] * 2,
        compiler_params=params(),
        cost_estimate=takes(0.7),
        name="divide",
    )(*state, *after)


def join_kernel(*refs):
    out = refs[-1]
    for i in range(out.shape[0]):
        out[i] = refs[i][0]


def join(blocks, after):
    return pl.pallas_call(
        join_kernel,
        in_specs=[vmem()] * len(blocks) + [anywhere()],
        out_specs=vmem(),
        out_shape=jax.ShapeDtypeStruct((len(blocks),) + blocks[0].shape[1:], jnp.bfloat16),
        compiler_params=params(),
        cost_estimate=takes(0.3),
        name="join",
    )(*blocks, after)


def merge_kernel(core, own, own_pair, sibling, sibling_pair, out):
    def level(part, side, head):
        return part[side, head, HD : HD + 8].astype(jnp.float32)[:1] + part[
            side, head, HD + 8 :
        ].astype(jnp.float32)[:1]

    for group, (one, two) in ((core[0], (own, own_pair)), (1 - core[0], (sibling, sibling_pair))):
        for side in range(2):
            for head in range(GROUP):
                mine, other = level(one, side, head), level(two, side, head)
                top = jnp.maximum(mine, other)
                first = jnp.exp2(mine - top)
                second = jnp.exp2(other - top)
                weight = 1.0 / (first + second)
                value = one[side, head, :HD].astype(jnp.float32) * (first * weight)
                value = value + two[side, head, :HD].astype(jnp.float32) * (second * weight)
                cols = pl.ds(pl.multiple_of((group * GROUP + head) * HD, HD), HD)
                out[side * HALF : (side + 1) * HALF, cols] = value.T.astype(jnp.bfloat16)


def merge(core, own, own_pair, sibling, sibling_pair):
    return pl.pallas_call(
        merge_kernel,
        in_specs=[smem()] + [vmem()] * 4,
        out_specs=vmem(),
        out_shape=jax.ShapeDtypeStruct((2 * HALF, 2 * GROUP * HD), jnp.bfloat16),
        compiler_params=params(),
        name="merge",
    )(core, own, own_pair, sibling, sibling_pair)


def rotations(ctx_index, rows):
    row = jnp.arange(rows, dtype=jnp.int32)
    half = rows // 2
    count = NY * NZ * NX * NK
    pos = jnp.where(row < half, ctx_index * half + row, (2 * count - 1 - ctx_index) * half + row - half)
    frequency = ROPE_BASE ** (-(jnp.arange(HD // 2, dtype=jnp.float32) * 2.0 / HD))
    angles = pos.astype(jnp.float32)[:, None] * frequency[None, :]
    cos, sin = jnp.cos(angles), jnp.sin(angles)
    return jnp.concatenate([cos, cos], axis=1), jnp.concatenate([-sin, sin], axis=1)


def chip_order(y, z, x):
    return (y * NZ + z) * NX + x


def shards(residual, shared_out, expert_out, routing, gate_score, norm_gain, w_query, w_key, w_value):
    rows, half_width = residual.shape
    ctx_index = lax.axis_index("ctx")
    tp_index = lax.axis_index("tp")
    y, z, x, k = split_index(ctx_index)
    cos, sin = rotations(ctx_index, rows)

    own_experts, sources, slots, _ = expert_out.shape
    returned = lax.all_to_all(relayout(expert_out), "ctx", split_axis=0, concat_axis=0, tiled=True)
    returned = returned.reshape(sources * own_experts * slots, half_width)
    hot = choose(routing, returned.shape[0])
    ha = pick(0, hot, gate_score, returned, residual, shared_out, hot)
    hb = pick(1, hot, gate_score, returned, residual, shared_out, ha)
    hidden = jnp.concatenate([ha, hb], axis=1)

    other_a, other_b = (lax.ppermute(h, "tp", [(0, 1), (1, 0)]) for h in (ha, hb))
    where = jnp.stack([tp_index, k])
    gain = norm_gain.reshape(4, 1, half_width // 2)
    weights = (w_key, w_value, w_query)
    partial = project_own(where, ha, hb, gain, weights)
    partial = project_more(where, other_a, gain, weights, partial)
    kv_mine, q_mine, q_other, to_other = project_last(where, other_b, gain, weights, partial, cos, sin)

    from_other = core_swap(to_other)
    block = jnp.stack([kv_mine, from_other[:KV_TILES].reshape(kv_mine.shape)])[None]
    q_own = jnp.stack([q_mine, from_other[KV_TILES:].reshape(q_mine.shape)])
    q_pair = jnp.stack([to_pair(q_mine), to_pair_other(q_other)])

    near = [first_axis(block, step) for step in (1, -1, 2)]
    own_state = attend(k.reshape(1), q_own, [block], None, diag=True, time=30)
    line = join([block] + near, own_state[2])
    ahead, behind = second_axis(line, 1), second_axis(line, -1)
    far = [ahead, behind, second_axis(ahead[:2], 1), second_axis(behind[2:], -1)]

    steps = jnp.array([0, 1, -1, 2], jnp.int32)

    def before(first, second, chip):
        by = jnp.where(k == 0, second, first)
        bx = jnp.where(k == 0, first, second)
        return (chip_order((y + by) % NY, z, (x + bx) % NX) < chip).astype(jnp.int32)

    zero = jnp.zeros((4,), jnp.int32)
    own_flags, pair_flags = (
        jnp.concatenate([before(steps, zero + step, chip_order(y, at, x)) for step in (0, 1, -1, 2)])
        for at in (z, 1 - z)
    )
    pair_state = attend(pair_flags[:4], q_pair, [line], None, time=7)
    pair_state = attend(pair_flags[4:12], q_pair, far[:2], pair_state)
    pair_same, pair_other = attend(pair_flags[12:], q_pair, far[2:], pair_state, finish=True)
    own_pair, sibling_pair = to_pair(pair_same), to_pair_other(pair_other)
    own_state = attend(own_flags[1:], q_own, near + far, own_state, after=(pair_same,))
    own_same, own_other = divide(own_state, (own_pair, sibling_pair))
    attended = merge(k.reshape(1), own_same, own_pair, core_swap(own_other), sibling_pair)
    return hidden, attended


def solution(mesh):
    return jax.shard_map(
        shards,
        mesh=mesh,
        in_specs=(
            P("ctx", "tp"),
            P("ctx", "tp"),
            P("ctx", None, None, "tp"),
            P("ctx", None),
            P("ctx", None),
            P(),
            P(None, "tp"),
            P(None, "tp"),
            P(None, "tp"),
        ),
        out_specs=(P("ctx", "tp"), P("ctx", "tp")),
        check_vma=False,
    )
```

time: 177 us -> 159 us (0.90)
  local copies, waits for them, and re-layouts: 19.5 us -> 7.26 us
  waiting for transfers between devices: 75.7 us -> 67.8 us
  starting transfers between devices: 24.8 us -> 30.1 us
  Pallas kernels: 53.1 us -> 50.6 us
    unnamed x39 -> x24, local copies, waits for them, and re-layouts: 16.4 us -> 7.14 us
    ppermute x12 -> x13, waiting for transfers between devices: 23 us -> 14.6 us  [permute(): return lax.ppermute(value, 'ctx', pairs)]
    ppermute x12 -> x13, starting transfers between devices: 11.6 us -> 16 us  [permute(): return lax.ppermute(value, 'ctx', pairs)]
    reshape x2 -> x1, local copies, waits for them, and re-layouts: 2.94 us -> 0.01 us  [shards(): gain = norm_gain.reshape(4, 1, half_width // 2)]
    pallas_call x6 -> x9, Pallas kernels: 16.4 us -> 14.4 us  [the longest x3 7.54 us: project(): pl.pallas_call(kernel, in_specs=[smem()] + [vmem()] * len(ins), out_specs...]
    ppermute x1 -> x2, waiting for transfers between devices: 16.7 us -> 18.3 us  [shards(): lax.ppermute(h, 'tp', [(0, 1), (1, 0)])]
  transfers between devices with their start and end apart: 14 -> 16, of which waited for: 8 -> 9; matrix products, arithmetic and copies ran while one was open for 1% -> 2% of each run, Pallas kernels for 24% -> 24%
where the time goes in v3:
time: 159 us
  waiting for transfers between devices  67.8 us (43%)
  Pallas kernels  50.6 us (32%)
  starting transfers between devices  30.1 us (19%)
  local copies, waits for them, and re-layouts  7.26 us (5%)
  other arithmetic  2.33 us (1%)
    pallas_call x5, Pallas kernels, attend(): pl.pallas_call(functools.partial(attend_kernel, counts, diag, state is no...  35.9 us
    all_to_all x1, waiting for transfers between devices, shards(): lax.all_to_all(relayout(expert_out), 'ctx', split_axis=0, concat_axis=0,...  34.9 us
    ppermute x2, waiting for transfers between devices, shards(): lax.ppermute(h, 'tp', [(0, 1), (1, 0)])  18.3 us
    ppermute x13, starting transfers between devices, permute(): return lax.ppermute(value, 'ctx', pairs)  16 us
    ppermute x13, waiting for transfers between devices, permute(): return lax.ppermute(value, 'ctx', pairs)  14.6 us
    all_to_all x1, starting transfers between devices, shards(): lax.all_to_all(relayout(expert_out), 'ctx', split_axis=0, concat_axis=0,...  12.4 us
    pallas_call x3, Pallas kernels, project(): pl.pallas_call(kernel, in_specs=[smem()] + [vmem()] * len(ins), out_specs...  7.54 us
    unnamed x24, local copies, waits for them, and re-layouts  7.14 us
  transfers between devices with their start and end apart: 16, of which 9 were waited for; matrix products, arithmetic and copies ran while one was open for 2% of the time, Pallas kernels for 24%

profile of v3, /device:TPU:1, one launch (start us, length us, event | category | flops | bytes accessed | tf_op | source)
XLA Modules:
  0.0 159.2 jit_solution(17478748256825439743)
XLA Ops:
  0.6 2.7 %relayout.1 = bf16[64,8,2560]{2,1,0:T(8,128)(2,1)} custom-call(bf16[2,64,4,2560]{3,2,1,0:T(4,128)(2,1)} %experts.1), custom_call_target="tpu_custom_call" | custom-call | tf_op jit(solution)/shard_map/relayout/pallas_call | solution.py:129
  3.4 12.4 %all-to-all-start = ((bf16[64,8,2560]{2,1,0:T(8,128)(2,1)}), bf16[64,8,2560]{2,1,0:T(8,128)(2,1)S(1)}, u32[]{:S(2)}, u32[]{:S(2)}) async-start(bf16[64,8,2560]{2,1,0:T(8,128)(2,1)} %relayout.1), calls=%async_computation | async-start | bytes 5242880 | tf_op jit(solution)/shard_map/all_to_all | solution.py:554
  15.9 0.1 copy.15.ids_col
  16.0 0.1 copy.16.gate
  16.3 0.3 choose.1.hot.after
  16.5 0.1 pad_add_fusion.1.where
  16.6 0.5 fusion
  17.2 0.1 pad_maximum_fusion.3
  17.4 34.9 %all-to-all-done = bf16[64,8,2560]{2,1,0:T(8,128)(2,1)S(1)} async-done(((bf16[64,8,2560]{2,1,0:T(8,128)(2,1)}), bf16[64,8,2560]{2,1,0:T(8,128)(2,1)S(1)}, u32[]{:S(2)}, u32[]{:S(2)}) %all-to-all-start) | async-done | bytes 2621472 | tf_op jit(solution)/shard_map/all_to_all | solution.py:554
  52.3 1.3 copy-done.4
  53.6 1.3 copy-done.6
  54.9 1.4 pick.2.after.ha
  56.3 0.8 collective-permute-start.1
  57.1 2.1 %copy-done.5 = bf16[256,2560]{1,0:T(8,128)(2,1)S(1)} copy-done((bf16[256,2560]{1,0:T(8,128)(2,1)S(1)}, bf16[256,2560]{1,0:T(8,128)(2,1)}, u32[]{:S(2)}) %copy-start.5) | copy-done | bytes 1310744
  59.2 2.1 %copy-done.7 = bf16[256,2560]{1,0:T(8,128)(2,1)S(1)} copy-done((bf16[256,2560]{1,0:T(8,128)(2,1)S(1)}, bf16[256,2560]{1,0:T(8,128)(2,1)}, u32[]{:S(2)}) %copy-start.7) | copy-done | bytes 1310744
  61.3 1.4 pick.3.hb
  62.7 0.8 collective-permute-start
  63.5 3.2 %project_own.1 = (f32[256,1792]{1,0:T(8,128)S(1)}, f32[256,1]{1,0:T(8,128)S(1)}) custom-call(s32[2]{0:T(128)S(1)} %pad_add_fusion.1.where, bf16[256,1280]{1,0:T(8,128)(2,1)S(1)} %pick.2.after.ha, bf16[256,1280]{1,0:T(8,128)(2,1)S(1)} %pick.3.hb, bf16[4,1,1280]{2,1,0:T(2,128)(2,1)S(1)} %reshape.38.gain, bf16[5120,256]{1,0:T(8,128)(2,1)S(1)} %copy-done.1, ...), custom_call_target="tpu_custom_call" | custom-call | flops 5750000128 | tf_op jit(solution)/shard_map/project_own/pallas_call | solution.py:278
  66.7 6.2 %collective-permute-done.1.h = bf16[256,1280]{1,0:T(8,128)(2,1)S(1)} collective-permute-done((bf16[256,1280]{1,0:T(8,128)(2,1)S(1)}, bf16[256,1280]{1,0:T(8,128)(2,1)S(1)}, u32[]{:S(2)}, u32[]{:S(2)}) %collective-permute-start.1) | collective-permute-done | bytes 655392 | tf_op jit(solution)/shard_map/ppermute | solution.py:561
  72.8 1.9 %project_more.1 = (f32[256,1792]{1,0:T(8,128)S(1)}, f32[256,1]{1,0:T(8,128)S(1)}) custom-call(s32[2]{0:T(128)S(1)} %pad_add_fusion.1.where, bf16[256,1280]{1,0:T(8,128)(2,1)S(1)} %collective-permute-done.1.h, bf16[4,1,1280]{2,1,0:T(2,128)(2,1)S(1)} %reshape.38.gain, bf16[5120,256]{1,0:T(8,128)(2,1)S(1)} %copy-done.1, bf16[5120,256]{1,0:T(8,128)(2,1)S(1)} %copy-done.2, ...), custom_call_target="tpu_custom_call" | custom-call | flops 2300000000 | tf_op jit(solution)/shard_map/project_more/pallas_call | solution.py:278
  74.8 12.1 %collective-permute-done.h = bf16[256,1280]{1,0:T(8,128)(2,1)S(1)} collective-permute-done((bf16[256,1280]{1,0:T(8,128)(2,1)S(1)}, bf16[256,1280]{1,0:T(8,128)(2,1)S(1)}, u32[]{:S(2)}, u32[]{:S(2)}) %collective-permute-start) | collective-permute-done | bytes 655392 | tf_op jit(solution)/shard_map/ppermute | solution.py:561
  86.9 2.5 %project_last.1 = (bf16[2,2,128,128]{3,2,1,0:T(8,128)(2,1)S(1)}, bf16[5,2,128,128]{3,2,1,0:T(8,128)(2,1)S(1)}, bf16[5,2,128,128]{3,2,1,0:T(8,128)(2,1)S(1)}, bf16[14,128,128]{2,1,0:T(8,128)(2,1)S(1)}) custom-call(s32[2]{0:T(128)S(1)} %pad_add_fusion.1.where, bf16[256,1280]{1,0:T(8,128)(2,1)S(1)} %collective-permute-done.h, ...), custom_call_target="tpu_custom_call" | custom-call | flops 2300000000 | tf_op jit(solution)/shard_map/project_last/pallas_call | solution.py:278
  89.4 0.8 collective-permute-start.2
  90.2 0.1 pad_add_fusion
  90.3 2.9 %collective-permute-start.10 = (bf16[5,2,128,128]{3,2,1,0:T(8,128)(2,1)S(1)}, bf16[5,2,128,128]{3,2,1,0:T(8,128)(2,1)S(1)}, u32[]{:S(2)}, u32[]{:S(2)}) collective-permute-start(bf16[5,2,128,128]{3,2,1,0:T(8,128)(2,1)S(1)} %get-tuple-element.30), channel_id=1, source_target_pairs={{0,16},{2,18},{4,20},{6,22},{8,24},{10,26},{12,28},{14,30},{16,0},... | collective-permute-start | bytes 983048 | tf_op jit(solution)/shard_map/ppermute | solution.py:29
  93.2 0.9 collective-permute-start.3
  94.1 0.7 collective-permute-start.4
  94.7 0.8 collective-permute-start.5
  95.6 2.0 %attend.5 = (f32[2,5,128,256]{3,2,1,0:T(8,128)S(1)}, f32[2,5,8,256]{3,2,1,0:T(8,128)S(1)}, f32[2,5,8,256]{3,2,1,0:T(8,128)S(1)}) custom-call(s32[1]{0:T(128)} %bitcast.2.refs_0_.core, bf16[2,5,2,128,128]{4,3,2,1,0:T(8,128)(2,1)S(1)} %pad_maximum_fusion.1.refs_1_, bf16[1,2,2,2,128,128]{5,4,3,2,1,0:T(8,128)(2,1)S(1)} %maximum_bitcast_fusion.refs_2_.refs_0_), custom_call_target="tpu_custom_call" | custom-call | flops 34500001792 | tf_op jit(solution)/shard_map/attend/pallas_call | solution.py:453
  97.6 1.2 collective-permute-done.3.refs_1_.refs_2_
  98.8 4.8 %collective-permute-done.4.refs_2_.refs_3_ = bf16[1,2,2,2,128,128]{5,4,3,2,1,0:T(8,128)(2,1)S(1)} collective-permute-done((bf16[1,2,2,2,128,128]{5,4,3,2,1,0:T(8,128)(2,1)S(1)}, bf16[1,2,2,2,128,128]{5,4,3,2,1,0:T(8,128)(2,1)S(1)}, u32[]{:S(2)}, u32[]{:S(2)}) %collective-permute-start.4) | collective-permute-done | bytes 262176 | tf_op jit(solution)/shard_map/ppermute | solution.py:29
  103.7 1.5 collective-permute-start.7
  105.4 2.5 %collective-permute-done.10 = bf16[5,2,128,128]{3,2,1,0:T(8,128)(2,1)S(1)} collective-permute-done((bf16[5,2,128,128]{3,2,1,0:T(8,128)(2,1)S(1)}, bf16[5,2,128,128]{3,2,1,0:T(8,128)(2,1)S(1)}, u32[]{:S(2)}, u32[]{:S(2)}) %collective-permute-start.10) | collective-permute-done | bytes 327712 | tf_op jit(solution)/shard_map/ppermute | solution.py:29
  107.9 4.9 %attend.6 = (f32[2,5,128,256]{3,2,1,0:T(8,128)S(1)}, f32[2,5,8,256]{3,2,1,0:T(8,128)S(1)}, f32[2,5,8,256]{3,2,1,0:T(8,128)S(1)}) custom-call(s32[4]{0:T(128)S(1)} %get-tuple-element.50.refs_0_, bf16[2,5,2,128,128]{4,3,2,1,0:T(8,128)(2,1)S(1)} %pad_maximum_fusion.2.refs_1_, bf16[4,2,2,2,128,128]{5,4,3,2,1,0:T(8,128)(2,1)S(1)} %join.1.refs_2_), custom_call_target="tpu_custom_call" | custom-call | flops 8049999872 | tf_op jit(solution)/shard_map/attend/pallas_call | solution.py:453
  112.8 4.9 %collective-permute-done.6.refs_2_.refs_5_ = bf16[4,2,2,2,128,128]{5,4,3,2,1,0:T(8,128)(2,1)S(1)} collective-permute-done((bf16[4,2,2,2,128,128]{5,4,3,2,1,0:T(8,128)(2,1)S(1)}, bf16[4,2,2,2,128,128]{5,4,3,2,1,0:T(8,128)(2,1)S(1)}, u32[]{:S(2)}, u32[]{:S(2)}) %collective-permute-start.6) | collective-permute-done | bytes 1048608 | tf_op jit(solution)/shard_map/ppermute | solution.py:29
  117.7 1.3 collective-permute-start.8
  119.1 0.3 collective-permute-start.9
  119.4 8.6 %attend.7 = (f32[2,5,128,256]{3,2,1,0:T(8,128)S(1)}, f32[2,5,8,256]{3,2,1,0:T(8,128)S(1)}, f32[2,5,8,256]{3,2,1,0:T(8,128)S(1)}) custom-call(s32[8]{0:T(128)S(1)} %add_convert_fusion.refs_0_, bf16[2,5,2,128,128]{4,3,2,1,0:T(8,128)(2,1)S(1)} %pad_maximum_fusion.2.refs_1_, bf16[4,2,2,2,128,128]{5,4,3,2,1,0:T(8,128)(2,1)S(1)} %collective-permute-done.6.refs_2_.refs_5_, ...), custom_call_target="tpu_custom_call" | custom-call | flops 10579999744 | tf_op jit(solution)/shard_map/attend/pallas_call | solution.py:453
  128.0 0.7 collective-permute-done.9.refs_3_.refs_8_
  128.7 5.0 %attend.8 = (bf16[2,5,144,128]{3,2,1,0:T(8,128)(2,1)S(1)}, bf16[2,5,144,128]{3,2,1,0:T(8,128)(2,1)S(1)}) custom-call(s32[4]{0:T(128)S(1)} %get-tuple-element.65.refs_0_, bf16[2,5,2,128,128]{4,3,2,1,0:T(8,128)(2,1)S(1)} %pad_maximum_fusion.2.refs_1_, bf16[2,2,2,2,128,128]{5,4,3,2,1,0:T(8,128)(2,1)S(1)} %collective-permute-done.8.refs_2_.refs_7_, ...), custom_call_target="tpu_custom_call" | custom-call | flops 5289999872 | tf_op jit(solution)/shard_map/attend/pallas_call | solution.py:453
  133.6 0.5 collective-permute-start.12
  134.1 6.4 %collective-permute-start.13 = (bf16[2,5,144,128]{3,2,1,0:T(8,128)(2,1)S(1)}, bf16[2,5,144,128]{3,2,1,0:T(8,128)(2,1)S(1)}, u32[]{:S(2)}, u32[]{:S(2)}) collective-permute-start(bf16[2,5,144,128]{3,2,1,0:T(8,128)(2,1)S(1)} %get-tuple-element.47), channel_id=1, source_target_pairs={{0,18},{2,16},{4,22},{6,20},{8,26},{10,24},{12,30},{14,28},{16,2},... | collective-permute-start | bytes 1105928 | tf_op jit(solution)/shard_map/ppermute | solution.py:29
  140.4 15.5 %attend.9 = (f32[2,5,128,256]{3,2,1,0:T(8,128)S(1)}, f32[2,5,8,256]{3,2,1,0:T(8,128)S(1)}, f32[2,5,8,256]{3,2,1,0:T(8,128)S(1)}) custom-call(s32[15]{0:T(128)S(1)} %slice_convert_fusion.refs_0_, bf16[2,5,2,128,128]{4,3,2,1,0:T(8,128)(2,1)S(1)} %pad_maximum_fusion.1.refs_1_, bf16[1,2,2,2,128,128]{5,4,3,2,1,0:T(8,128)(2,1)S(1)} %collective-permute-done.3.refs_1_.refs_2_, ...), custom_call_target="tpu_custom_call" | custom-call | flops 19837499392 | tf_op jit(solution)/shard_map/attend/pallas_call | solution.py:453
  156.0 0.1 divide.1
  156.1 0.1 collective-permute-start.14
  156.2 1.1 pad_maximum_fusion
  157.3 0.5 collective-permute-done.14.sibling
  157.9 1.3 merge.1
  (43 shorter events, 0.7 us)
Async XLA Ops:
  3.3 12.6 %copy-start.3 = (s32[256,1]{0,1:T(1,128)S(1)}, s32[256,1]{0,1:T(1,128)}, u32[]{:S(2)}) copy-start(s32[256,1]{0,1:T(1,128)} %param.13) | copy-start | bytes 3076
  3.3 12.7 %copy-start.9 = (f32[256,1]{0,1:T(1,128)S(1)}, f32[256,1]{0,1:T(1,128)}, u32[]{:S(2)}) copy-start(f32[256,1]{0,1:T(1,128)} %param.14) | copy-start | bytes 3076
  3.3 12.8 %copy-start.8 = (bf16[5120]{0:T(1024)(128)(2,1)S(1)}, bf16[5120]{0:T(1024)(128)(2,1)}, u32[]{:S(2)}) copy-start(bf16[5120]{0:T(1024)(128)(2,1)} %param.15) | copy-start | bytes 30724
  3.4 48.9 %all-to-all-start = ((bf16[64,8,2560]{2,1,0:T(8,128)(2,1)}), bf16[64,8,2560]{2,1,0:T(8,128)(2,1)S(1)}, u32[]{:S(2)}, u32[]{:S(2)}) async-start(bf16[64,8,2560]{2,1,0:T(8,128)(2,1)} %relayout.1), calls=%async_computation | async-start | bytes 5242880 | tf_op jit(solution)/shard_map/all_to_all | solution.py:554
  15.8 1.5 copy-start.10
  52.3 1.3 copy-start.4
  53.6 1.3 copy-start.6
  54.9 8.6 %copy-start = (bf16[5120,1280]{1,0:T(8,128)(2,1)S(1)}, bf16[5120,1280]{1,0:T(8,128)(2,1)}, u32[]{:S(2)}) copy-start(bf16[5120,1280]{1,0:T(8,128)(2,1)} %wq.5) | copy-start | bytes 39321604
  56.3 7.2 %copy-start.1 = (bf16[5120,256]{1,0:T(8,128)(2,1)S(1)}, bf16[5120,256]{1,0:T(8,128)(2,1)}, u32[]{:S(2)}) copy-start(bf16[5120,256]{1,0:T(8,128)(2,1)} %wk.5) | copy-start | bytes 7864324
  56.3 7.2 %copy-start.2 = (bf16[5120,256]{1,0:T(8,128)(2,1)S(1)}, bf16[5120,256]{1,0:T(8,128)(2,1)}, u32[]{:S(2)}) copy-start(bf16[5120,256]{1,0:T(8,128)(2,1)} %wv.5) | copy-start | bytes 7864324
  56.3 16.5 %collective-permute-start.1 = (bf16[256,1280]{1,0:T(8,128)(2,1)S(1)}, bf16[256,1280]{1,0:T(8,128)(2,1)S(1)}, u32[]{:S(2)}, u32[]{:S(2)}) collective-permute-start(bf16[256,1280]{1,0:T(8,128)(2,1)S(1)} %pick.2.after.ha), channel_id=1, source_target_pairs={{0,1},{1,0},{2,3},{3,2},{4,5},{5,4},{6,7},{7,6},{8,9},{9,8},{10,11... | collective-permute-start | bytes 1966088 | tf_op jit(solution)/shard_map/ppermute | solution.py:561
  57.1 2.1 %copy-start.5 = (bf16[256,2560]{1,0:T(8,128)(2,1)S(1)}, bf16[256,2560]{1,0:T(8,128)(2,1)}, u32[]{:S(2)}) copy-start(bf16[256,2560]{1,0:T(8,128)(2,1)} %residual.3) | copy-start | bytes 3932164
  59.2 2.1 %copy-start.7 = (bf16[256,2560]{1,0:T(8,128)(2,1)S(1)}, bf16[256,2560]{1,0:T(8,128)(2,1)}, u32[]{:S(2)}) copy-start(bf16[256,2560]{1,0:T(8,128)(2,1)} %shared.3) | copy-start | bytes 3932164
  62.7 24.2 %collective-permute-start = (bf16[256,1280]{1,0:T(8,128)(2,1)S(1)}, bf16[256,1280]{1,0:T(8,128)(2,1)S(1)}, u32[]{:S(2)}, u32[]{:S(2)}) collective-permute-start(bf16[256,1280]{1,0:T(8,128)(2,1)S(1)} %pick.3.hb), channel_id=1, source_target_pairs={{0,1},{1,0},{2,3},{3,2},{4,5},{5,4},{6,7},{7,6},{8,9},{9,8},{10,11... | collective-permute-start | bytes 1966088 | tf_op jit(solution)/shard_map/ppermute | solution.py:561
  89.4 3.8 %collective-permute-start.2 = (bf16[14,128,128]{2,1,0:T(8,128)(2,1)S(1)}, bf16[14,128,128]{2,1,0:T(8,128)(2,1)S(1)}, u32[]{:S(2)}, u32[]{:S(2)}) collective-permute-start(bf16[14,128,128]{2,1,0:T(8,128)(2,1)S(1)} %get-tuple-element.31), channel_id=1, source_target_pairs={{0,2},{2,0},{4,6},{6,4},{8,10},{10,8},{12,14},{14,12},{16,18},{18,... | collective-permute-start | bytes 1376264 | tf_op jit(solution)/shard_map/ppermute | solution.py:29
  90.2 15.1 %collective-permute-start.11 = (bf16[5,2,128,128]{3,2,1,0:T(8,128)(2,1)S(1)}, bf16[5,2,128,128]{3,2,1,0:T(8,128)(2,1)S(1)}, u32[]{:S(2)}, u32[]{:S(2)}) collective-permute-start(bf16[5,2,128,128]{3,2,1,0:T(8,128)(2,1)S(1)} %get-tuple-element.36), channel_id=1, source_target_pairs={{0,18},{2,16},{4,22},{6,20},{8,26},{10,24},{12,30},{14,28},{16,2},... | collective-permute-start | bytes 983048 | tf_op jit(solution)/shard_map/ppermute | solution.py:29
  90.3 17.5 %collective-permute-start.10 = (bf16[5,2,128,128]{3,2,1,0:T(8,128)(2,1)S(1)}, bf16[5,2,128,128]{3,2,1,0:T(8,128)(2,1)S(1)}, u32[]{:S(2)}, u32[]{:S(2)}) collective-permute-start(bf16[5,2,128,128]{3,2,1,0:T(8,128)(2,1)S(1)} %get-tuple-element.30), channel_id=1, source_target_pairs={{0,16},{2,18},{4,20},{6,22},{8,24},{10,26},{12,28},{14,30},{16,0},... | collective-permute-start | bytes 983048 | tf_op jit(solution)/shard_map/ppermute | solution.py:29
  93.2 5.6 %collective-permute-start.3 = (bf16[1,2,2,2,128,128]{5,4,3,2,1,0:T(8,128)(2,1)S(1)}, bf16[1,2,2,2,128,128]{5,4,3,2,1,0:T(8,128)(2,1)S(1)}, u32[]{:S(2)}, u32[]{:S(2)}) collective-permute-start(bf16[1,2,2,2,128,128]{5,4,3,2,1,0:T(8,128)(2,1)S(1)} %maximum_bitcast_fusion.refs_2_.refs_0_), channel_id=1, source_target_pairs={{0,12},{2,98},{4,0},{6,102},{8,4},{10,106},{12,8},{14,110},{16,28}... | collective-permute-start | bytes 786440 | tf_op jit(solution)/shard_map/ppermute | solution.py:29
  94.1 9.5 %collective-permute-start.4 = (bf16[1,2,2,2,128,128]{5,4,3,2,1,0:T(8,128)(2,1)S(1)}, bf16[1,2,2,2,128,128]{5,4,3,2,1,0:T(8,128)(2,1)S(1)}, u32[]{:S(2)}, u32[]{:S(2)}) collective-permute-start(bf16[1,2,2,2,128,128]{5,4,3,2,1,0:T(8,128)(2,1)S(1)} %maximum_bitcast_fusion.refs_2_.refs_0_), channel_id=1, source_target_pairs={{0,4},{2,34},{4,8},{6,38},{8,12},{10,42},{12,0},{14,46},{16,20},{1... | collective-permute-start | bytes 786440 | tf_op jit(solution)/shard_map/ppermute | solution.py:29
  94.7 8.9 %collective-permute-start.5 = (bf16[1,2,2,2,128,128]{5,4,3,2,1,0:T(8,128)(2,1)S(1)}, bf16[1,2,2,2,128,128]{5,4,3,2,1,0:T(8,128)(2,1)S(1)}, u32[]{:S(2)}, u32[]{:S(2)}) collective-permute-start(bf16[1,2,2,2,128,128]{5,4,3,2,1,0:T(8,128)(2,1)S(1)} %maximum_bitcast_fusion.refs_2_.refs_0_), channel_id=1, source_target_pairs={{0,8},{2,66},{4,12},{6,70},{8,0},{10,74},{12,4},{14,78},{16,24},{1... | collective-permute-start | bytes 786440 | tf_op jit(solution)/shard_map/ppermute | solution.py:29
  103.7 14.0 %collective-permute-start.6 = (bf16[4,2,2,2,128,128]{5,4,3,2,1,0:T(8,128)(2,1)S(1)}, bf16[4,2,2,2,128,128]{5,4,3,2,1,0:T(8,128)(2,1)S(1)}, u32[]{:S(2)}, u32[]{:S(2)}) collective-permute-start(bf16[4,2,2,2,128,128]{5,4,3,2,1,0:T(8,128)(2,1)S(1)} %join.1.refs_2_), channel_id=1, source_target_pairs={{0,96},{2,14},{4,100},{6,2},{8,104},{10,6},{12,108},{14,10},{16,11... | collective-permute-start | bytes 3145736 | tf_op jit(solution)/shard_map/ppermute | solution.py:29
  103.7 15.3 %collective-permute-start.7 = (bf16[4,2,2,2,128,128]{5,4,3,2,1,0:T(8,128)(2,1)S(1)}, bf16[4,2,2,2,128,128]{5,4,3,2,1,0:T(8,128)(2,1)S(1)}, u32[]{:S(2)}, u32[]{:S(2)}) collective-permute-start(bf16[4,2,2,2,128,128]{5,4,3,2,1,0:T(8,128)(2,1)S(1)} %join.1.refs_2_), channel_id=1, source_target_pairs={{0,32},{2,6},{4,36},{6,10},{8,40},{10,14},{12,44},{14,2},{16,48},{... | collective-permute-start | bytes 3145736 | tf_op jit(solution)/shard_map/ppermute | solution.py:29
  117.7 10.3 %collective-permute-start.8 = (bf16[2,2,2,2,128,128]{5,4,3,2,1,0:T(8,128)(2,1)S(1)}, bf16[2,2,2,2,128,128]{5,4,3,2,1,0:T(8,128)(2,1)S(1)}, u32[]{:S(2)}, u32[]{:S(2)}) collective-permute-start(bf16[2,2,2,2,128,128]{5,4,3,2,1,0:T(8,128)(2,1)S(1)} %slice.25), channel_id=1, source_target_pairs={{0,96},{2,14},{4,100},{6,2},{8,104},{10,6},{12,108},{14,10},{16,11... | collective-permute-start | bytes 1572872 | tf_op jit(solution)/shard_map/ppermute | solution.py:29
  119.1 9.6 %collective-permute-start.9 = (bf16[2,2,2,2,128,128]{5,4,3,2,1,0:T(8,128)(2,1)S(1)}, bf16[2,2,2,2,128,128]{5,4,3,2,1,0:T(8,128)(2,1)S(1)}, u32[]{:S(2)}, u32[]{:S(2)}) collective-permute-start(bf16[2,2,2,2,128,128]{5,4,3,2,1,0:T(8,128)(2,1)S(1)} %slice.26), channel_id=1, source_target_pairs={{0,32},{2,6},{4,36},{6,10},{8,40},{10,14},{12,44},{14,2},{16,48},{... | collective-permute-start | bytes 1572872 | tf_op jit(solution)/shard_map/ppermute | solution.py:29
  133.6 22.3 %collective-permute-start.12 = (bf16[2,5,144,128]{3,2,1,0:T(8,128)(2,1)S(1)}, bf16[2,5,144,128]{3,2,1,0:T(8,128)(2,1)S(1)}, u32[]{:S(2)}, u32[]{:S(2)}) collective-permute-start(bf16[2,5,144,128]{3,2,1,0:T(8,128)(2,1)S(1)} %get-tuple-element.43.refs_12_), channel_id=1, source_target_pairs={{0,16},{2,18},{4,20},{6,22},{8,24},{10,26},{12,28},{14,30},{16,0},... | collective-permute-start | bytes 1105928 | tf_op jit(solution)/shard_map/ppermute | solution.py:29
  134.1 21.9 %collective-permute-start.13 = (bf16[2,5,144,128]{3,2,1,0:T(8,128)(2,1)S(1)}, bf16[2,5,144,128]{3,2,1,0:T(8,128)(2,1)S(1)}, u32[]{:S(2)}, u32[]{:S(2)}) collective-permute-start(bf16[2,5,144,128]{3,2,1,0:T(8,128)(2,1)S(1)} %get-tuple-element.47), channel_id=1, source_target_pairs={{0,18},{2,16},{4,22},{6,20},{8,26},{10,24},{12,30},{14,28},{16,2},... | collective-permute-start | bytes 1105928 | tf_op jit(solution)/shard_map/ppermute | solution.py:29
  156.1 1.8 %collective-permute-start.14 = (bf16[2,5,144,128]{3,2,1,0:T(8,128)(2,1)S(1)}, bf16[2,5,144,128]{3,2,1,0:T(8,128)(2,1)S(1)}, u32[]{:S(2)}, u32[]{:S(2)}) collective-permute-start(bf16[2,5,144,128]{3,2,1,0:T(8,128)(2,1)S(1)} %get-tuple-element.49), channel_id=1, source_target_pairs={{0,2},{2,0},{4,6},{6,4},{8,10},{10,8},{12,14},{14,12},{16,18},{18,... | collective-permute-start | bytes 1105928 | tf_op jit(solution)/shard_map/ppermute | solution.py:29

commit v4 on v3

--- a/solution.py
+++ b/solution.py
@@ -102,8 +102,7 @@
 
 
 def relayout_kernel(experts, out, loaded, ready, arrive, leave):
-    chunks, slots = loaded.shape[0], experts.shape[2]
-    group = loaded.shape[2]
+    chunks, group = loaded.shape[0], loaded.shape[2]
 
     def load(i):
         return pltpu.make_async_copy(experts.at[:, pl.ds(i * group, group)], loaded.at[i], arrive.at[i])
@@ -115,8 +114,7 @@
         load(i).start()
     for i in range(chunks):
         load(i).wait()
-        for expert in range(experts.shape[0]):
-            ready[i, :, expert * slots : (expert + 1) * slots, :] = loaded[i, expert]
+        ready[i] = jnp.concatenate([loaded[i, e] for e in range(experts.shape[0])], axis=1)
         store(i).start()
     for i in range(chunks):
         store(i).wait()
@@ -176,6 +174,7 @@
     width = width // 2
     chunks = 2
     tile = pltpu.VMEM((chunks, rows // chunks, width), jnp.bfloat16)
+    residual, shared = (pltpu.with_memory_space_constraint(a, pltpu.HBM) for a in (residual, shared))
     return pl.pallas_call(
         functools.partial(pick_kernel, part * width),
         in_specs=[vmem()] * 3 + [hbm()] * 2 + [anywhere()],
@@ -235,7 +234,7 @@
         start += values.shape[1]
 
 
-def last_kernel(where, h, gain, wk, wv, wq, old, old_squares, cos, sin, kv_mine, q_mine, q_other, other):
+def last_kernel(where, h, gain, wk, wv, wq, old, old_squares, cos, sin, kv_mine, q_mine, other):
     total = old_squares[...] + squared(h[...])
     factor = lax.rsqrt(total / (4 * h.shape[1]) + NORM_EPS)
     part_in = 3 - 2 * where[0]
@@ -267,7 +266,6 @@
             other[i] = others[0][i]
         for i in range(Q_TILES):
             q_mine[i // 2, i % 2] = mine[1][i]
-            q_other[i // 2, i % 2] = others[1][i]
             other[KV_TILES + i] = others[1][i]
 
     pl.when(where[1] == 0)(lambda: write(*groups))
@@ -299,7 +297,7 @@
 
 def project_last(where, h, gain, weights, partial, cos, sin):
     q = (GROUP, 2, HD, HALF)
-    shapes = [(2, 2, HALF, HD), q, q, (KV_TILES + Q_TILES, HALF, HD)]
+    shapes = [(2, 2, HALF, HD), q, (KV_TILES + Q_TILES, HALF, HD)]
     outs = [(shape, jnp.bfloat16) for shape in shapes]
     return project(last_kernel, where, (h, gain, *weights, *partial, cos, sin), outs, 2, "project_last")
 
@@ -499,9 +497,8 @@
 
 def merge_kernel(core, own, own_pair, sibling, sibling_pair, out):
     def level(part, side, head):
-        return part[side, head, HD : HD + 8].astype(jnp.float32)[:1] + part[
-            side, head, HD + 8 :
-        ].astype(jnp.float32)[:1]
+        terms = part[side, head, HD:].astype(jnp.float32)
+        return terms[:1] + terms[8:9]
 
     for group, (one, two) in ((core[0], (own, own_pair)), (1 - core[0], (sibling, sibling_pair))):
         for side in range(2):
@@ -528,6 +525,25 @@
     )(core, own, own_pair, sibling, sibling_pair)
 
 
+def cut_kernel(ahead, behind, after, first, second):
+    half = first.shape[0]
+    first[...] = ahead[:half]
+    second[...] = behind[half:]
+
+
+def cut(ahead, behind, after):
+    shape = (ahead.shape[0] // 2,) + ahead.shape[1:]
+    return pl.pallas_call(
+        cut_kernel,
+        in_specs=[vmem()] * 2 + [anywhere()],
+        out_specs=[vmem()] * 2,
+        out_shape=[jax.ShapeDtypeStruct(shape, ahead.dtype)] * 2,
+        compiler_params=params(8),
+        cost_estimate=takes(0.3),
+        name="cut",
+    )(ahead, behind, after)
+
+
 def rotations(ctx_index, rows):
     row = jnp.arange(rows, dtype=jnp.int32)
     half = rows // 2
@@ -564,19 +580,16 @@
     weights = (w_key, w_value, w_query)
     partial = project_own(where, ha, hb, gain, weights)
     partial = project_more(where, other_a, gain, weights, partial)
-    kv_mine, q_mine, q_other, to_other = project_last(where, other_b, gain, weights, partial, cos, sin)
+    kv_mine, q_mine, to_other = project_last(where, other_b, gain, weights, partial, cos, sin)
 
     from_other = core_swap(to_other)
     block = jnp.stack([kv_mine, from_other[:KV_TILES].reshape(kv_mine.shape)])[None]
     q_own = jnp.stack([q_mine, from_other[KV_TILES:].reshape(q_mine.shape)])
-    q_pair = jnp.stack([to_pair(q_mine), to_pair_other(q_other)])
+    q_pair = to_pair(q_own)
 
     near = [first_axis(block, step) for step in (1, -1, 2)]
     own_state = attend(k.reshape(1), q_own, [block], None, diag=True, time=30)
     line = join([block] + near, own_state[2])
-    ahead, behind = second_axis(line, 1), second_axis(line, -1)
-    far = [ahead, behind, second_axis(ahead[:2], 1), second_axis(behind[2:], -1)]
-
     steps = jnp.array([0, 1, -1, 2], jnp.int32)
 
     def before(first, second, chip):
@@ -589,11 +602,15 @@
         jnp.concatenate([before(steps, zero + step, chip_order(y, at, x)) for step in (0, 1, -1, 2)])
         for at in (z, 1 - z)
     )
-    pair_state = attend(pair_flags[:4], q_pair, [line], None, time=7)
-    pair_state = attend(pair_flags[4:12], q_pair, far[:2], pair_state)
-    pair_same, pair_other = attend(pair_flags[12:], q_pair, far[2:], pair_state, finish=True)
+    ahead, behind = second_axis(line, 1), second_axis(line, -1)
+    own_state = attend(own_flags[1:4], q_own, near, own_state, after=(line,))
+    pair_state = attend(pair_flags[:4], q_pair, [line], None, after=(own_state[2],), time=7)
+    far_ahead, far_behind = cut(ahead, behind, pair_state[2])
+    farther = [second_axis(far_ahead, 1), second_axis(far_behind, -1)]
+    pair_state = attend(pair_flags[4:12], q_pair, [ahead, behind], pair_state, after=(far_ahead,))
+    pair_same, pair_other = attend(pair_flags[12:], q_pair, farther, pair_state, finish=True)
     own_pair, sibling_pair = to_pair(pair_same), to_pair_other(pair_other)
-    own_state = attend(own_flags[1:], q_own, near + far, own_state, after=(pair_same,))
+    own_state = attend(own_flags[4:], q_own, [ahead, behind] + farther, own_state, after=(pair_same,))
     own_same, own_other = divide(own_state, (own_pair, sibling_pair))
     attended = merge(k.reshape(1), own_same, own_pair, core_swap(own_other), sibling_pair)
     return hidden, attended

time: 159 us -> 155 us (0.975)
  local copies, waits for them, and re-layouts: 7.26 us -> 1.03 us
  Pallas kernels: 50.6 us -> 53.7 us
    unnamed x24 -> x16, local copies, waits for them, and re-layouts: 7.14 us -> 0.99 us
    pallas_call x2, Pallas kernels: 2.72 us -> 4.89 us  [pick(): pl.pallas_call(functools.partial(pick_kernel, part * width), in_specs=[vm...]
    ppermute x13 -> x12, waiting for transfers between devices: 14.6 us -> 12.6 us  [permute(): return lax.ppermute(value, 'ctx', pairs)]
    ppermute x2, waiting for transfers between devices: 18.3 us -> 20.3 us  [shards(): lax.ppermute(h, 'tp', [(0, 1), (1, 0)])]
    ppermute x13 -> x12, starting transfers between devices: 16 us -> 15.1 us  [permute(): return lax.ppermute(value, 'ctx', pairs)]
    pallas_call x5 -> x6, Pallas kernels: 35.9 us -> 36.5 us  [attend(): pl.pallas_call(functools.partial(attend_kernel, counts, diag, state is no...]
  transfers between devices with their start and end apart: 16 -> 15, of which waited for: 9 -> 10; matrix products, arithmetic and copies ran while one was open for 2% -> 2% of each run, Pallas kernels for 24% -> 26%
where the time goes in v4:
time: 155 us
  waiting for transfers between devices  67.7 us (44%)
  Pallas kernels  53.7 us (35%)
  starting transfers between devices  29.2 us (19%)
  other arithmetic  2.27 us (1%)
    pallas_call x6, Pallas kernels, attend(): pl.pallas_call(functools.partial(attend_kernel, counts, diag, state is no...  36.5 us
    all_to_all x1, waiting for transfers between devices, shards(): lax.all_to_all(relayout(expert_out), 'ctx', split_axis=0, concat_axis=0,...  34.9 us
    ppermute x2, waiting for transfers between devices, shards(): lax.ppermute(h, 'tp', [(0, 1), (1, 0)])  20.3 us
    ppermute x12, starting transfers between devices, permute(): return lax.ppermute(value, 'ctx', pairs)  15.1 us
    ppermute x12, waiting for transfers between devices, permute(): return lax.ppermute(value, 'ctx', pairs)  12.6 us
    all_to_all x1, starting transfers between devices, shards(): lax.all_to_all(relayout(expert_out), 'ctx', split_axis=0, concat_axis=0,...  12.4 us
    pallas_call x3, Pallas kernels, project(): pl.pallas_call(kernel, in_specs=[smem()] + [vmem()] * len(ins), out_specs...  7.8 us
    pallas_call x2, Pallas kernels, pick(): pl.pallas_call(functools.partial(pick_kernel, part * width), in_specs=[vm...  4.89 us
  transfers between devices with their start and end apart: 15, of which 10 were waited for; matrix products, arithmetic and copies ran while one was open for 2% of the time, Pallas kernels for 26%

profile of v4, /device:TPU:1, one launch (start us, length us, event | category | flops | bytes accessed | tf_op | source)
XLA Modules:
  0.0 154.9 jit_solution(17056692248636462624)
XLA Ops:
  0.6 2.7 %relayout.1 = bf16[64,8,2560]{2,1,0:T(8,128)(2,1)} custom-call(bf16[2,64,4,2560]{3,2,1,0:T(4,128)(2,1)} %experts.1), custom_call_target="tpu_custom_call" | custom-call | tf_op jit(solution)/shard_map/relayout/pallas_call | solution.py:127
  3.4 12.4 %all-to-all-start = ((bf16[64,8,2560]{2,1,0:T(8,128)(2,1)}), bf16[64,8,2560]{2,1,0:T(8,128)(2,1)S(1)}, u32[]{:S(2)}, u32[]{:S(2)}) async-start(bf16[64,8,2560]{2,1,0:T(8,128)(2,1)} %relayout.1), calls=%async_computation | async-start | bytes 5242880 | tf_op jit(solution)/shard_map/all_to_all | solution.py:570
  16.0 0.1 copy.16.gate
  16.1 0.1 copy.15.ids_col
  16.3 0.3 choose.1.hot.after
  16.5 0.1 pad_add_fusion.where
  16.6 0.1 add_convert_fusion.1.refs_0_
  16.7 0.5 fusion
  17.3 0.1 pad_maximum_fusion.2
  17.4 34.9 %all-to-all-done = bf16[64,8,2560]{2,1,0:T(8,128)(2,1)S(1)} async-done(((bf16[64,8,2560]{2,1,0:T(8,128)(2,1)}), bf16[64,8,2560]{2,1,0:T(8,128)(2,1)S(1)}, u32[]{:S(2)}, u32[]{:S(2)}) %all-to-all-start) | async-done | bytes 2621472 | tf_op jit(solution)/shard_map/all_to_all | solution.py:570
  52.3 2.1 %pick.2.after.ha = bf16[256,1280]{1,0:T(8,128)(2,1)S(1)} custom-call(bf16[256,512]{1,0:T(8,128)(2,1)S(1)} %choose.1.hot.after, f32[256,1]{1,0:T(8,128)S(1)} %copy.16.gate, bf16[512,2560]{1,0:T(8,128)(2,1)S(1)} %bitcast.10, bf16[256,2560]{1,0:T(8,128)(2,1)} %residual.3, bf16[256,2560]{1,0:T(8,128)(2,1)} %shared.3, bf16[256,512]{1,0:T(8,128)(2,1)S(1)} %choose.1.hot.after), custom_call_target="tpu_custom_call" | custom-call | flops 2875000064 | tf_op jit(solution)/shard_map/pick/pallas_call | solution.py:178
  54.5 0.8 collective-permute-start.1
  55.3 2.8 %pick.3.hb = bf16[256,1280]{1,0:T(8,128)(2,1)S(1)} custom-call(bf16[256,512]{1,0:T(8,128)(2,1)S(1)} %choose.1.hot.after, f32[256,1]{1,0:T(8,128)S(1)} %copy.16.gate, bf16[512,2560]{1,0:T(8,128)(2,1)S(1)} %bitcast.11, bf16[256,2560]{1,0:T(8,128)(2,1)} %residual.3, bf16[256,2560]{1,0:T(8,128)(2,1)} %shared.3, bf16[256,1280]{1,0:T(8,128)(2,1)S(1)} %pick.2.after.ha), custom_call_target="tpu_custom_call" | custom-call | flops 2875000064 | tf_op jit(solution)/shard_map/pick/pallas_call | solution.py:178
  58.1 0.8 collective-permute-start
  58.9 0.7 copy-done.2
  59.6 3.2 %project_own.1 = (f32[256,1792]{1,0:T(8,128)S(1)}, f32[256,1]{1,0:T(8,128)S(1)}) custom-call(s32[2]{0:T(128)S(1)} %pad_add_fusion.where, bf16[256,1280]{1,0:T(8,128)(2,1)S(1)} %pick.2.after.ha, bf16[256,1280]{1,0:T(8,128)(2,1)S(1)} %pick.3.hb, bf16[4,1,1280]{2,1,0:T(2,128)(2,1)S(1)} %reshape.38.gain, bf16[5120,256]{1,0:T(8,128)(2,1)S(1)} %copy-done.1, ...), custom_call_target="tpu_custom_call" | custom-call | flops 5750000128 | tf_op jit(solution)/shard_map/project_own/pallas_call | solution.py:276
  62.8 8.2 %collective-permute-done.1.h = bf16[256,1280]{1,0:T(8,128)(2,1)S(1)} collective-permute-done((bf16[256,1280]{1,0:T(8,128)(2,1)S(1)}, bf16[256,1280]{1,0:T(8,128)(2,1)S(1)}, u32[]{:S(2)}, u32[]{:S(2)}) %collective-permute-start.1) | collective-permute-done | bytes 655392 | tf_op jit(solution)/shard_map/ppermute | solution.py:577
  71.0 2.0 %project_more.1 = (f32[256,1792]{1,0:T(8,128)S(1)}, f32[256,1]{1,0:T(8,128)S(1)}) custom-call(s32[2]{0:T(128)S(1)} %pad_add_fusion.where, bf16[256,1280]{1,0:T(8,128)(2,1)S(1)} %collective-permute-done.1.h, bf16[4,1,1280]{2,1,0:T(2,128)(2,1)S(1)} %reshape.38.gain, bf16[5120,256]{1,0:T(8,128)(2,1)S(1)} %copy-done.1, bf16[5120,256]{1,0:T(8,128)(2,1)S(1)} %copy-done.2, ...), custom_call_target="tpu_custom_call" | custom-call | flops 2300000000 | tf_op jit(solution)/shard_map/project_more/pallas_call | solution.py:276
  73.0 12.1 %collective-permute-done.h = bf16[256,1280]{1,0:T(8,128)(2,1)S(1)} collective-permute-done((bf16[256,1280]{1,0:T(8,128)(2,1)S(1)}, bf16[256,1280]{1,0:T(8,128)(2,1)S(1)}, u32[]{:S(2)}, u32[]{:S(2)}) %collective-permute-start) | collective-permute-done | bytes 655392 | tf_op jit(solution)/shard_map/ppermute | solution.py:577
  85.1 2.6 %project_last.1 = (bf16[2,2,128,128]{3,2,1,0:T(8,128)(2,1)S(1)}, bf16[5,2,128,128]{3,2,1,0:T(8,128)(2,1)S(1)}, bf16[14,128,128]{2,1,0:T(8,128)(2,1)S(1)}) custom-call(s32[2]{0:T(128)S(1)} %pad_add_fusion.where, bf16[256,1280]{1,0:T(8,128)(2,1)S(1)} %collective-permute-done.h, bf16[4,1,1280]{2,1,0:T(2,128)(2,1)S(1)} %reshape.38.gain, ...), custom_call_target="tpu_custom_call" | custom-call | flops 2300000000 | tf_op jit(solution)/shard_map/project_last/pallas_call | solution.py:276
  87.7 0.8 collective-permute-start.2
  88.5 0.1 add_convert_fusion.refs_0_
  88.6 1.3 collective-permute-done.2
  90.0 0.2 collective-permute-start.5
  90.1 1.3 collective-permute-start.4
  91.4 1.4 collective-permute-start.3
  92.9 0.6 collective-permute-start.8
  93.5 2.0 %attend.6 = (f32[2,5,128,256]{3,2,1,0:T(8,128)S(1)}, f32[2,5,8,256]{3,2,1,0:T(8,128)S(1)}, f32[2,5,8,256]{3,2,1,0:T(8,128)S(1)}) custom-call(s32[1]{0:T(128)} %bitcast.2.refs_0_.core, bf16[2,5,2,128,128]{4,3,2,1,0:T(8,128)(2,1)S(1)} %pad_maximum_fusion.1.refs_1_, bf16[1,2,2,2,128,128]{5,4,3,2,1,0:T(8,128)(2,1)S(1)} %maximum_bitcast_fusion.refs_2_.refs_0_), custom_call_target="tpu_custom_call" | custom-call | flops 34500001792 | tf_op jit(solution)/shard_map/attend/pallas_call | solution.py:451
  95.5 1.6 %collective-permute-done.5.refs_3_.refs_4_ = bf16[1,2,2,2,128,128]{5,4,3,2,1,0:T(8,128)(2,1)S(1)} collective-permute-done((bf16[1,2,2,2,128,128]{5,4,3,2,1,0:T(8,128)(2,1)S(1)}, bf16[1,2,2,2,128,128]{5,4,3,2,1,0:T(8,128)(2,1)S(1)}, u32[]{:S(2)}, u32[]{:S(2)}) %collective-permute-start.5) | collective-permute-done | bytes 262176 | tf_op jit(solution)/shard_map/ppermute | solution.py:29
  97.1 2.6 %collective-permute-done.4.refs_2_.refs_3_ = bf16[1,2,2,2,128,128]{5,4,3,2,1,0:T(8,128)(2,1)S(1)} collective-permute-done((bf16[1,2,2,2,128,128]{5,4,3,2,1,0:T(8,128)(2,1)S(1)}, bf16[1,2,2,2,128,128]{5,4,3,2,1,0:T(8,128)(2,1)S(1)}, u32[]{:S(2)}, u32[]{:S(2)}) %collective-permute-start.4) | collective-permute-done | bytes 262176 | tf_op jit(solution)/shard_map/ppermute | solution.py:29
  99.8 0.1 collective-permute-start.7
  99.8 2.7 %collective-permute-start.6 = (bf16[4,2,2,2,128,128]{5,4,3,2,1,0:T(8,128)(2,1)S(1)}, bf16[4,2,2,2,128,128]{5,4,3,2,1,0:T(8,128)(2,1)S(1)}, u32[]{:S(2)}, u32[]{:S(2)}) collective-permute-start(bf16[4,2,2,2,128,128]{5,4,3,2,1,0:T(8,128)(2,1)S(1)} %join.1.refs_8_.refs_2_), channel_id=1, source_target_pairs={{0,96},{2,14},{4,100},{6,2},{8,104},{10,6},{12,108},{14,10},{16,11... | collective-permute-start | bytes 3145736 | tf_op jit(solution)/shard_map/ppermute | solution.py:29
  102.5 3.6 %attend.7 = (f32[2,5,128,256]{3,2,1,0:T(8,128)S(1)}, f32[2,5,8,256]{3,2,1,0:T(8,128)S(1)}, f32[2,5,8,256]{3,2,1,0:T(8,128)S(1)}) custom-call(s32[3]{0:T(128)S(1)} %slice_convert_fusion.refs_0_, bf16[2,5,2,128,128]{4,3,2,1,0:T(8,128)(2,1)S(1)} %pad_maximum_fusion.1.refs_1_, bf16[1,2,2,2,128,128]{5,4,3,2,1,0:T(8,128)(2,1)S(1)} %collective-permute-done.3.refs_1_.refs_2_, ...), custom_call_target="tpu_custom_call" | custom-call | flops 3967500032 | tf_op jit(solution)/shard_map/attend/pallas_call | solution.py:451
  106.1 3.9 %collective-permute-done.8.refs_1_ = bf16[2,5,2,128,128]{4,3,2,1,0:T(8,128)(2,1)S(1)} collective-permute-done((bf16[2,5,2,128,128]{4,3,2,1,0:T(8,128)(2,1)S(1)}, bf16[2,5,2,128,128]{4,3,2,1,0:T(8,128)(2,1)S(1)}, u32[]{:S(2)}, u32[]{:S(2)}) %collective-permute-start.8) | collective-permute-done | bytes 655392 | tf_op jit(solution)/shard_map/ppermute | solution.py:29
  110.0 4.9 %attend.8 = (f32[2,5,128,256]{3,2,1,0:T(8,128)S(1)}, f32[2,5,8,256]{3,2,1,0:T(8,128)S(1)}, f32[2,5,8,256]{3,2,1,0:T(8,128)S(1)}) custom-call(s32[4]{0:T(128)S(1)} %compare_convert_fusion.1.refs_0_, bf16[2,5,2,128,128]{4,3,2,1,0:T(8,128)(2,1)S(1)} %collective-permute-done.8.refs_1_, bf16[4,2,2,2,128,128]{5,4,3,2,1,0:T(8,128)(2,1)S(1)} %join.1.refs_8_.refs_2_, ...), custom_call_target="tpu_custom_call" | custom-call | flops 8049999872 | tf_op jit(solution)/shard_map/attend/pallas_call | solution.py:451
  114.9 0.1 collective-permute-done.7.behind.refs_3_
  115.1 2.7 %collective-permute-start.9 = (bf16[2,2,2,2,128,128]{5,4,3,2,1,0:T(8,128)(2,1)S(1)}, bf16[2,2,2,2,128,128]{5,4,3,2,1,0:T(8,128)(2,1)S(1)}, u32[]{:S(2)}, u32[]{:S(2)}) collective-permute-start(bf16[2,2,2,2,128,128]{5,4,3,2,1,0:T(8,128)(2,1)S(1)} %get-tuple-element.42.refs_7_), channel_id=1, source_target_pairs={{0,96},{2,14},{4,100},{6,2},{8,104},{10,6},{12,108},{14,10},{16,11... | collective-permute-start | bytes 1572872 | tf_op jit(solution)/shard_map/ppermute | solution.py:29
  117.8 8.6 %attend.9 = (f32[2,5,128,256]{3,2,1,0:T(8,128)S(1)}, f32[2,5,8,256]{3,2,1,0:T(8,128)S(1)}, f32[2,5,8,256]{3,2,1,0:T(8,128)S(1)}) custom-call(s32[8]{0:T(128)S(1)} %add_convert_fusion.1.refs_0_, bf16[2,5,2,128,128]{4,3,2,1,0:T(8,128)(2,1)S(1)} %collective-permute-done.8.refs_1_, bf16[4,2,2,2,128,128]{5,4,3,2,1,0:T(8,128)(2,1)S(1)} %collective-permute-done.6.ahead.refs_2_, ...), custom_call_target="tpu_custom_call" | custom-call | flops 10579999744 | tf_op jit(solution)/shard_map/attend/pallas_call | solution.py:451
  126.4 5.0 %attend.10 = (bf16[2,5,144,128]{3,2,1,0:T(8,128)(2,1)S(1)}, bf16[2,5,144,128]{3,2,1,0:T(8,128)(2,1)S(1)}) custom-call(s32[4]{0:T(128)S(1)} %get-tuple-element.69.refs_0_, bf16[2,5,2,128,128]{4,3,2,1,0:T(8,128)(2,1)S(1)} %collective-permute-done.8.refs_1_, bf16[2,2,2,2,128,128]{5,4,3,2,1,0:T(8,128)(2,1)S(1)} %collective-permute-done.9.refs_2_.refs_4_, ...), custom_call_target="tpu_custom_call" | custom-call | flops 5289999872 | tf_op jit(solution)/shard_map/attend/pallas_call | solution.py:451
  131.4 2.6 %collective-permute-start.12 = (bf16[2,5,144,128]{3,2,1,0:T(8,128)(2,1)S(1)}, bf16[2,5,144,128]{3,2,1,0:T(8,128)(2,1)S(1)}, u32[]{:S(2)}, u32[]{:S(2)}) collective-permute-start(bf16[2,5,144,128]{3,2,1,0:T(8,128)(2,1)S(1)} %get-tuple-element.55), channel_id=1, source_target_pairs={{0,18},{2,16},{4,22},{6,20},{8,26},{10,24},{12,30},{14,28},{16,2},... | collective-permute-start | bytes 1105928 | tf_op jit(solution)/shard_map/ppermute | solution.py:29
  134.0 2.7 %collective-permute-start.11 = (bf16[2,5,144,128]{3,2,1,0:T(8,128)(2,1)S(1)}, bf16[2,5,144,128]{3,2,1,0:T(8,128)(2,1)S(1)}, u32[]{:S(2)}, u32[]{:S(2)}) collective-permute-start(bf16[2,5,144,128]{3,2,1,0:T(8,128)(2,1)S(1)} %get-tuple-element.51.refs_9_), channel_id=1, source_target_pairs={{0,16},{2,18},{4,20},{6,22},{8,24},{10,26},{12,28},{14,30},{16,0},... | collective-permute-start | bytes 1105928 | tf_op jit(solution)/shard_map/ppermute | solution.py:29
  136.7 12.4 %attend.11 = (f32[2,5,128,256]{3,2,1,0:T(8,128)S(1)}, f32[2,5,8,256]{3,2,1,0:T(8,128)S(1)}, f32[2,5,8,256]{3,2,1,0:T(8,128)S(1)}) custom-call(s32[12]{0:T(128)S(1)} %add_convert_fusion.refs_0_, bf16[2,5,2,128,128]{4,3,2,1,0:T(8,128)(2,1)S(1)} %pad_maximum_fusion.1.refs_1_, bf16[4,2,2,2,128,128]{5,4,3,2,1,0:T(8,128)(2,1)S(1)} %collective-permute-done.6.ahead.refs_2_, ...), custom_call_target="tpu_custom_call" | custom-call | flops 15870000128 | tf_op jit(solution)/shard_map/attend/pallas_call | solution.py:451
  149.2 2.6 %collective-permute-done.11.refs_3_.own_pair = bf16[2,5,144,128]{3,2,1,0:T(8,128)(2,1)S(1)} collective-permute-done((bf16[2,5,144,128]{3,2,1,0:T(8,128)(2,1)S(1)}, bf16[2,5,144,128]{3,2,1,0:T(8,128)(2,1)S(1)}, u32[]{:S(2)}, u32[]{:S(2)}) %collective-permute-start.11) | collective-permute-done | bytes 368672 | tf_op jit(solution)/shard_map/ppermute | solution.py:29
  151.7 0.1 divide.1
  151.9 0.1 collective-permute-start.13
  152.0 1.1 pad_maximum_fusion
  153.1 0.5 collective-permute-done.13.sibling
  153.6 1.3 merge.1
  (33 shorter events, 0.5 us)
Async XLA Ops:
  3.3 12.6 %copy-start.4 = (bf16[5120]{0:T(1024)(128)(2,1)S(1)}, bf16[5120]{0:T(1024)(128)(2,1)}, u32[]{:S(2)}) copy-start(bf16[5120]{0:T(1024)(128)(2,1)} %param.15) | copy-start | bytes 30724
  3.4 12.6 %copy-start.5 = (f32[256,1]{0,1:T(1,128)S(1)}, f32[256,1]{0,1:T(1,128)}, u32[]{:S(2)}) copy-start(f32[256,1]{0,1:T(1,128)} %param.14) | copy-start | bytes 3076
  3.4 12.7 %copy-start.3 = (s32[256,1]{0,1:T(1,128)S(1)}, s32[256,1]{0,1:T(1,128)}, u32[]{:S(2)}) copy-start(s32[256,1]{0,1:T(1,128)} %param.13) | copy-start | bytes 3076
  3.4 13.2 %copy-start.6 = (s32[4]{0:T(128)S(1)}, s32[4]{0:T(128)}, u32[]{:S(2)}) copy-start(s32[4]{0:T(128)} %constant.156.clone) | copy-start | bytes 52
  3.4 48.9 %all-to-all-start = ((bf16[64,8,2560]{2,1,0:T(8,128)(2,1)}), bf16[64,8,2560]{2,1,0:T(8,128)(2,1)S(1)}, u32[]{:S(2)}, u32[]{:S(2)}) async-start(bf16[64,8,2560]{2,1,0:T(8,128)(2,1)} %relayout.1), calls=%async_computation | async-start | bytes 5242880 | tf_op jit(solution)/shard_map/all_to_all | solution.py:570
  52.3 6.6 %copy-start = (bf16[5120,1280]{1,0:T(8,128)(2,1)S(1)}, bf16[5120,1280]{1,0:T(8,128)(2,1)}, u32[]{:S(2)}) copy-start(bf16[5120,1280]{1,0:T(8,128)(2,1)} %wq.5) | copy-start | bytes 39321604
  54.5 4.4 %copy-start.1 = (bf16[5120,256]{1,0:T(8,128)(2,1)S(1)}, bf16[5120,256]{1,0:T(8,128)(2,1)}, u32[]{:S(2)}) copy-start(bf16[5120,256]{1,0:T(8,128)(2,1)} %wk.5) | copy-start | bytes 7864324
  54.5 5.1 %copy-start.2 = (bf16[5120,256]{1,0:T(8,128)(2,1)S(1)}, bf16[5120,256]{1,0:T(8,128)(2,1)}, u32[]{:S(2)}) copy-start(bf16[5120,256]{1,0:T(8,128)(2,1)} %wv.5) | copy-start | bytes 7864324
  54.5 16.5 %collective-permute-start.1 = (bf16[256,1280]{1,0:T(8,128)(2,1)S(1)}, bf16[256,1280]{1,0:T(8,128)(2,1)S(1)}, u32[]{:S(2)}, u32[]{:S(2)}) collective-permute-start(bf16[256,1280]{1,0:T(8,128)(2,1)S(1)} %pick.2.after.ha), channel_id=1, source_target_pairs={{0,1},{1,0},{2,3},{3,2},{4,5},{5,4},{6,7},{7,6},{8,9},{9,8},{10,11... | collective-permute-start | bytes 1966088 | tf_op jit(solution)/shard_map/ppermute | solution.py:577
  58.1 27.0 %collective-permute-start = (bf16[256,1280]{1,0:T(8,128)(2,1)S(1)}, bf16[256,1280]{1,0:T(8,128)(2,1)S(1)}, u32[]{:S(2)}, u32[]{:S(2)}) collective-permute-start(bf16[256,1280]{1,0:T(8,128)(2,1)S(1)} %pick.3.hb), channel_id=1, source_target_pairs={{0,1},{1,0},{2,3},{3,2},{4,5},{5,4},{6,7},{7,6},{8,9},{9,8},{10,11... | collective-permute-start | bytes 1966088 | tf_op jit(solution)/shard_map/ppermute | solution.py:577
  87.7 2.2 %collective-permute-start.2 = (bf16[14,128,128]{2,1,0:T(8,128)(2,1)S(1)}, bf16[14,128,128]{2,1,0:T(8,128)(2,1)S(1)}, u32[]{:S(2)}, u32[]{:S(2)}) collective-permute-start(bf16[14,128,128]{2,1,0:T(8,128)(2,1)S(1)} %get-tuple-element.35), channel_id=1, source_target_pairs={{0,2},{2,0},{4,6},{6,4},{8,10},{10,8},{12,14},{14,12},{16,18},{18,... | collective-permute-start | bytes 1376264 | tf_op jit(solution)/shard_map/ppermute | solution.py:29
  90.0 7.1 %collective-permute-start.5 = (bf16[1,2,2,2,128,128]{5,4,3,2,1,0:T(8,128)(2,1)S(1)}, bf16[1,2,2,2,128,128]{5,4,3,2,1,0:T(8,128)(2,1)S(1)}, u32[]{:S(2)}, u32[]{:S(2)}) collective-permute-start(bf16[1,2,2,2,128,128]{5,4,3,2,1,0:T(8,128)(2,1)S(1)} %maximum_bitcast_fusion.refs_2_.refs_0_), channel_id=1, source_target_pairs={{0,8},{2,66},{4,12},{6,70},{8,0},{10,74},{12,4},{14,78},{16,24},{1... | collective-permute-start | bytes 786440 | tf_op jit(solution)/shard_map/ppermute | solution.py:29
  90.1 9.6 %collective-permute-start.4 = (bf16[1,2,2,2,128,128]{5,4,3,2,1,0:T(8,128)(2,1)S(1)}, bf16[1,2,2,2,128,128]{5,4,3,2,1,0:T(8,128)(2,1)S(1)}, u32[]{:S(2)}, u32[]{:S(2)}) collective-permute-start(bf16[1,2,2,2,128,128]{5,4,3,2,1,0:T(8,128)(2,1)S(1)} %maximum_bitcast_fusion.refs_2_.refs_0_), channel_id=1, source_target_pairs={{0,4},{2,34},{4,8},{6,38},{8,12},{10,42},{12,0},{14,46},{16,20},{1... | collective-permute-start | bytes 786440 | tf_op jit(solution)/shard_map/ppermute | solution.py:29
  91.4 8.3 %collective-permute-start.3 = (bf16[1,2,2,2,128,128]{5,4,3,2,1,0:T(8,128)(2,1)S(1)}, bf16[1,2,2,2,128,128]{5,4,3,2,1,0:T(8,128)(2,1)S(1)}, u32[]{:S(2)}, u32[]{:S(2)}) collective-permute-start(bf16[1,2,2,2,128,128]{5,4,3,2,1,0:T(8,128)(2,1)S(1)} %maximum_bitcast_fusion.refs_2_.refs_0_), channel_id=1, source_target_pairs={{0,12},{2,98},{4,0},{6,102},{8,4},{10,106},{12,8},{14,110},{16,28}... | collective-permute-start | bytes 786440 | tf_op jit(solution)/shard_map/ppermute | solution.py:29
  92.9 17.1 %collective-permute-start.8 = (bf16[2,5,2,128,128]{4,3,2,1,0:T(8,128)(2,1)S(1)}, bf16[2,5,2,128,128]{4,3,2,1,0:T(8,128)(2,1)S(1)}, u32[]{:S(2)}, u32[]{:S(2)}) collective-permute-start(bf16[2,5,2,128,128]{4,3,2,1,0:T(8,128)(2,1)S(1)} %pad_maximum_fusion.1.refs_1_), channel_id=1, source_target_pairs={{0,16},{2,18},{4,20},{6,22},{8,24},{10,26},{12,28},{14,30},{16,0},... | collective-permute-start | bytes 1966088 | tf_op jit(solution)/shard_map/ppermute | solution.py:29
  99.8 15.2 %collective-permute-start.7 = (bf16[4,2,2,2,128,128]{5,4,3,2,1,0:T(8,128)(2,1)S(1)}, bf16[4,2,2,2,128,128]{5,4,3,2,1,0:T(8,128)(2,1)S(1)}, u32[]{:S(2)}, u32[]{:S(2)}) collective-permute-start(bf16[4,2,2,2,128,128]{5,4,3,2,1,0:T(8,128)(2,1)S(1)} %join.1.refs_8_.refs_2_), channel_id=1, source_target_pairs={{0,32},{2,6},{4,36},{6,10},{8,40},{10,14},{12,44},{14,2},{16,48},{... | collective-permute-start | bytes 3145736 | tf_op jit(solution)/shard_map/ppermute | solution.py:29
  99.8 15.1 %collective-permute-start.6 = (bf16[4,2,2,2,128,128]{5,4,3,2,1,0:T(8,128)(2,1)S(1)}, bf16[4,2,2,2,128,128]{5,4,3,2,1,0:T(8,128)(2,1)S(1)}, u32[]{:S(2)}, u32[]{:S(2)}) collective-permute-start(bf16[4,2,2,2,128,128]{5,4,3,2,1,0:T(8,128)(2,1)S(1)} %join.1.refs_8_.refs_2_), channel_id=1, source_target_pairs={{0,96},{2,14},{4,100},{6,2},{8,104},{10,6},{12,108},{14,10},{16,11... | collective-permute-start | bytes 3145736 | tf_op jit(solution)/shard_map/ppermute | solution.py:29
  115.1 11.3 %collective-permute-start.10 = (bf16[2,2,2,2,128,128]{5,4,3,2,1,0:T(8,128)(2,1)S(1)}, bf16[2,2,2,2,128,128]{5,4,3,2,1,0:T(8,128)(2,1)S(1)}, u32[]{:S(2)}, u32[]{:S(2)}) collective-permute-start(bf16[2,2,2,2,128,128]{5,4,3,2,1,0:T(8,128)(2,1)S(1)} %get-tuple-element.43), channel_id=1, source_target_pairs={{0,32},{2,6},{4,36},{6,10},{8,40},{10,14},{12,44},{14,2},{16,48},{... | collective-permute-start | bytes 1572872 | tf_op jit(solution)/shard_map/ppermute | solution.py:29
  115.1 11.3 %collective-permute-start.9 = (bf16[2,2,2,2,128,128]{5,4,3,2,1,0:T(8,128)(2,1)S(1)}, bf16[2,2,2,2,128,128]{5,4,3,2,1,0:T(8,128)(2,1)S(1)}, u32[]{:S(2)}, u32[]{:S(2)}) collective-permute-start(bf16[2,2,2,2,128,128]{5,4,3,2,1,0:T(8,128)(2,1)S(1)} %get-tuple-element.42.refs_7_), channel_id=1, source_target_pairs={{0,96},{2,14},{4,100},{6,2},{8,104},{10,6},{12,108},{14,10},{16,11... | collective-permute-start | bytes 1572872 | tf_op jit(solution)/shard_map/ppermute | solution.py:29
  131.4 17.8 %collective-permute-start.12 = (bf16[2,5,144,128]{3,2,1,0:T(8,128)(2,1)S(1)}, bf16[2,5,144,128]{3,2,1,0:T(8,128)(2,1)S(1)}, u32[]{:S(2)}, u32[]{:S(2)}) collective-permute-start(bf16[2,5,144,128]{3,2,1,0:T(8,128)(2,1)S(1)} %get-tuple-element.55), channel_id=1, source_target_pairs={{0,18},{2,16},{4,22},{6,20},{8,26},{10,24},{12,30},{14,28},{16,2},... | collective-permute-start | bytes 1105928 | tf_op jit(solution)/shard_map/ppermute | solution.py:29
  134.0 17.7 %collective-permute-start.11 = (bf16[2,5,144,128]{3,2,1,0:T(8,128)(2,1)S(1)}, bf16[2,5,144,128]{3,2,1,0:T(8,128)(2,1)S(1)}, u32[]{:S(2)}, u32[]{:S(2)}) collective-permute-start(bf16[2,5,144,128]{3,2,1,0:T(8,128)(2,1)S(1)} %get-tuple-element.51.refs_9_), channel_id=1, source_target_pairs={{0,16},{2,18},{4,20},{6,22},{8,24},{10,26},{12,28},{14,30},{16,0},... | collective-permute-start | bytes 1105928 | tf_op jit(solution)/shard_map/ppermute | solution.py:29
  151.9 1.8 %collective-permute-start.13 = (bf16[2,5,144,128]{3,2,1,0:T(8,128)(2,1)S(1)}, bf16[2,5,144,128]{3,2,1,0:T(8,128)(2,1)S(1)}, u32[]{:S(2)}, u32[]{:S(2)}) collective-permute-start(bf16[2,5,144,128]{3,2,1,0:T(8,128)(2,1)S(1)} %get-tuple-element.57), channel_id=1, source_target_pairs={{0,2},{2,0},{4,6},{6,4},{8,10},{10,8},{12,14},{14,12},{16,18},{18,... | collective-permute-start | bytes 1105928 | tf_op jit(solution)/shard_map/ppermute | solution.py:29

commit v5 on v4

--- a/solution.py
+++ b/solution.py
@@ -140,7 +140,9 @@
     )(expert_out)
 
 
-def pick_kernel(first, hot, gate, returned, residual, shared, after, out, base, extra, done, arrive, leave):
+def pick_kernel(first, hot, gate, returned, residual, shared, before, *refs):
+    hidden = refs[0]
+    out, base, extra, done, arrive, leave = refs[-6:]
     chunks, block, width = base.shape
     cols = slice(first, first + width)
 
@@ -151,8 +153,13 @@
             pltpu.make_async_copy(shared.at[rows, cols], extra.at[i], arrive.at[1, i]),
         ]
 
-    def store(i):
-        return pltpu.make_async_copy(done.at[i], out.at[pl.ds(i * block, block)], leave.at[i])
+    def stores(i):
+        rows = pl.ds(i * block, block)
+        copies = [pltpu.make_async_copy(done.at[i], out.at[rows], leave.at[0, i])]
+        if first > 0:
+            copies.append(pltpu.make_async_copy(done.at[i], hidden.at[rows, cols], leave.at[1, i]))
+            copies.append(pltpu.make_async_copy(before.at[rows], hidden.at[rows, :first], leave.at[2, i]))
+        return copies
 
     for i in range(chunks):
         for copy in loads(i):
@@ -164,12 +171,14 @@
             copy.wait()
         total = base[i].astype(jnp.float32) + extra[i].astype(jnp.float32)
         done[i] = (total + gate[rows] * picked).astype(jnp.bfloat16)
-        store(i).start()
+        for copy in stores(i):
+            copy.start()
     for i in range(chunks):
-        store(i).wait()
-
-
-def pick(part, hot, gate, returned, residual, shared, after):
+        for copy in stores(i):
+            copy.wait()
+
+
+def pick(part, hot, gate, returned, residual, shared, before):
     rows, width = residual.shape
     width = width // 2
     chunks = 2
@@ -178,19 +187,22 @@
     return pl.pallas_call(
         functools.partial(pick_kernel, part * width),
         in_specs=[vmem()] * 3 + [hbm()] * 2 + [anywhere()],
-        out_specs=hbm(),
-        out_shape=jax.ShapeDtypeStruct((rows, width), jnp.bfloat16),
+        out_specs=[hbm()] * (part + 1),
+        out_shape=[
+            jax.ShapeDtypeStruct((rows, columns), jnp.bfloat16)
+            for columns in ((2 * width, width) if part else (width,))
+        ],
         scratch_shapes=[
             tile,
             tile,
             tile,
             pltpu.SemaphoreType.DMA((2, chunks)),
-            pltpu.SemaphoreType.DMA((chunks,)),
+            pltpu.SemaphoreType.DMA((3, chunks)),
         ],
         compiler_params=params(10),
         cost_estimate=takes(2.5),
         name="pick",
-    )(hot, gate, returned, residual, shared, after)
+    )(hot, gate, returned, residual, shared, before)
 
 
 KV_TILES, Q_TILES = 4, 2 * GROUP
@@ -410,27 +422,36 @@
         write_parts(acc, den, top, parts)
 
 
+def side_of(part, side):
+    return part[side] if isinstance(part, tuple) else part.at[side]
+
+
 def write_parts(acc, den, top, parts):
     for side in range(2):
+        targets = [side_of(part, side) for part in parts]
+        highs, lows = [], []
         for head in range(GROUP):
             denominator = den[side, head]
             some = denominator > 0.0
             safe = jnp.where(some, denominator, 1.0)
             inverse = jnp.where(some, 1.0 / safe, 0.0)
             value = (acc[side, head] * inverse[:1]).astype(jnp.bfloat16)
-            level = jnp.where(some, top[side, head] + jnp.log2(safe), NEG_FILL)
-            high = level.astype(jnp.bfloat16)
-            low = (level - high.astype(jnp.float32)).astype(jnp.bfloat16)
-            levels = jnp.concatenate([high, low], axis=0)
-            for core in range(2):
-                rows = slice(core * HALF, (core + 1) * HALF)
-                parts[core][side, head, :HD] = value[:, rows]
-                parts[core][side, head, HD:] = levels[:, rows]
+            level = jnp.where(some, top[side, head] + jnp.log2(safe), NEG_FILL)[:1]
+            high = level.astype(jnp.bfloat16).astype(jnp.float32)
+            highs.append(high)
+            lows.append(level - high)
+            for core, target in enumerate(targets):
+                target[head * HD : (head + 1) * HD] = value[:, core * HALF : (core + 1) * HALF]
+        filler = jnp.zeros((LOGS - 2 * GROUP, 2 * HALF), jnp.float32)
+        levels = jnp.concatenate(highs + lows + [filler], axis=0).astype(jnp.bfloat16)
+        for core, target in enumerate(targets):
+            target[GROUP * HD :] = levels[:, core * HALF : (core + 1) * HALF]
 
 
 ACC = (2, GROUP, HD, 2 * HALF)
 ROWS = (2, GROUP, 8, 2 * HALF)
-PART = (2, GROUP, HD + 16, HALF)
+LOGS = 16
+PART = (2, GROUP * HD + LOGS, HALF)
 
 
 def attend(flags, q, kvs, state, diag=False, finish=False, after=(), time=None):
@@ -460,21 +481,21 @@
     )(flags, q, *kvs, *olds, *after)
 
 
-def divide_kernel(waits, *refs):
-    acc, den, top = refs[:3]
-    write_parts(acc, den, top, refs[3 + waits :])
+def divide_kernel(acc, den, top, after, same, other_early, other_late):
+    write_parts(acc, den, top, (same, (other_early, other_late)))
 
 
 def divide(state, after):
-    return pl.pallas_call(
-        functools.partial(divide_kernel, len(after)),
-        in_specs=[vmem()] * 3 + [anywhere()] * len(after),
-        out_specs=[vmem()] * 2,
-        out_shape=[jax.ShapeDtypeStruct(PART, jnp.bfloat16)] * 2,
+    shapes = (PART, PART[1:], PART[1:])
+    return pl.pallas_call(
+        divide_kernel,
+        in_specs=[vmem()] * 3 + [anywhere()],
+        out_specs=[vmem()] * 3,
+        out_shape=[jax.ShapeDtypeStruct(shape, jnp.bfloat16) for shape in shapes],
         compiler_params=params(),
         cost_estimate=takes(0.7),
         name="divide",
-    )(*state, *after)
+    )(*state, after)
 
 
 def join_kernel(*refs):
@@ -495,34 +516,38 @@
     )(*blocks, after)
 
 
-def merge_kernel(core, own, own_pair, sibling, sibling_pair, out):
-    def level(part, side, head):
-        terms = part[side, head, HD:].astype(jnp.float32)
-        return terms[:1] + terms[8:9]
-
+def merge_kernel(core, own, own_pair, sibling_early, sibling_late, sibling_pair, out):
+    def read(part, side):
+        terms = side_of(part, side)[GROUP * HD :].astype(jnp.float32)
+        values = side_of(part, side)[: GROUP * HD].astype(jnp.float32)
+        return terms[:GROUP] + terms[GROUP : 2 * GROUP], values
+
+    sibling = (sibling_early, sibling_late)
     for group, (one, two) in ((core[0], (own, own_pair)), (1 - core[0], (sibling, sibling_pair))):
         for side in range(2):
+            mine, value = read(one, side)
+            other, other_value = read(two, side)
+            high = jnp.maximum(mine, other)
+            first = jnp.exp2(mine - high)
+            second = jnp.exp2(other - high)
+            weight = 1.0 / (first + second)
+            first, second = first * weight, second * weight
             for head in range(GROUP):
-                mine, other = level(one, side, head), level(two, side, head)
-                top = jnp.maximum(mine, other)
-                first = jnp.exp2(mine - top)
-                second = jnp.exp2(other - top)
-                weight = 1.0 / (first + second)
-                value = one[side, head, :HD].astype(jnp.float32) * (first * weight)
-                value = value + two[side, head, :HD].astype(jnp.float32) * (second * weight)
+                rows = slice(head * HD, (head + 1) * HD)
+                mixed = value[rows] * first[head : head + 1] + other_value[rows] * second[head : head + 1]
                 cols = pl.ds(pl.multiple_of((group * GROUP + head) * HD, HD), HD)
-                out[side * HALF : (side + 1) * HALF, cols] = value.T.astype(jnp.bfloat16)
-
-
-def merge(core, own, own_pair, sibling, sibling_pair):
+                out[side * HALF : (side + 1) * HALF, cols] = mixed.T.astype(jnp.bfloat16)
+
+
+def merge(core, own, own_pair, sibling_early, sibling_late, sibling_pair):
     return pl.pallas_call(
         merge_kernel,
-        in_specs=[smem()] + [vmem()] * 4,
+        in_specs=[smem()] + [vmem()] * 5,
         out_specs=vmem(),
         out_shape=jax.ShapeDtypeStruct((2 * HALF, 2 * GROUP * HD), jnp.bfloat16),
         compiler_params=params(),
         name="merge",
-    )(core, own, own_pair, sibling, sibling_pair)
+    )(core, own, own_pair, sibling_early, sibling_late, sibling_pair)
 
 
 def cut_kernel(ahead, behind, after, first, second):
@@ -570,9 +595,8 @@
     returned = lax.all_to_all(relayout(expert_out), "ctx", split_axis=0, concat_axis=0, tiled=True)
     returned = returned.reshape(sources * own_experts * slots, half_width)
     hot = choose(routing, returned.shape[0])
-    ha = pick(0, hot, gate_score, returned, residual, shared_out, hot)
-    hb = pick(1, hot, gate_score, returned, residual, shared_out, ha)
-    hidden = jnp.concatenate([ha, hb], axis=1)
+    (ha,) = pick(0, hot, gate_score, returned, residual, shared_out, hot)
+    hidden, hb = pick(1, hot, gate_score, returned, residual, shared_out, ha)
 
     other_a, other_b = (lax.ppermute(h, "tp", [(0, 1), (1, 0)]) for h in (ha, hb))
     where = jnp.stack([tp_index, k])
@@ -611,8 +635,9 @@
     pair_same, pair_other = attend(pair_flags[12:], q_pair, farther, pair_state, finish=True)
     own_pair, sibling_pair = to_pair(pair_same), to_pair_other(pair_other)
     own_state = attend(own_flags[4:], q_own, [ahead, behind] + farther, own_state, after=(pair_same,))
-    own_same, own_other = divide(own_state, (own_pair, sibling_pair))
-    attended = merge(k.reshape(1), own_same, own_pair, core_swap(own_other), sibling_pair)
+    own_same, *own_other = divide(own_state, sibling_pair)
+    siblings = [core_swap(part) for part in own_other]
+    attended = merge(k.reshape(1), own_same, own_pair, *siblings, sibling_pair)
     return hidden, attended
 
 

time: 155 us -> 153 us (0.987)
  waiting for transfers between devices: 67.7 us -> 65.3 us
    ppermute x12 -> x13, waiting for transfers between devices: 12.6 us -> 10.6 us  [permute(): return lax.ppermute(value, 'ctx', pairs)]
    ppermute x12 -> x13, starting transfers between devices: 15.1 us -> 15.6 us  [permute(): return lax.ppermute(value, 'ctx', pairs)]
  transfers between devices with their start and end apart: 15 -> 16, of which waited for: 10 -> 11; matrix products, arithmetic and copies ran while one was open for 2% -> 1% of each run, Pallas kernels for 26% -> 27%
where the time goes in v5:
time: 153 us; the launch traced here: 152 us
  waiting for transfers between devices  65.3 us (43%)
  Pallas kernels  54.5 us (36%)
  starting transfers between devices  29.7 us (19%)
    pallas_call x6, Pallas kernels, attend(): pl.pallas_call(functools.partial(attend_kernel, counts, diag, state is no...  36.4 us
    all_to_all x1, waiting for transfers between devices, shards(): lax.all_to_all(relayout(expert_out), 'ctx', split_axis=0, concat_axis=0,...  34.9 us
    ppermute x2, waiting for transfers between devices, shards(): lax.ppermute(h, 'tp', [(0, 1), (1, 0)])  19.9 us
    ppermute x13, starting transfers between devices, permute(): return lax.ppermute(value, 'ctx', pairs)  15.6 us
    all_to_all x1, starting transfers between devices, shards(): lax.all_to_all(relayout(expert_out), 'ctx', split_axis=0, concat_axis=0,...  12.4 us
    ppermute x13, waiting for transfers between devices, permute(): return lax.ppermute(value, 'ctx', pairs)  10.6 us
    pallas_call x3, Pallas kernels, project(): pl.pallas_call(kernel, in_specs=[smem()] + [vmem()] * len(ins), out_specs...  7.81 us
    pallas_call x2, Pallas kernels, pick(): pl.pallas_call(functools.partial(pick_kernel, part * width), in_specs=[vm...  5.79 us
  transfers between devices with their start and end apart: 16, of which 11 were waited for; matrix products, arithmetic and copies ran while one was open for 1% of the time, Pallas kernels for 27%

profile of v5, /device:TPU:1, one launch (start us, length us, event | category | flops | bytes accessed | tf_op | source)
XLA Modules:
  0.0 152.3 jit_solution(1167412188101784661)
XLA Ops:
  0.6 2.7 %relayout.1 = bf16[64,8,2560]{2,1,0:T(8,128)(2,1)} custom-call(bf16[2,64,4,2560]{3,2,1,0:T(4,128)(2,1)} %experts.1), custom_call_target="tpu_custom_call" | custom-call | tf_op jit(solution)/shard_map/relayout/pallas_call | solution.py:127
  3.4 12.4 %all-to-all-start = ((bf16[64,8,2560]{2,1,0:T(8,128)(2,1)}), bf16[64,8,2560]{2,1,0:T(8,128)(2,1)S(1)}, u32[]{:S(2)}, u32[]{:S(2)}) async-start(bf16[64,8,2560]{2,1,0:T(8,128)(2,1)} %relayout.1), calls=%async_computation | async-start | bytes 5242880 | tf_op jit(solution)/shard_map/all_to_all | solution.py:595
  16.0 0.1 copy.17.gate
  16.1 0.1 copy.15.ids_col
  16.2 0.3 choose.1.hot.before
  16.5 0.1 pad_add_fusion.where
  16.6 0.1 add_convert_fusion.1.refs_0_
  16.7 0.5 fusion
  17.3 0.1 pad_maximum_fusion.1
  17.4 34.9 %all-to-all-done = bf16[64,8,2560]{2,1,0:T(8,128)(2,1)S(1)} async-done(((bf16[64,8,2560]{2,1,0:T(8,128)(2,1)}), bf16[64,8,2560]{2,1,0:T(8,128)(2,1)S(1)}, u32[]{:S(2)}, u32[]{:S(2)}) %all-to-all-start) | async-done | bytes 2621472 | tf_op jit(solution)/shard_map/all_to_all | solution.py:595
  52.3 2.2 %pick.2.before.ha = bf16[256,1280]{1,0:T(8,128)(2,1)S(1)} custom-call(bf16[256,512]{1,0:T(8,128)(2,1)S(1)} %choose.1.hot.before, f32[256,1]{1,0:T(8,128)S(1)} %copy.17.gate, bf16[512,2560]{1,0:T(8,128)(2,1)S(1)} %bitcast.10, bf16[256,2560]{1,0:T(8,128)(2,1)} %residual.3, bf16[256,2560]{1,0:T(8,128)(2,1)} %shared.3, bf16[256,512]{1,0:T(8,128)(2,1)S(1)} %choose.1.hot.before), custom_call_target="tpu_custom_call" | custom-call | flops 2875000064 | tf_op jit(solution)/shard_map/pick/pallas_call | solution.py:187
  54.5 0.8 collective-permute-start.1
  55.3 3.6 %pick.3 = (bf16[256,2560]{1,0:T(8,128)(2,1)}, bf16[256,1280]{1,0:T(8,128)(2,1)S(1)}) custom-call(bf16[256,512]{1,0:T(8,128)(2,1)S(1)} %choose.1.hot.before, f32[256,1]{1,0:T(8,128)S(1)} %copy.17.gate, bf16[512,2560]{1,0:T(8,128)(2,1)S(1)} %bitcast.11, bf16[256,2560]{1,0:T(8,128)(2,1)} %residual.3, bf16[256,2560]{1,0:T(8,128)(2,1)} %shared.3, ...), custom_call_target="tpu_custom_call" | custom-call | flops 2875000064 | tf_op jit(solution)/shard_map/pick/pallas_call | solution.py:187
  59.0 0.8 collective-permute-start
  59.8 0.3 copy-done.2
  60.0 3.2 %project_own.1 = (f32[256,1792]{1,0:T(8,128)S(1)}, f32[256,1]{1,0:T(8,128)S(1)}) custom-call(s32[2]{0:T(128)S(1)} %pad_add_fusion.where, bf16[256,1280]{1,0:T(8,128)(2,1)S(1)} %pick.2.before.ha, bf16[256,1280]{1,0:T(8,128)(2,1)S(1)} %get-tuple-element.34.hb, bf16[4,1,1280]{2,1,0:T(2,128)(2,1)S(1)} %reshape.38.gain, bf16[5120,256]{1,0:T(8,128)(2,1)S(1)} %copy-done.1, ...), custom_call_target="tpu_custom_call" | custom-call | flops 5750000128 | tf_op jit(solution)/shard_map/project_own/pallas_call | solution.py:288
  63.3 7.8 %collective-permute-done.1.h = bf16[256,1280]{1,0:T(8,128)(2,1)S(1)} collective-permute-done((bf16[256,1280]{1,0:T(8,128)(2,1)S(1)}, bf16[256,1280]{1,0:T(8,128)(2,1)S(1)}, u32[]{:S(2)}, u32[]{:S(2)}) %collective-permute-start.1) | collective-permute-done | bytes 655392 | tf_op jit(solution)/shard_map/ppermute | solution.py:601
  71.0 2.0 %project_more.1 = (f32[256,1792]{1,0:T(8,128)S(1)}, f32[256,1]{1,0:T(8,128)S(1)}) custom-call(s32[2]{0:T(128)S(1)} %pad_add_fusion.where, bf16[256,1280]{1,0:T(8,128)(2,1)S(1)} %collective-permute-done.1.h, bf16[4,1,1280]{2,1,0:T(2,128)(2,1)S(1)} %reshape.38.gain, bf16[5120,256]{1,0:T(8,128)(2,1)S(1)} %copy-done.1, bf16[5120,256]{1,0:T(8,128)(2,1)S(1)} %copy-done.2, ...), custom_call_target="tpu_custom_call" | custom-call | flops 2300000000 | tf_op jit(solution)/shard_map/project_more/pallas_call | solution.py:288
  73.0 12.1 %collective-permute-done.h = bf16[256,1280]{1,0:T(8,128)(2,1)S(1)} collective-permute-done((bf16[256,1280]{1,0:T(8,128)(2,1)S(1)}, bf16[256,1280]{1,0:T(8,128)(2,1)S(1)}, u32[]{:S(2)}, u32[]{:S(2)}) %collective-permute-start) | collective-permute-done | bytes 655392 | tf_op jit(solution)/shard_map/ppermute | solution.py:601
  85.1 2.6 %project_last.1 = (bf16[2,2,128,128]{3,2,1,0:T(8,128)(2,1)S(1)}, bf16[5,2,128,128]{3,2,1,0:T(8,128)(2,1)S(1)}, bf16[14,128,128]{2,1,0:T(8,128)(2,1)S(1)}) custom-call(s32[2]{0:T(128)S(1)} %pad_add_fusion.where, bf16[256,1280]{1,0:T(8,128)(2,1)S(1)} %collective-permute-done.h, bf16[4,1,1280]{2,1,0:T(2,128)(2,1)S(1)} %reshape.38.gain, ...), custom_call_target="tpu_custom_call" | custom-call | flops 2300000000 | tf_op jit(solution)/shard_map/project_last/pallas_call | solution.py:288
  87.7 0.8 collective-permute-start.2
  88.5 0.1 add_convert_fusion.refs_0_
  88.6 1.3 collective-permute-done.2
  90.0 0.2 collective-permute-start.5
  90.1 1.3 collective-permute-start.4
  91.4 1.4 collective-permute-start.3
  92.9 0.6 collective-permute-start.8
  93.5 2.0 %attend.6 = (f32[2,5,128,256]{3,2,1,0:T(8,128)S(1)}, f32[2,5,8,256]{3,2,1,0:T(8,128)S(1)}, f32[2,5,8,256]{3,2,1,0:T(8,128)S(1)}) custom-call(s32[1]{0:T(128)} %bitcast.2.refs_0_.core, bf16[2,5,2,128,128]{4,3,2,1,0:T(8,128)(2,1)S(1)} %pad_maximum_fusion.refs_1_, bf16[1,2,2,2,128,128]{5,4,3,2,1,0:T(8,128)(2,1)S(1)} %maximum_bitcast_fusion.refs_2_.refs_0_), custom_call_target="tpu_custom_call" | custom-call | flops 34500001792 | tf_op jit(solution)/shard_map/attend/pallas_call | solution.py:472
  95.5 1.6 %collective-permute-done.5.refs_3_.refs_4_ = bf16[1,2,2,2,128,128]{5,4,3,2,1,0:T(8,128)(2,1)S(1)} collective-permute-done((bf16[1,2,2,2,128,128]{5,4,3,2,1,0:T(8,128)(2,1)S(1)}, bf16[1,2,2,2,128,128]{5,4,3,2,1,0:T(8,128)(2,1)S(1)}, u32[]{:S(2)}, u32[]{:S(2)}) %collective-permute-start.5) | collective-permute-done | bytes 262176 | tf_op jit(solution)/shard_map/ppermute | solution.py:29
  97.1 2.6 %collective-permute-done.4.refs_2_.refs_3_ = bf16[1,2,2,2,128,128]{5,4,3,2,1,0:T(8,128)(2,1)S(1)} collective-permute-done((bf16[1,2,2,2,128,128]{5,4,3,2,1,0:T(8,128)(2,1)S(1)}, bf16[1,2,2,2,128,128]{5,4,3,2,1,0:T(8,128)(2,1)S(1)}, u32[]{:S(2)}, u32[]{:S(2)}) %collective-permute-start.4) | collective-permute-done | bytes 262176 | tf_op jit(solution)/shard_map/ppermute | solution.py:29
  99.9 2.7 %collective-permute-start.6 = (bf16[4,2,2,2,128,128]{5,4,3,2,1,0:T(8,128)(2,1)S(1)}, bf16[4,2,2,2,128,128]{5,4,3,2,1,0:T(8,128)(2,1)S(1)}, u32[]{:S(2)}, u32[]{:S(2)}) collective-permute-start(bf16[4,2,2,2,128,128]{5,4,3,2,1,0:T(8,128)(2,1)S(1)} %join.1.refs_8_.refs_2_), channel_id=1, source_target_pairs={{0,96},{2,14},{4,100},{6,2},{8,104},{10,6},{12,108},{14,10},{16,11... | collective-permute-start | bytes 3145736 | tf_op jit(solution)/shard_map/ppermute | solution.py:29
  102.5 3.6 %attend.7 = (f32[2,5,128,256]{3,2,1,0:T(8,128)S(1)}, f32[2,5,8,256]{3,2,1,0:T(8,128)S(1)}, f32[2,5,8,256]{3,2,1,0:T(8,128)S(1)}) custom-call(s32[3]{0:T(128)S(1)} %slice_convert_fusion.refs_0_, bf16[2,5,2,128,128]{4,3,2,1,0:T(8,128)(2,1)S(1)} %pad_maximum_fusion.refs_1_, bf16[1,2,2,2,128,128]{5,4,3,2,1,0:T(8,128)(2,1)S(1)} %collective-permute-done.3.refs_1_.refs_2_, ...), custom_call_target="tpu_custom_call" | custom-call | flops 3967500032 | tf_op jit(solution)/shard_map/attend/pallas_call | solution.py:472
  106.1 3.9 %collective-permute-done.8.refs_1_ = bf16[2,5,2,128,128]{4,3,2,1,0:T(8,128)(2,1)S(1)} collective-permute-done((bf16[2,5,2,128,128]{4,3,2,1,0:T(8,128)(2,1)S(1)}, bf16[2,5,2,128,128]{4,3,2,1,0:T(8,128)(2,1)S(1)}, u32[]{:S(2)}, u32[]{:S(2)}) %collective-permute-start.8) | collective-permute-done | bytes 655392 | tf_op jit(solution)/shard_map/ppermute | solution.py:29
  110.0 4.9 %attend.8 = (f32[2,5,128,256]{3,2,1,0:T(8,128)S(1)}, f32[2,5,8,256]{3,2,1,0:T(8,128)S(1)}, f32[2,5,8,256]{3,2,1,0:T(8,128)S(1)}) custom-call(s32[4]{0:T(128)S(1)} %compare_convert_fusion.1.refs_0_, bf16[2,5,2,128,128]{4,3,2,1,0:T(8,128)(2,1)S(1)} %collective-permute-done.8.refs_1_, bf16[4,2,2,2,128,128]{5,4,3,2,1,0:T(8,128)(2,1)S(1)} %join.1.refs_8_.refs_2_, ...), custom_call_target="tpu_custom_call" | custom-call | flops 8049999872 | tf_op jit(solution)/shard_map/attend/pallas_call | solution.py:472
  114.9 0.1 collective-permute-done.7.behind.refs_3_
  115.2 2.7 %collective-permute-start.9 = (bf16[2,2,2,2,128,128]{5,4,3,2,1,0:T(8,128)(2,1)S(1)}, bf16[2,2,2,2,128,128]{5,4,3,2,1,0:T(8,128)(2,1)S(1)}, u32[]{:S(2)}, u32[]{:S(2)}) collective-permute-start(bf16[2,2,2,2,128,128]{5,4,3,2,1,0:T(8,128)(2,1)S(1)} %get-tuple-element.47.refs_7_), channel_id=1, source_target_pairs={{0,96},{2,14},{4,100},{6,2},{8,104},{10,6},{12,108},{14,10},{16,11... | collective-permute-start | bytes 1572872 | tf_op jit(solution)/shard_map/ppermute | solution.py:29
  117.8 8.6 %attend.9 = (f32[2,5,128,256]{3,2,1,0:T(8,128)S(1)}, f32[2,5,8,256]{3,2,1,0:T(8,128)S(1)}, f32[2,5,8,256]{3,2,1,0:T(8,128)S(1)}) custom-call(s32[8]{0:T(128)S(1)} %add_convert_fusion.1.refs_0_, bf16[2,5,2,128,128]{4,3,2,1,0:T(8,128)(2,1)S(1)} %collective-permute-done.8.refs_1_, bf16[4,2,2,2,128,128]{5,4,3,2,1,0:T(8,128)(2,1)S(1)} %collective-permute-done.6.ahead.refs_2_, ...), custom_call_target="tpu_custom_call" | custom-call | flops 10579999744 | tf_op jit(solution)/shard_map/attend/pallas_call | solution.py:472
  126.4 5.0 %attend.10 = (bf16[2,656,128]{2,1,0:T(8,128)(2,1)S(1)}, bf16[2,656,128]{2,1,0:T(8,128)(2,1)S(1)}) custom-call(s32[4]{0:T(128)S(1)} %get-tuple-element.75.refs_0_, bf16[2,5,2,128,128]{4,3,2,1,0:T(8,128)(2,1)S(1)} %collective-permute-done.8.refs_1_, bf16[2,2,2,2,128,128]{5,4,3,2,1,0:T(8,128)(2,1)S(1)} %collective-permute-done.9.refs_2_.refs_4_, ...), custom_call_target="tpu_custom_call" | custom-call | flops 5289999872 | tf_op jit(solution)/shard_map/attend/pallas_call | solution.py:472
  131.4 2.6 %collective-permute-start.11 = (bf16[2,656,128]{2,1,0:T(8,128)(2,1)S(1)}, bf16[2,656,128]{2,1,0:T(8,128)(2,1)S(1)}, u32[]{:S(2)}, u32[]{:S(2)}) collective-permute-start(bf16[2,656,128]{2,1,0:T(8,128)(2,1)S(1)} %get-tuple-element.60), channel_id=1, source_target_pairs={{0,18},{2,16},{4,22},{6,20},{8,26},{10,24},{12,30},{14,28},{16,2},... | collective-permute-start | bytes 1007624 | tf_op jit(solution)/shard_map/ppermute | solution.py:29
  134.0 2.7 %collective-permute-start.12 = (bf16[2,656,128]{2,1,0:T(8,128)(2,1)S(1)}, bf16[2,656,128]{2,1,0:T(8,128)(2,1)S(1)}, u32[]{:S(2)}, u32[]{:S(2)}) collective-permute-start(bf16[2,656,128]{2,1,0:T(8,128)(2,1)S(1)} %get-tuple-element.56.refs_9_), channel_id=1, source_target_pairs={{0,16},{2,18},{4,20},{6,22},{8,24},{10,26},{12,28},{14,30},{16,0},... | collective-permute-start | bytes 1007624 | tf_op jit(solution)/shard_map/ppermute | solution.py:29
  136.7 12.4 %attend.11 = (f32[2,5,128,256]{3,2,1,0:T(8,128)S(1)}, f32[2,5,8,256]{3,2,1,0:T(8,128)S(1)}, f32[2,5,8,256]{3,2,1,0:T(8,128)S(1)}) custom-call(s32[12]{0:T(128)S(1)} %add_convert_fusion.refs_0_, bf16[2,5,2,128,128]{4,3,2,1,0:T(8,128)(2,1)S(1)} %pad_maximum_fusion.refs_1_, bf16[4,2,2,2,128,128]{5,4,3,2,1,0:T(8,128)(2,1)S(1)} %collective-permute-done.6.ahead.refs_2_, ...), custom_call_target="tpu_custom_call" | custom-call | flops 15870000128 | tf_op jit(solution)/shard_map/attend/pallas_call | solution.py:472
  149.2 0.1 divide.1
  149.3 0.1 collective-permute-start.13
  149.4 0.5 collective-permute-start.14
  149.9 0.5 collective-permute-done.12.own_pair
  150.4 0.4 collective-permute-done.13.sibling_early
  150.8 0.2 collective-permute-done.14.sibling_late
  151.0 1.3 merge.1
  (34 shorter events, 0.6 us)
Async XLA Ops:
  3.3 12.6 %copy-start.4 = (bf16[5120]{0:T(1024)(128)(2,1)S(1)}, bf16[5120]{0:T(1024)(128)(2,1)}, u32[]{:S(2)}) copy-start(bf16[5120]{0:T(1024)(128)(2,1)} %param.15) | copy-start | bytes 30724
  3.3 12.6 %copy-start.5 = (f32[256,1]{0,1:T(1,128)S(1)}, f32[256,1]{0,1:T(1,128)}, u32[]{:S(2)}) copy-start(f32[256,1]{0,1:T(1,128)} %param.14) | copy-start | bytes 3076
  3.4 12.7 %copy-start.3 = (s32[256,1]{0,1:T(1,128)S(1)}, s32[256,1]{0,1:T(1,128)}, u32[]{:S(2)}) copy-start(s32[256,1]{0,1:T(1,128)} %param.13) | copy-start | bytes 3076
  3.4 13.2 %copy-start.6 = (s32[4]{0:T(128)S(1)}, s32[4]{0:T(128)}, u32[]{:S(2)}) copy-start(s32[4]{0:T(128)} %constant.156.clone) | copy-start | bytes 52
  3.4 48.9 %all-to-all-start = ((bf16[64,8,2560]{2,1,0:T(8,128)(2,1)}), bf16[64,8,2560]{2,1,0:T(8,128)(2,1)S(1)}, u32[]{:S(2)}, u32[]{:S(2)}) async-start(bf16[64,8,2560]{2,1,0:T(8,128)(2,1)} %relayout.1), calls=%async_computation | async-start | bytes 5242880 | tf_op jit(solution)/shard_map/all_to_all | solution.py:595
  52.3 7.5 %copy-start = (bf16[5120,1280]{1,0:T(8,128)(2,1)S(1)}, bf16[5120,1280]{1,0:T(8,128)(2,1)}, u32[]{:S(2)}) copy-start(bf16[5120,1280]{1,0:T(8,128)(2,1)} %wq.5) | copy-start | bytes 39321604
  54.5 5.3 %copy-start.1 = (bf16[5120,256]{1,0:T(8,128)(2,1)S(1)}, bf16[5120,256]{1,0:T(8,128)(2,1)}, u32[]{:S(2)}) copy-start(bf16[5120,256]{1,0:T(8,128)(2,1)} %wk.5) | copy-start | bytes 7864324
  54.5 5.5 %copy-start.2 = (bf16[5120,256]{1,0:T(8,128)(2,1)S(1)}, bf16[5120,256]{1,0:T(8,128)(2,1)}, u32[]{:S(2)}) copy-start(bf16[5120,256]{1,0:T(8,128)(2,1)} %wv.5) | copy-start | bytes 7864324
  54.5 16.5 %collective-permute-start.1 = (bf16[256,1280]{1,0:T(8,128)(2,1)S(1)}, bf16[256,1280]{1,0:T(8,128)(2,1)S(1)}, u32[]{:S(2)}, u32[]{:S(2)}) collective-permute-start(bf16[256,1280]{1,0:T(8,128)(2,1)S(1)} %pick.2.before.ha), channel_id=1, source_target_pairs={{0,1},{1,0},{2,3},{3,2},{4,5},{5,4},{6,7},{7,6},{8,9},{9,8},{10,11... | collective-permute-start | bytes 1966088 | tf_op jit(solution)/shard_map/ppermute | solution.py:601
  59.0 26.1 %collective-permute-start = (bf16[256,1280]{1,0:T(8,128)(2,1)S(1)}, bf16[256,1280]{1,0:T(8,128)(2,1)S(1)}, u32[]{:S(2)}, u32[]{:S(2)}) collective-permute-start(bf16[256,1280]{1,0:T(8,128)(2,1)S(1)} %get-tuple-element.34.hb), channel_id=1, source_target_pairs={{0,1},{1,0},{2,3},{3,2},{4,5},{5,4},{6,7},{7,6},{8,9},{9,8},{10,11... | collective-permute-start | bytes 1966088 | tf_op jit(solution)/shard_map/ppermute | solution.py:601
  87.7 2.2 %collective-permute-start.2 = (bf16[14,128,128]{2,1,0:T(8,128)(2,1)S(1)}, bf16[14,128,128]{2,1,0:T(8,128)(2,1)S(1)}, u32[]{:S(2)}, u32[]{:S(2)}) collective-permute-start(bf16[14,128,128]{2,1,0:T(8,128)(2,1)S(1)} %get-tuple-element.40), channel_id=1, source_target_pairs={{0,2},{2,0},{4,6},{6,4},{8,10},{10,8},{12,14},{14,12},{16,18},{18,... | collective-permute-start | bytes 1376264 | tf_op jit(solution)/shard_map/ppermute | solution.py:29
  90.0 7.1 %collective-permute-start.5 = (bf16[1,2,2,2,128,128]{5,4,3,2,1,0:T(8,128)(2,1)S(1)}, bf16[1,2,2,2,128,128]{5,4,3,2,1,0:T(8,128)(2,1)S(1)}, u32[]{:S(2)}, u32[]{:S(2)}) collective-permute-start(bf16[1,2,2,2,128,128]{5,4,3,2,1,0:T(8,128)(2,1)S(1)} %maximum_bitcast_fusion.refs_2_.refs_0_), channel_id=1, source_target_pairs={{0,8},{2,66},{4,12},{6,70},{8,0},{10,74},{12,4},{14,78},{16,24},{1... | collective-permute-start | bytes 786440 | tf_op jit(solution)/shard_map/ppermute | solution.py:29
  90.1 9.6 %collective-permute-start.4 = (bf16[1,2,2,2,128,128]{5,4,3,2,1,0:T(8,128)(2,1)S(1)}, bf16[1,2,2,2,128,128]{5,4,3,2,1,0:T(8,128)(2,1)S(1)}, u32[]{:S(2)}, u32[]{:S(2)}) collective-permute-start(bf16[1,2,2,2,128,128]{5,4,3,2,1,0:T(8,128)(2,1)S(1)} %maximum_bitcast_fusion.refs_2_.refs_0_), channel_id=1, source_target_pairs={{0,4},{2,34},{4,8},{6,38},{8,12},{10,42},{12,0},{14,46},{16,20},{1... | collective-permute-start | bytes 786440 | tf_op jit(solution)/shard_map/ppermute | solution.py:29
  91.4 8.3 %collective-permute-start.3 = (bf16[1,2,2,2,128,128]{5,4,3,2,1,0:T(8,128)(2,1)S(1)}, bf16[1,2,2,2,128,128]{5,4,3,2,1,0:T(8,128)(2,1)S(1)}, u32[]{:S(2)}, u32[]{:S(2)}) collective-permute-start(bf16[1,2,2,2,128,128]{5,4,3,2,1,0:T(8,128)(2,1)S(1)} %maximum_bitcast_fusion.refs_2_.refs_0_), channel_id=1, source_target_pairs={{0,12},{2,98},{4,0},{6,102},{8,4},{10,106},{12,8},{14,110},{16,28}... | collective-permute-start | bytes 786440 | tf_op jit(solution)/shard_map/ppermute | solution.py:29
  92.9 17.1 %collective-permute-start.8 = (bf16[2,5,2,128,128]{4,3,2,1,0:T(8,128)(2,1)S(1)}, bf16[2,5,2,128,128]{4,3,2,1,0:T(8,128)(2,1)S(1)}, u32[]{:S(2)}, u32[]{:S(2)}) collective-permute-start(bf16[2,5,2,128,128]{4,3,2,1,0:T(8,128)(2,1)S(1)} %pad_maximum_fusion.refs_1_), channel_id=1, source_target_pairs={{0,16},{2,18},{4,20},{6,22},{8,24},{10,26},{12,28},{14,30},{16,0},... | collective-permute-start | bytes 1966088 | tf_op jit(solution)/shard_map/ppermute | solution.py:29
  99.8 15.2 %collective-permute-start.7 = (bf16[4,2,2,2,128,128]{5,4,3,2,1,0:T(8,128)(2,1)S(1)}, bf16[4,2,2,2,128,128]{5,4,3,2,1,0:T(8,128)(2,1)S(1)}, u32[]{:S(2)}, u32[]{:S(2)}) collective-permute-start(bf16[4,2,2,2,128,128]{5,4,3,2,1,0:T(8,128)(2,1)S(1)} %join.1.refs_8_.refs_2_), channel_id=1, source_target_pairs={{0,32},{2,6},{4,36},{6,10},{8,40},{10,14},{12,44},{14,2},{16,48},{... | collective-permute-start | bytes 3145736 | tf_op jit(solution)/shard_map/ppermute | solution.py:29
  99.9 15.1 %collective-permute-start.6 = (bf16[4,2,2,2,128,128]{5,4,3,2,1,0:T(8,128)(2,1)S(1)}, bf16[4,2,2,2,128,128]{5,4,3,2,1,0:T(8,128)(2,1)S(1)}, u32[]{:S(2)}, u32[]{:S(2)}) collective-permute-start(bf16[4,2,2,2,128,128]{5,4,3,2,1,0:T(8,128)(2,1)S(1)} %join.1.refs_8_.refs_2_), channel_id=1, source_target_pairs={{0,96},{2,14},{4,100},{6,2},{8,104},{10,6},{12,108},{14,10},{16,11... | collective-permute-start | bytes 3145736 | tf_op jit(solution)/shard_map/ppermute | solution.py:29
  115.1 11.3 %collective-permute-start.10 = (bf16[2,2,2,2,128,128]{5,4,3,2,1,0:T(8,128)(2,1)S(1)}, bf16[2,2,2,2,128,128]{5,4,3,2,1,0:T(8,128)(2,1)S(1)}, u32[]{:S(2)}, u32[]{:S(2)}) collective-permute-start(bf16[2,2,2,2,128,128]{5,4,3,2,1,0:T(8,128)(2,1)S(1)} %get-tuple-element.48), channel_id=1, source_target_pairs={{0,32},{2,6},{4,36},{6,10},{8,40},{10,14},{12,44},{14,2},{16,48},{... | collective-permute-start | bytes 1572872 | tf_op jit(solution)/shard_map/ppermute | solution.py:29
  115.2 11.3 %collective-permute-start.9 = (bf16[2,2,2,2,128,128]{5,4,3,2,1,0:T(8,128)(2,1)S(1)}, bf16[2,2,2,2,128,128]{5,4,3,2,1,0:T(8,128)(2,1)S(1)}, u32[]{:S(2)}, u32[]{:S(2)}) collective-permute-start(bf16[2,2,2,2,128,128]{5,4,3,2,1,0:T(8,128)(2,1)S(1)} %get-tuple-element.47.refs_7_), channel_id=1, source_target_pairs={{0,96},{2,14},{4,100},{6,2},{8,104},{10,6},{12,108},{14,10},{16,11... | collective-permute-start | bytes 1572872 | tf_op jit(solution)/shard_map/ppermute | solution.py:29
  131.4 17.8 %collective-permute-start.11 = (bf16[2,656,128]{2,1,0:T(8,128)(2,1)S(1)}, bf16[2,656,128]{2,1,0:T(8,128)(2,1)S(1)}, u32[]{:S(2)}, u32[]{:S(2)}) collective-permute-start(bf16[2,656,128]{2,1,0:T(8,128)(2,1)S(1)} %get-tuple-element.60), channel_id=1, source_target_pairs={{0,18},{2,16},{4,22},{6,20},{8,26},{10,24},{12,30},{14,28},{16,2},... | collective-permute-start | bytes 1007624 | tf_op jit(solution)/shard_map/ppermute | solution.py:29
  134.0 16.3 %collective-permute-start.12 = (bf16[2,656,128]{2,1,0:T(8,128)(2,1)S(1)}, bf16[2,656,128]{2,1,0:T(8,128)(2,1)S(1)}, u32[]{:S(2)}, u32[]{:S(2)}) collective-permute-start(bf16[2,656,128]{2,1,0:T(8,128)(2,1)S(1)} %get-tuple-element.56.refs_9_), channel_id=1, source_target_pairs={{0,16},{2,18},{4,20},{6,22},{8,24},{10,26},{12,28},{14,30},{16,0},... | collective-permute-start | bytes 1007624 | tf_op jit(solution)/shard_map/ppermute | solution.py:29
  149.3 1.5 collective-permute-start.13
  149.4 1.6 %collective-permute-start.14 = (bf16[656,128]{1,0:T(8,128)(2,1)S(1)}, bf16[656,128]{1,0:T(8,128)(2,1)S(1)}, u32[]{:S(2)}, u32[]{:S(2)}) collective-permute-start(bf16[656,128]{1,0:T(8,128)(2,1)S(1)} %get-tuple-element.63), channel_id=1, source_target_pairs={{0,2},{2,0},{4,6},{6,4},{8,10},{10,8},{12,14},{14,12},{16,18},{18,... | collective-permute-start | bytes 503816 | tf_op jit(solution)/shard_map/ppermute | solution.py:29

commit v6 on v5

--- a/solution.py
+++ b/solution.py
@@ -397,17 +397,26 @@
 
         lax.fori_loop(0, 2, own, 0)
 
-    pairs = n_late // 2
-    early_pairs = n_early // 2
+    quads, early_quads = n_late // 4, n_early // 4
+
+    def four(i, carry):
+        late = i < quads
+        j = i - quads
+        places = tuple(jnp.where(late, 4 * i + t, last - 4 * j - t) for t in range(4))
+        update(jnp.where(late, 1, 0), places, None)
+        return carry
+
+    lax.fori_loop(0, quads + early_quads, four, 0)
+    pairs, early_pairs = n_late // 2, n_early // 2
+    rest = pairs - 2 * quads
+
     def two(i, carry):
-        late = i < pairs
-        j = i - pairs
-        one = jnp.where(late, 2 * i, last - 2 * j)
-        other = jnp.where(late, 2 * i + 1, last - 2 * j - 1)
-        update(jnp.where(late, 1, 0), (one, other), None)
+        late = i < rest
+        places = tuple(jnp.where(late, 4 * quads + t, last - 4 * early_quads - t) for t in range(2))
+        update(jnp.where(late, 1, 0), places, None)
         return carry
 
-    lax.fori_loop(0, pairs + early_pairs, two, 0)
+    lax.fori_loop(0, rest + early_pairs - 2 * early_quads, two, 0)
     odd_late = n_late - 2 * pairs
     odd_early = n_early - 2 * early_pairs
 

time: 153 us -> 151 us (0.987)
  Pallas kernels: 54.5 us -> 52.6 us
    pallas_call x6, Pallas kernels: 36.4 us -> 34.5 us  [attend(): pl.pallas_call(functools.partial(attend_kernel, counts, diag, state is no...]
  transfers between devices with their start and end apart: 16 -> 16, of which waited for: 11 -> 9; matrix products, arithmetic and copies ran while one was open for 1% -> 1% of each run, Pallas kernels for 27% -> 26%
where the time goes in v6:
time: 151 us
  waiting for transfers between devices  66.5 us (44%)
  Pallas kernels  52.6 us (35%)
  starting transfers between devices  29.3 us (19%)
    all_to_all x1, waiting for transfers between devices, shards(): lax.all_to_all(relayout(expert_out), 'ctx', split_axis=0, concat_axis=0,...  34.9 us
    pallas_call x6, Pallas kernels, attend(): pl.pallas_call(functools.partial(attend_kernel, counts, diag, state is no...  34.5 us
    ppermute x2, waiting for transfers between devices, shards(): lax.ppermute(h, 'tp', [(0, 1), (1, 0)])  19.9 us
    ppermute x13, starting transfers between devices, permute(): return lax.ppermute(value, 'ctx', pairs)  15.3 us
    all_to_all x1, starting transfers between devices, shards(): lax.all_to_all(relayout(expert_out), 'ctx', split_axis=0, concat_axis=0,...  12.4 us
    ppermute x13, waiting for transfers between devices, permute(): return lax.ppermute(value, 'ctx', pairs)  11.7 us
    pallas_call x3, Pallas kernels, project(): pl.pallas_call(kernel, in_specs=[smem()] + [vmem()] * len(ins), out_specs...  7.81 us
    pallas_call x2, Pallas kernels, pick(): pl.pallas_call(functools.partial(pick_kernel, part * width), in_specs=[vm...  5.79 us
  transfers between devices with their start and end apart: 16, of which 9 were waited for; matrix products, arithmetic and copies ran while one was open for 1% of the time, Pallas kernels for 26%

profile of v6, /device:TPU:1, one launch (start us, length us, event | category | flops | bytes accessed | tf_op | source)
XLA Modules:
  0.0 151.1 jit_solution(11913653813268460145)
XLA Ops:
  0.6 2.7 %relayout.1 = bf16[64,8,2560]{2,1,0:T(8,128)(2,1)} custom-call(bf16[2,64,4,2560]{3,2,1,0:T(4,128)(2,1)} %experts.1), custom_call_target="tpu_custom_call" | custom-call | tf_op jit(solution)/shard_map/relayout/pallas_call | solution.py:127
  3.4 12.4 %all-to-all-start = ((bf16[64,8,2560]{2,1,0:T(8,128)(2,1)}), bf16[64,8,2560]{2,1,0:T(8,128)(2,1)S(1)}, u32[]{:S(2)}, u32[]{:S(2)}) async-start(bf16[64,8,2560]{2,1,0:T(8,128)(2,1)} %relayout.1), calls=%async_computation | async-start | bytes 5242880 | tf_op jit(solution)/shard_map/all_to_all | solution.py:604
  16.0 0.1 copy.17.gate
  16.1 0.1 copy.15.ids_col
  16.2 0.3 choose.1.hot.before
  16.5 0.1 pad_add_fusion.where
  16.6 0.1 add_convert_fusion.1.refs_0_
  16.7 0.5 fusion
  17.3 0.1 pad_maximum_fusion.1
  17.4 34.9 %all-to-all-done = bf16[64,8,2560]{2,1,0:T(8,128)(2,1)S(1)} async-done(((bf16[64,8,2560]{2,1,0:T(8,128)(2,1)}), bf16[64,8,2560]{2,1,0:T(8,128)(2,1)S(1)}, u32[]{:S(2)}, u32[]{:S(2)}) %all-to-all-start) | async-done | bytes 2621472 | tf_op jit(solution)/shard_map/all_to_all | solution.py:604
  52.3 2.2 %pick.2.before.ha = bf16[256,1280]{1,0:T(8,128)(2,1)S(1)} custom-call(bf16[256,512]{1,0:T(8,128)(2,1)S(1)} %choose.1.hot.before, f32[256,1]{1,0:T(8,128)S(1)} %copy.17.gate, bf16[512,2560]{1,0:T(8,128)(2,1)S(1)} %bitcast.10, bf16[256,2560]{1,0:T(8,128)(2,1)} %residual.3, bf16[256,2560]{1,0:T(8,128)(2,1)} %shared.3, bf16[256,512]{1,0:T(8,128)(2,1)S(1)} %choose.1.hot.before), custom_call_target="tpu_custom_call" | custom-call | flops 2875000064 | tf_op jit(solution)/shard_map/pick/pallas_call | solution.py:187
  54.5 0.8 collective-permute-start.1
  55.3 3.6 %pick.3 = (bf16[256,2560]{1,0:T(8,128)(2,1)}, bf16[256,1280]{1,0:T(8,128)(2,1)S(1)}) custom-call(bf16[256,512]{1,0:T(8,128)(2,1)S(1)} %choose.1.hot.before, f32[256,1]{1,0:T(8,128)S(1)} %copy.17.gate, bf16[512,2560]{1,0:T(8,128)(2,1)S(1)} %bitcast.11, bf16[256,2560]{1,0:T(8,128)(2,1)} %residual.3, bf16[256,2560]{1,0:T(8,128)(2,1)} %shared.3, ...), custom_call_target="tpu_custom_call" | custom-call | flops 2875000064 | tf_op jit(solution)/shard_map/pick/pallas_call | solution.py:187
  59.0 0.8 collective-permute-start
  59.8 0.3 copy-done.2
  60.0 3.2 %project_own.1 = (f32[256,1792]{1,0:T(8,128)S(1)}, f32[256,1]{1,0:T(8,128)S(1)}) custom-call(s32[2]{0:T(128)S(1)} %pad_add_fusion.where, bf16[256,1280]{1,0:T(8,128)(2,1)S(1)} %pick.2.before.ha, bf16[256,1280]{1,0:T(8,128)(2,1)S(1)} %get-tuple-element.34.hb, bf16[4,1,1280]{2,1,0:T(2,128)(2,1)S(1)} %reshape.38.gain, bf16[5120,256]{1,0:T(8,128)(2,1)S(1)} %copy-done.1, ...), custom_call_target="tpu_custom_call" | custom-call | flops 5750000128 | tf_op jit(solution)/shard_map/project_own/pallas_call | solution.py:288
  63.3 7.8 %collective-permute-done.1.h = bf16[256,1280]{1,0:T(8,128)(2,1)S(1)} collective-permute-done((bf16[256,1280]{1,0:T(8,128)(2,1)S(1)}, bf16[256,1280]{1,0:T(8,128)(2,1)S(1)}, u32[]{:S(2)}, u32[]{:S(2)}) %collective-permute-start.1) | collective-permute-done | bytes 655392 | tf_op jit(solution)/shard_map/ppermute | solution.py:610
  71.0 2.0 %project_more.1 = (f32[256,1792]{1,0:T(8,128)S(1)}, f32[256,1]{1,0:T(8,128)S(1)}) custom-call(s32[2]{0:T(128)S(1)} %pad_add_fusion.where, bf16[256,1280]{1,0:T(8,128)(2,1)S(1)} %collective-permute-done.1.h, bf16[4,1,1280]{2,1,0:T(2,128)(2,1)S(1)} %reshape.38.gain, bf16[5120,256]{1,0:T(8,128)(2,1)S(1)} %copy-done.1, bf16[5120,256]{1,0:T(8,128)(2,1)S(1)} %copy-done.2, ...), custom_call_target="tpu_custom_call" | custom-call | flops 2300000000 | tf_op jit(solution)/shard_map/project_more/pallas_call | solution.py:288
  73.0 12.1 %collective-permute-done.h = bf16[256,1280]{1,0:T(8,128)(2,1)S(1)} collective-permute-done((bf16[256,1280]{1,0:T(8,128)(2,1)S(1)}, bf16[256,1280]{1,0:T(8,128)(2,1)S(1)}, u32[]{:S(2)}, u32[]{:S(2)}) %collective-permute-start) | collective-permute-done | bytes 655392 | tf_op jit(solution)/shard_map/ppermute | solution.py:610
  85.1 2.6 %project_last.1 = (bf16[2,2,128,128]{3,2,1,0:T(8,128)(2,1)S(1)}, bf16[5,2,128,128]{3,2,1,0:T(8,128)(2,1)S(1)}, bf16[14,128,128]{2,1,0:T(8,128)(2,1)S(1)}) custom-call(s32[2]{0:T(128)S(1)} %pad_add_fusion.where, bf16[256,1280]{1,0:T(8,128)(2,1)S(1)} %collective-permute-done.h, bf16[4,1,1280]{2,1,0:T(2,128)(2,1)S(1)} %reshape.38.gain, ...), custom_call_target="tpu_custom_call" | custom-call | flops 2300000000 | tf_op jit(solution)/shard_map/project_last/pallas_call | solution.py:288
  87.7 0.8 collective-permute-start.2
  88.5 0.1 add_convert_fusion.refs_0_
  88.6 1.3 collective-permute-done.2
  90.0 0.2 collective-permute-start.5
  90.1 1.3 collective-permute-start.4
  91.4 1.4 collective-permute-start.3
  92.9 0.6 collective-permute-start.8
  93.5 2.0 %attend.6 = (f32[2,5,128,256]{3,2,1,0:T(8,128)S(1)}, f32[2,5,8,256]{3,2,1,0:T(8,128)S(1)}, f32[2,5,8,256]{3,2,1,0:T(8,128)S(1)}) custom-call(s32[1]{0:T(128)} %bitcast.2.refs_0_.core, bf16[2,5,2,128,128]{4,3,2,1,0:T(8,128)(2,1)S(1)} %pad_maximum_fusion.refs_1_, bf16[1,2,2,2,128,128]{5,4,3,2,1,0:T(8,128)(2,1)S(1)} %maximum_bitcast_fusion.refs_2_.refs_0_), custom_call_target="tpu_custom_call" | custom-call | flops 34500001792 | tf_op jit(solution)/shard_map/attend/pallas_call | solution.py:481
  95.5 1.6 %collective-permute-done.5.refs_3_.refs_4_ = bf16[1,2,2,2,128,128]{5,4,3,2,1,0:T(8,128)(2,1)S(1)} collective-permute-done((bf16[1,2,2,2,128,128]{5,4,3,2,1,0:T(8,128)(2,1)S(1)}, bf16[1,2,2,2,128,128]{5,4,3,2,1,0:T(8,128)(2,1)S(1)}, u32[]{:S(2)}, u32[]{:S(2)}) %collective-permute-start.5) | collective-permute-done | bytes 262176 | tf_op jit(solution)/shard_map/ppermute | solution.py:29
  97.1 2.6 %collective-permute-done.4.refs_2_.refs_3_ = bf16[1,2,2,2,128,128]{5,4,3,2,1,0:T(8,128)(2,1)S(1)} collective-permute-done((bf16[1,2,2,2,128,128]{5,4,3,2,1,0:T(8,128)(2,1)S(1)}, bf16[1,2,2,2,128,128]{5,4,3,2,1,0:T(8,128)(2,1)S(1)}, u32[]{:S(2)}, u32[]{:S(2)}) %collective-permute-start.4) | collective-permute-done | bytes 262176 | tf_op jit(solution)/shard_map/ppermute | solution.py:29
  99.8 0.1 collective-permute-start.7
  99.9 2.7 %collective-permute-start.6 = (bf16[4,2,2,2,128,128]{5,4,3,2,1,0:T(8,128)(2,1)S(1)}, bf16[4,2,2,2,128,128]{5,4,3,2,1,0:T(8,128)(2,1)S(1)}, u32[]{:S(2)}, u32[]{:S(2)}) collective-permute-start(bf16[4,2,2,2,128,128]{5,4,3,2,1,0:T(8,128)(2,1)S(1)} %join.1.refs_8_.refs_2_), channel_id=1, source_target_pairs={{0,96},{2,14},{4,100},{6,2},{8,104},{10,6},{12,108},{14,10},{16,11... | collective-permute-start | bytes 3145736 | tf_op jit(solution)/shard_map/ppermute | solution.py:29
  102.5 3.4 %attend.7 = (f32[2,5,128,256]{3,2,1,0:T(8,128)S(1)}, f32[2,5,8,256]{3,2,1,0:T(8,128)S(1)}, f32[2,5,8,256]{3,2,1,0:T(8,128)S(1)}) custom-call(s32[3]{0:T(128)S(1)} %slice_convert_fusion.refs_0_, bf16[2,5,2,128,128]{4,3,2,1,0:T(8,128)(2,1)S(1)} %pad_maximum_fusion.refs_1_, bf16[1,2,2,2,128,128]{5,4,3,2,1,0:T(8,128)(2,1)S(1)} %collective-permute-done.3.refs_1_.refs_2_, ...), custom_call_target="tpu_custom_call" | custom-call | flops 3967500032 | tf_op jit(solution)/shard_map/attend/pallas_call | solution.py:481
  106.0 4.1 %collective-permute-done.8.refs_1_ = bf16[2,5,2,128,128]{4,3,2,1,0:T(8,128)(2,1)S(1)} collective-permute-done((bf16[2,5,2,128,128]{4,3,2,1,0:T(8,128)(2,1)S(1)}, bf16[2,5,2,128,128]{4,3,2,1,0:T(8,128)(2,1)S(1)}, u32[]{:S(2)}, u32[]{:S(2)}) %collective-permute-start.8) | collective-permute-done | bytes 655392 | tf_op jit(solution)/shard_map/ppermute | solution.py:29
  110.0 4.7 %attend.8 = (f32[2,5,128,256]{3,2,1,0:T(8,128)S(1)}, f32[2,5,8,256]{3,2,1,0:T(8,128)S(1)}, f32[2,5,8,256]{3,2,1,0:T(8,128)S(1)}) custom-call(s32[4]{0:T(128)S(1)} %compare_convert_fusion.1.refs_0_, bf16[2,5,2,128,128]{4,3,2,1,0:T(8,128)(2,1)S(1)} %collective-permute-done.8.refs_1_, bf16[4,2,2,2,128,128]{5,4,3,2,1,0:T(8,128)(2,1)S(1)} %join.1.refs_8_.refs_2_, ...), custom_call_target="tpu_custom_call" | custom-call | flops 8049999872 | tf_op jit(solution)/shard_map/attend/pallas_call | solution.py:481
  114.7 0.3 collective-permute-done.7.behind.refs_3_
  115.1 0.1 collective-permute-start.10
  115.2 2.7 %collective-permute-start.9 = (bf16[2,2,2,2,128,128]{5,4,3,2,1,0:T(8,128)(2,1)S(1)}, bf16[2,2,2,2,128,128]{5,4,3,2,1,0:T(8,128)(2,1)S(1)}, u32[]{:S(2)}, u32[]{:S(2)}) collective-permute-start(bf16[2,2,2,2,128,128]{5,4,3,2,1,0:T(8,128)(2,1)S(1)} %get-tuple-element.47.refs_7_), channel_id=1, source_target_pairs={{0,96},{2,14},{4,100},{6,2},{8,104},{10,6},{12,108},{14,10},{16,11... | collective-permute-start | bytes 1572872 | tf_op jit(solution)/shard_map/ppermute | solution.py:29
  117.8 8.2 %attend.9 = (f32[2,5,128,256]{3,2,1,0:T(8,128)S(1)}, f32[2,5,8,256]{3,2,1,0:T(8,128)S(1)}, f32[2,5,8,256]{3,2,1,0:T(8,128)S(1)}) custom-call(s32[8]{0:T(128)S(1)} %add_convert_fusion.1.refs_0_, bf16[2,5,2,128,128]{4,3,2,1,0:T(8,128)(2,1)S(1)} %collective-permute-done.8.refs_1_, bf16[4,2,2,2,128,128]{5,4,3,2,1,0:T(8,128)(2,1)S(1)} %collective-permute-done.6.ahead.refs_2_, ...), custom_call_target="tpu_custom_call" | custom-call | flops 10579999744 | tf_op jit(solution)/shard_map/attend/pallas_call | solution.py:481
  126.1 4.8 %attend.10 = (bf16[2,656,128]{2,1,0:T(8,128)(2,1)S(1)}, bf16[2,656,128]{2,1,0:T(8,128)(2,1)S(1)}) custom-call(s32[4]{0:T(128)S(1)} %get-tuple-element.75.refs_0_, bf16[2,5,2,128,128]{4,3,2,1,0:T(8,128)(2,1)S(1)} %collective-permute-done.8.refs_1_, bf16[2,2,2,2,128,128]{5,4,3,2,1,0:T(8,128)(2,1)S(1)} %collective-permute-done.9.refs_2_.refs_4_, ...), custom_call_target="tpu_custom_call" | custom-call | flops 5289999872 | tf_op jit(solution)/shard_map/attend/pallas_call | solution.py:481
  130.9 2.3 %collective-permute-start.11 = (bf16[2,656,128]{2,1,0:T(8,128)(2,1)S(1)}, bf16[2,656,128]{2,1,0:T(8,128)(2,1)S(1)}, u32[]{:S(2)}, u32[]{:S(2)}) collective-permute-start(bf16[2,656,128]{2,1,0:T(8,128)(2,1)S(1)} %get-tuple-element.60), channel_id=1, source_target_pairs={{0,18},{2,16},{4,22},{6,20},{8,26},{10,24},{12,30},{14,28},{16,2},... | collective-permute-start | bytes 1007624 | tf_op jit(solution)/shard_map/ppermute | solution.py:29
  133.2 2.7 %collective-permute-start.12 = (bf16[2,656,128]{2,1,0:T(8,128)(2,1)S(1)}, bf16[2,656,128]{2,1,0:T(8,128)(2,1)S(1)}, u32[]{:S(2)}, u32[]{:S(2)}) collective-permute-start(bf16[2,656,128]{2,1,0:T(8,128)(2,1)S(1)} %get-tuple-element.56.refs_9_), channel_id=1, source_target_pairs={{0,16},{2,18},{4,20},{6,22},{8,24},{10,26},{12,28},{14,30},{16,0},... | collective-permute-start | bytes 1007624 | tf_op jit(solution)/shard_map/ppermute | solution.py:29
  135.9 11.3 %attend.11 = (f32[2,5,128,256]{3,2,1,0:T(8,128)S(1)}, f32[2,5,8,256]{3,2,1,0:T(8,128)S(1)}, f32[2,5,8,256]{3,2,1,0:T(8,128)S(1)}) custom-call(s32[12]{0:T(128)S(1)} %add_convert_fusion.refs_0_, bf16[2,5,2,128,128]{4,3,2,1,0:T(8,128)(2,1)S(1)} %pad_maximum_fusion.refs_1_, bf16[4,2,2,2,128,128]{5,4,3,2,1,0:T(8,128)(2,1)S(1)} %collective-permute-done.6.ahead.refs_2_, ...), custom_call_target="tpu_custom_call" | custom-call | flops 15870000128 | tf_op jit(solution)/shard_map/attend/pallas_call | solution.py:481
  147.2 0.1 divide.1
  147.4 0.1 collective-permute-start.13
  147.5 0.5 collective-permute-start.14
  148.0 1.9 %collective-permute-done.12.own_pair = bf16[2,656,128]{2,1,0:T(8,128)(2,1)S(1)} collective-permute-done((bf16[2,656,128]{2,1,0:T(8,128)(2,1)S(1)}, bf16[2,656,128]{2,1,0:T(8,128)(2,1)S(1)}, u32[]{:S(2)}, u32[]{:S(2)}) %collective-permute-start.12) | collective-permute-done | bytes 335904 | tf_op jit(solution)/shard_map/ppermute | solution.py:29
  149.9 1.3 merge.1
  (34 shorter events, 0.5 us)
Async XLA Ops:
  3.3 12.6 %copy-start.4 = (bf16[5120]{0:T(1024)(128)(2,1)S(1)}, bf16[5120]{0:T(1024)(128)(2,1)}, u32[]{:S(2)}) copy-start(bf16[5120]{0:T(1024)(128)(2,1)} %param.15) | copy-start | bytes 30724
  3.3 12.6 %copy-start.5 = (f32[256,1]{0,1:T(1,128)S(1)}, f32[256,1]{0,1:T(1,128)}, u32[]{:S(2)}) copy-start(f32[256,1]{0,1:T(1,128)} %param.14) | copy-start | bytes 3076
  3.4 12.7 %copy-start.3 = (s32[256,1]{0,1:T(1,128)S(1)}, s32[256,1]{0,1:T(1,128)}, u32[]{:S(2)}) copy-start(s32[256,1]{0,1:T(1,128)} %param.13) | copy-start | bytes 3076
  3.4 13.2 %copy-start.6 = (s32[4]{0:T(128)S(1)}, s32[4]{0:T(128)}, u32[]{:S(2)}) copy-start(s32[4]{0:T(128)} %constant.156.clone) | copy-start | bytes 52
  3.4 48.9 %all-to-all-start = ((bf16[64,8,2560]{2,1,0:T(8,128)(2,1)}), bf16[64,8,2560]{2,1,0:T(8,128)(2,1)S(1)}, u32[]{:S(2)}, u32[]{:S(2)}) async-start(bf16[64,8,2560]{2,1,0:T(8,128)(2,1)} %relayout.1), calls=%async_computation | async-start | bytes 5242880 | tf_op jit(solution)/shard_map/all_to_all | solution.py:604
  52.3 7.5 %copy-start = (bf16[5120,1280]{1,0:T(8,128)(2,1)S(1)}, bf16[5120,1280]{1,0:T(8,128)(2,1)}, u32[]{:S(2)}) copy-start(bf16[5120,1280]{1,0:T(8,128)(2,1)} %wq.5) | copy-start | bytes 39321604
  54.5 5.3 %copy-start.1 = (bf16[5120,256]{1,0:T(8,128)(2,1)S(1)}, bf16[5120,256]{1,0:T(8,128)(2,1)}, u32[]{:S(2)}) copy-start(bf16[5120,256]{1,0:T(8,128)(2,1)} %wk.5) | copy-start | bytes 7864324
  54.5 5.5 %copy-start.2 = (bf16[5120,256]{1,0:T(8,128)(2,1)S(1)}, bf16[5120,256]{1,0:T(8,128)(2,1)}, u32[]{:S(2)}) copy-start(bf16[5120,256]{1,0:T(8,128)(2,1)} %wv.5) | copy-start | bytes 7864324
  54.5 16.5 %collective-permute-start.1 = (bf16[256,1280]{1,0:T(8,128)(2,1)S(1)}, bf16[256,1280]{1,0:T(8,128)(2,1)S(1)}, u32[]{:S(2)}, u32[]{:S(2)}) collective-permute-start(bf16[256,1280]{1,0:T(8,128)(2,1)S(1)} %pick.2.before.ha), channel_id=1, source_target_pairs={{0,1},{1,0},{2,3},{3,2},{4,5},{5,4},{6,7},{7,6},{8,9},{9,8},{10,11... | collective-permute-start | bytes 1966088 | tf_op jit(solution)/shard_map/ppermute | solution.py:610
  59.0 26.1 %collective-permute-start = (bf16[256,1280]{1,0:T(8,128)(2,1)S(1)}, bf16[256,1280]{1,0:T(8,128)(2,1)S(1)}, u32[]{:S(2)}, u32[]{:S(2)}) collective-permute-start(bf16[256,1280]{1,0:T(8,128)(2,1)S(1)} %get-tuple-element.34.hb), channel_id=1, source_target_pairs={{0,1},{1,0},{2,3},{3,2},{4,5},{5,4},{6,7},{7,6},{8,9},{9,8},{10,11... | collective-permute-start | bytes 1966088 | tf_op jit(solution)/shard_map/ppermute | solution.py:610
  87.7 2.2 %collective-permute-start.2 = (bf16[14,128,128]{2,1,0:T(8,128)(2,1)S(1)}, bf16[14,128,128]{2,1,0:T(8,128)(2,1)S(1)}, u32[]{:S(2)}, u32[]{:S(2)}) collective-permute-start(bf16[14,128,128]{2,1,0:T(8,128)(2,1)S(1)} %get-tuple-element.40), channel_id=1, source_target_pairs={{0,2},{2,0},{4,6},{6,4},{8,10},{10,8},{12,14},{14,12},{16,18},{18,... | collective-permute-start | bytes 1376264 | tf_op jit(solution)/shard_map/ppermute | solution.py:29
  90.0 7.1 %collective-permute-start.5 = (bf16[1,2,2,2,128,128]{5,4,3,2,1,0:T(8,128)(2,1)S(1)}, bf16[1,2,2,2,128,128]{5,4,3,2,1,0:T(8,128)(2,1)S(1)}, u32[]{:S(2)}, u32[]{:S(2)}) collective-permute-start(bf16[1,2,2,2,128,128]{5,4,3,2,1,0:T(8,128)(2,1)S(1)} %maximum_bitcast_fusion.refs_2_.refs_0_), channel_id=1, source_target_pairs={{0,8},{2,66},{4,12},{6,70},{8,0},{10,74},{12,4},{14,78},{16,24},{1... | collective-permute-start | bytes 786440 | tf_op jit(solution)/shard_map/ppermute | solution.py:29
  90.1 9.6 %collective-permute-start.4 = (bf16[1,2,2,2,128,128]{5,4,3,2,1,0:T(8,128)(2,1)S(1)}, bf16[1,2,2,2,128,128]{5,4,3,2,1,0:T(8,128)(2,1)S(1)}, u32[]{:S(2)}, u32[]{:S(2)}) collective-permute-start(bf16[1,2,2,2,128,128]{5,4,3,2,1,0:T(8,128)(2,1)S(1)} %maximum_bitcast_fusion.refs_2_.refs_0_), channel_id=1, source_target_pairs={{0,4},{2,34},{4,8},{6,38},{8,12},{10,42},{12,0},{14,46},{16,20},{1... | collective-permute-start | bytes 786440 | tf_op jit(solution)/shard_map/ppermute | solution.py:29
  91.4 8.3 %collective-permute-start.3 = (bf16[1,2,2,2,128,128]{5,4,3,2,1,0:T(8,128)(2,1)S(1)}, bf16[1,2,2,2,128,128]{5,4,3,2,1,0:T(8,128)(2,1)S(1)}, u32[]{:S(2)}, u32[]{:S(2)}) collective-permute-start(bf16[1,2,2,2,128,128]{5,4,3,2,1,0:T(8,128)(2,1)S(1)} %maximum_bitcast_fusion.refs_2_.refs_0_), channel_id=1, source_target_pairs={{0,12},{2,98},{4,0},{6,102},{8,4},{10,106},{12,8},{14,110},{16,28}... | collective-permute-start | bytes 786440 | tf_op jit(solution)/shard_map/ppermute | solution.py:29
  92.9 17.1 %collective-permute-start.8 = (bf16[2,5,2,128,128]{4,3,2,1,0:T(8,128)(2,1)S(1)}, bf16[2,5,2,128,128]{4,3,2,1,0:T(8,128)(2,1)S(1)}, u32[]{:S(2)}, u32[]{:S(2)}) collective-permute-start(bf16[2,5,2,128,128]{4,3,2,1,0:T(8,128)(2,1)S(1)} %pad_maximum_fusion.refs_1_), channel_id=1, source_target_pairs={{0,16},{2,18},{4,20},{6,22},{8,24},{10,26},{12,28},{14,30},{16,0},... | collective-permute-start | bytes 1966088 | tf_op jit(solution)/shard_map/ppermute | solution.py:29
  99.8 15.2 %collective-permute-start.7 = (bf16[4,2,2,2,128,128]{5,4,3,2,1,0:T(8,128)(2,1)S(1)}, bf16[4,2,2,2,128,128]{5,4,3,2,1,0:T(8,128)(2,1)S(1)}, u32[]{:S(2)}, u32[]{:S(2)}) collective-permute-start(bf16[4,2,2,2,128,128]{5,4,3,2,1,0:T(8,128)(2,1)S(1)} %join.1.refs_8_.refs_2_), channel_id=1, source_target_pairs={{0,32},{2,6},{4,36},{6,10},{8,40},{10,14},{12,44},{14,2},{16,48},{... | collective-permute-start | bytes 3145736 | tf_op jit(solution)/shard_map/ppermute | solution.py:29
  99.9 15.1 %collective-permute-start.6 = (bf16[4,2,2,2,128,128]{5,4,3,2,1,0:T(8,128)(2,1)S(1)}, bf16[4,2,2,2,128,128]{5,4,3,2,1,0:T(8,128)(2,1)S(1)}, u32[]{:S(2)}, u32[]{:S(2)}) collective-permute-start(bf16[4,2,2,2,128,128]{5,4,3,2,1,0:T(8,128)(2,1)S(1)} %join.1.refs_8_.refs_2_), channel_id=1, source_target_pairs={{0,96},{2,14},{4,100},{6,2},{8,104},{10,6},{12,108},{14,10},{16,11... | collective-permute-start | bytes 3145736 | tf_op jit(solution)/shard_map/ppermute | solution.py:29
  115.1 11.0 %collective-permute-start.10 = (bf16[2,2,2,2,128,128]{5,4,3,2,1,0:T(8,128)(2,1)S(1)}, bf16[2,2,2,2,128,128]{5,4,3,2,1,0:T(8,128)(2,1)S(1)}, u32[]{:S(2)}, u32[]{:S(2)}) collective-permute-start(bf16[2,2,2,2,128,128]{5,4,3,2,1,0:T(8,128)(2,1)S(1)} %get-tuple-element.48), channel_id=1, source_target_pairs={{0,32},{2,6},{4,36},{6,10},{8,40},{10,14},{12,44},{14,2},{16,48},{... | collective-permute-start | bytes 1572872 | tf_op jit(solution)/shard_map/ppermute | solution.py:29
  115.2 10.9 %collective-permute-start.9 = (bf16[2,2,2,2,128,128]{5,4,3,2,1,0:T(8,128)(2,1)S(1)}, bf16[2,2,2,2,128,128]{5,4,3,2,1,0:T(8,128)(2,1)S(1)}, u32[]{:S(2)}, u32[]{:S(2)}) collective-permute-start(bf16[2,2,2,2,128,128]{5,4,3,2,1,0:T(8,128)(2,1)S(1)} %get-tuple-element.47.refs_7_), channel_id=1, source_target_pairs={{0,96},{2,14},{4,100},{6,2},{8,104},{10,6},{12,108},{14,10},{16,11... | collective-permute-start | bytes 1572872 | tf_op jit(solution)/shard_map/ppermute | solution.py:29
  130.9 16.3 %collective-permute-start.11 = (bf16[2,656,128]{2,1,0:T(8,128)(2,1)S(1)}, bf16[2,656,128]{2,1,0:T(8,128)(2,1)S(1)}, u32[]{:S(2)}, u32[]{:S(2)}) collective-permute-start(bf16[2,656,128]{2,1,0:T(8,128)(2,1)S(1)} %get-tuple-element.60), channel_id=1, source_target_pairs={{0,18},{2,16},{4,22},{6,20},{8,26},{10,24},{12,30},{14,28},{16,2},... | collective-permute-start | bytes 1007624 | tf_op jit(solution)/shard_map/ppermute | solution.py:29
  133.2 16.7 %collective-permute-start.12 = (bf16[2,656,128]{2,1,0:T(8,128)(2,1)S(1)}, bf16[2,656,128]{2,1,0:T(8,128)(2,1)S(1)}, u32[]{:S(2)}, u32[]{:S(2)}) collective-permute-start(bf16[2,656,128]{2,1,0:T(8,128)(2,1)S(1)} %get-tuple-element.56.refs_9_), channel_id=1, source_target_pairs={{0,16},{2,18},{4,20},{6,22},{8,24},{10,26},{12,28},{14,30},{16,0},... | collective-permute-start | bytes 1007624 | tf_op jit(solution)/shard_map/ppermute | solution.py:29
  147.4 2.5 %collective-permute-start.13 = (bf16[656,128]{1,0:T(8,128)(2,1)S(1)}, bf16[656,128]{1,0:T(8,128)(2,1)S(1)}, u32[]{:S(2)}, u32[]{:S(2)}) collective-permute-start(bf16[656,128]{1,0:T(8,128)(2,1)S(1)} %get-tuple-element.62), channel_id=1, source_target_pairs={{0,2},{2,0},{4,6},{6,4},{8,10},{10,8},{12,14},{14,12},{16,18},{18,... | collective-permute-start | bytes 503816 | tf_op jit(solution)/shard_map/ppermute | solution.py:29
  147.5 2.4 %collective-permute-start.14 = (bf16[656,128]{1,0:T(8,128)(2,1)S(1)}, bf16[656,128]{1,0:T(8,128)(2,1)S(1)}, u32[]{:S(2)}, u32[]{:S(2)}) collective-permute-start(bf16[656,128]{1,0:T(8,128)(2,1)S(1)} %get-tuple-element.63), channel_id=1, source_target_pairs={{0,2},{2,0},{4,6},{6,4},{8,10},{10,8},{12,14},{14,12},{16,18},{18,... | collective-permute-start | bytes 503816 | tf_op jit(solution)/shard_map/ppermute | solution.py:29
